TPU v7x, 32 devices: a whole 2x2x4 slice. The times are simulated.
32 devices in a mesh: wide: 8 (over y, x, core), narrow: 4 (over z).
Axes of the slice: x: 2, y: 2, z: 4, core: 2. Of those that a mesh axis runs over, the one named last changes fastest.
Arguments:
- tokens_in: bfloat16 [640, 24576], P('narrow', 'wide'), may hold values from -6 to 6
- ln1_gain: bfloat16 [640], P('narrow'), may hold values from 0.25 to 1.75
- ln1_shift: bfloat16 [640], P('narrow'), may hold values from -3 to 3
- w_qkv: bfloat16 [3, 640, 640], P(None, 'wide', 'narrow'), may hold values from -0.25 to 0.25
- qv_bias: bfloat16 [2, 640], P(None, 'narrow'), may hold values from -1 to 1
- w_out: bfloat16 [640, 640], P('narrow', 'wide'), may hold values from -1.25 to 1.25
- out_bias: bfloat16 [640], P('narrow'), may hold values from -3 to 3
- ln2_gain: bfloat16 [640], P('narrow'), may hold values from 0.25 to 1.75
- ln2_shift: bfloat16 [640], P('narrow'), may hold values from -3 to 3
- w_up: bfloat16 [640, 5120], P('narrow', 'wide'), may hold values from -0.25 to 0.25
- up_bias: bfloat16 [5120], P('wide'), may hold values from -3 to 3
- w_down: bfloat16 [5120, 640], P('wide', 'narrow'), may hold values from -0.078125 to 0.078125
- down_bias: bfloat16 [640], P('narrow'), may hold values from -3 to 3
- segment_ids: int32 [24576], P('wide'), may hold values from 0 to 191, never falling along the last dimension, each value on 1 to 256 neighbouring positions
- out_grad: bfloat16 [640, 24576], P('narrow', 'wide'), may hold values from -6 to 6
- predicted: int32 [24576], P('wide'), may hold values from 0 to 3
- labels: int32 [24576], P('wide'), may hold values from 0 to 4
Outputs:
- layer_out: bfloat16 [640, 24576], P('narrow', 'wide')
- tokens_grad: float32 [640, 24576], P('narrow', 'wide')
- ln1_gain_grad: float32 [640], P('narrow')
- ln1_shift_grad: float32 [640], P('narrow')
- w_qkv_grad: float32 [3, 640, 640], P(None, 'wide', 'narrow')
- qv_bias_grad: float32 [2, 640], P(None, 'narrow')
- w_out_grad: float32 [640, 640], P('narrow', 'wide')
- out_bias_grad: float32 [640], P('narrow')
- ln2_gain_grad: float32 [640], P('narrow')
- ln2_shift_grad: float32 [640], P('narrow')
- w_up_grad: float32 [640, 5120], P('narrow', 'wide')
- up_bias_grad: float32 [5120], P('wide')
- w_down_grad: float32 [5120, 640], P('wide', 'narrow')
- down_bias_grad: float32 [640], P('narrow')
- tallies: int32 [2, 4], replicated
- accuracy: float32 [], replicated
Inputs may be any that keep to these rules, and one draw needn't show every extreme that they name: `segment_ids`: segment numbers never fall along the tokens, and one segment holds at most 256 tokens. `labels`: the value 4 marks a token that is not scored.
All inputs are finite; a program needn't handle non-finite values.
Results may differ from a plain program's by a relative error of at most 0.012.
Values may be sent and summed in bfloat16 or wider, within the bound.
No kernel may reach another device: no remote copies, remote signals or barrier semaphores. Data moves between devices by JAX's collectives and lax.ppermute only.
A program may use at most 256 MiB of HBM per device.

v0:
```python
import functools

import jax
import jax.numpy as jnp
from jax import lax
from jax.experimental import pallas as pl
from jax.experimental.pallas import tpu as pltpu
from jax.sharding import PartitionSpec as P

HEAD_DIM = 32
SEQ = 1024
CLASSES = 4
LONGEST = 256
EPS = 1e-05
QT = 256
KT = 128
GROUP = 4
LANES = 128
LOG2E = 1.4426950408889634
SCALE = HEAD_DIM**-0.5
MASKED = -1e30
VMEM_LIMIT = 58 * 1024 * 1024
VEC_BLOCK, VEC_AT = 2, 64
VEC_LAST = VEC_BLOCK * 128 + VEC_AT + 7
bf16, f32 = jnp.bfloat16, jnp.float32

NN = (((1,), (0,)), ((), ()))
NT = (((1,), (1,)), ((), ()))
TN = (((0,), (0,)), ((), ()))

PHI_P = 0.33
PHI_C = (
    0.1328227541618569,
    0.117797452145417,
    0.18652846971894854,
    -0.09893620415601319,
    0.3406397450924515,
    -0.22542553879715763,
    0.046573313873415075,
)


def mm(left, right, dims=NN):
    return lax.dot_general(left, right, dims, preferred_element_type=f32)


def normal_cdf(u):
    bell = jnp.exp(-0.5 * (u * u))
    t = 1.0 / (1.0 + PHI_P * jnp.abs(u))
    tail = jnp.full_like(t, PHI_C[-1])
    for c in PHI_C[-2::-1]:
        tail = tail * t + c
    tail = tail * t * bell
    return jnp.where(u >= 0, 1.0 - tail, tail), bell * 0.3989422804014327


def head_only(block, h, axis):
    index = lax.broadcasted_iota(jnp.int32, block.shape, axis)
    keep = (index >= h * HEAD_DIM) & (index < (h + 1) * HEAD_DIM)
    return jnp.where(keep, block, jnp.zeros_like(block))


def key_bias(segk_ref, segq_ref, start, window):
    segk = segk_ref[pl.ds(start, window), :]
    segk = jnp.concatenate([segk] * (QT // LANES), axis=1)
    return jnp.where(segk == segq_ref[0:1, :], 0.0, MASKED).astype(f32)


def attend_forward(start_ref, small_ref, q_ref, k_ref, vt_ref, segk_ref, segq_ref, *refs):
    att_ref, lse_ref = refs[-2:]
    tile = pl.program_id(1)

    def run(window):
        start = pl.multiple_of(start_ref[tile] * KT, KT)
        keys = k_ref[pl.ds(start, window), :]
        bias = key_bias(segk_ref, segq_ref, start, window)
        q = q_ref[...]
        for h in range(GROUP):
            rows = slice(h * HEAD_DIM, (h + 1) * HEAD_DIM)
            scores = mm(keys, head_only(q, h, 0)) + bias
            top = jnp.max(scores, axis=0, keepdims=True)
            probs = jnp.exp2((scores - top) * (SCALE * LOG2E))
            total = jnp.sum(probs, axis=0, keepdims=True)
            out = mm(vt_ref[rows, pl.ds(start, window)], probs.astype(bf16))
            att_ref[rows, :] = (out / total).astype(bf16)
            lse_ref[h : h + 1, :] = top * (SCALE * LOG2E) + jnp.log2(total)

    @pl.when(small_ref[tile] == 1)
    def _():
        run(4 * KT)

    @pl.when(small_ref[tile] == 0)
    def _():
        run(6 * KT)


def attend_backward(
    start_ref, small_ref, qt_ref, kt_ref, k_ref, v_ref, dot_ref, att_ref, lse_ref, segk_ref, segq_ref, *refs
):
    dqt_ref, dk_ref, dv_ref, dk_sum, dv_sum = refs[-5:]
    tile = pl.program_id(1)

    @pl.when(tile == 0)
    def _():
        dk_sum[...] = jnp.zeros_like(dk_sum)
        dv_sum[...] = jnp.zeros_like(dv_sum)

    def run(window):
        start = pl.multiple_of(start_ref[tile] * KT, KT)
        at = pl.ds(start, window)
        keys, values = k_ref[at, :], v_ref[at, :]
        bias = key_bias(segk_ref, segq_ref, start, window)
        qt, dot = qt_ref[...], dot_ref[...]
        q, do = qt.T, dot.T
        inner = dot.astype(f32) * att_ref[...].astype(f32)
        dk = jnp.zeros((window, LANES), f32)
        dv = jnp.zeros((window, LANES), f32)
        for h in range(GROUP):
            rows = slice(h * HEAD_DIM, (h + 1) * HEAD_DIM)
            delta = jnp.sum(inner[rows, :], axis=0, keepdims=True)
            scores = mm(keys, head_only(qt, h, 0)) * (SCALE * LOG2E)
            probs = jnp.exp2((scores - lse_ref[h : h + 1, :]) + bias)
            dv = dv + mm(probs.astype(bf16), head_only(do, h, 1))
            grad_probs = mm(values, head_only(dot, h, 0))
            grad_scores = (probs * (grad_probs - delta)).astype(bf16)
            dk = dk + mm(grad_scores, head_only(q, h, 1))
            dq = mm(kt_ref[rows, at], grad_scores)
            dqt_ref[rows, :] = (dq * SCALE).astype(bf16)
        dk_sum[at, :] += dk
        dv_sum[at, :] += dv

    @pl.when(small_ref[tile] == 1)
    def _():
        run(4 * KT)

    @pl.when(small_ref[tile] == 0)
    def _():
        run(6 * KT)

    @pl.when(tile == pl.num_programs(1) - 1)
    def _():
        dk_ref[...] = (dk_sum[...] * SCALE).astype(bf16)
        dv_ref[...] = dv_sum[...].astype(bf16)


def attention_specs(span, begin):
    spec = pl.BlockSpec
    return {
        "q_cols": spec((LANES, QT), lambda g, j, *_: (g + begin, j)),
        "k_cols": spec((LANES, span), lambda g, j, *_: (g + begin, 0)),
        "k_rows": spec((span, LANES), lambda g, j, *_: (0, g + begin)),
        "lse": spec((8, QT), lambda g, j, *_: (g + begin, j)),
        "segk": spec((span, LANES), lambda g, j, *_: (0, 0)),
        "segq": spec((8, QT), lambda g, j, *_: (0, j)),
    }


def run_forward(starts, small, qt, k, vt, segk, segq, span_of_groups, outs=()):
    D, rows = qt.shape
    span = k.shape[0]
    begin, end = span_of_groups
    s = attention_specs(span, begin)
    groups = D // LANES
    outs = tuple(outs)
    return pl.pallas_call(
        attend_forward,
        grid_spec=pltpu.PrefetchScalarGridSpec(
            num_scalar_prefetch=2,
            grid=(end - begin, rows // QT),
            in_specs=[s["q_cols"], s["k_rows"], s["k_cols"], s["segk"], s["segq"]]
            + [pl.BlockSpec(memory_space=pl.ANY)] * len(outs),
            out_specs=[s["q_cols"], s["lse"]],
        ),
        input_output_aliases={7: 0, 8: 1} if outs else {},
        out_shape=[
            jax.ShapeDtypeStruct((D, rows), bf16),
            jax.ShapeDtypeStruct((groups * 8, rows), f32),
        ],
        name="attend_forward",
        **kernel_params(6 * (end - begin)),
    )(starts, small, qt, k, vt, segk, segq, *outs)


def run_backward(starts, small, qt, kt, k, v, dot, att, lse, segk, segq, span_of_groups, outs=()):
    D, rows = qt.shape
    span = k.shape[0]
    begin, end = span_of_groups
    s = attention_specs(span, begin)
    outs = tuple(outs)
    return pl.pallas_call(
        attend_backward,
        grid_spec=pltpu.PrefetchScalarGridSpec(
            num_scalar_prefetch=2,
            grid=(end - begin, rows // QT),
            in_specs=[
                s["q_cols"], s["k_cols"], s["k_rows"], s["k_rows"], s["q_cols"], s["q_cols"],
                s["lse"], s["segk"], s["segq"],
            ]
            + [pl.BlockSpec(memory_space=pl.ANY)] * len(outs),
            out_specs=[s["q_cols"], s["k_rows"], s["k_rows"]],
            scratch_shapes=[pltpu.VMEM((span, LANES), f32), pltpu.VMEM((span, LANES), f32)],
        ),
        out_shape=[
            jax.ShapeDtypeStruct((D, rows), bf16),
            jax.ShapeDtypeStruct((span, D), bf16),
            jax.ShapeDtypeStruct((span, D), bf16),
        ],
        input_output_aliases={11: 0, 12: 1, 13: 2} if outs else {},
        name="attend_backward",
        **kernel_params(7 * (end - begin)),
    )(starts, small, qt, kt, k, v, dot, att, lse, segk, segq, *outs)


def norm_parts(cols):
    centre = jnp.mean(cols, axis=0, keepdims=True)
    shifted = cols - centre
    spread = jnp.mean(jnp.square(shifted), axis=0, keepdims=True)
    scale = lax.rsqrt(spread + EPS)
    return shifted * scale, scale


def norm_back(grad, xhat, scale, gain):
    e = grad * gain
    mean_e = jnp.mean(e, axis=0, keepdims=True)
    mean_ex = jnp.mean(e * xhat, axis=0, keepdims=True)
    return scale * (e - mean_e - xhat * mean_ex)


VECTORS = ("gain_one", "shift_one", "q_bias", "v_bias", "bias_out", "gain_two", "shift_two", "bias_down")


def vector(vec_ref, name):
    i = VEC_AT + VECTORS.index(name)
    return vec_ref[:, i : i + 1].astype(f32)


def fold(x):
    return sum(x[:, i : i + LANES] for i in range(0, x.shape[1], LANES))


def row_sums(parts):
    rows = [jnp.sum(part.T, axis=0, keepdims=True) for part in parts]
    return jnp.concatenate(rows + [jnp.zeros((8 - len(rows), rows[0].shape[1]), f32)], axis=0)


def whole(shape, block=None):
    return pl.BlockSpec(shape, lambda *_: (0,) * len(shape) if block is None else block)


def kernel_params(micros):
    return {
        "compiler_params": pltpu.CompilerParams(vmem_limit_bytes=VMEM_LIMIT),
        "cost_estimate": pl.CostEstimate(flops=micros * 10**9, bytes_accessed=10**6, transcendentals=0),
    }


def project(parts, count, member_ref, x_ref, vec_ref, *refs):
    pieces, refs = refs[:count], refs[count:]
    n_ref, qt_ref, kt_ref, vt_ref, k_ref, v_ref, w_ref, w, wt, in_sem, out_sem = refs
    i = pl.program_id(0)
    out = pltpu.make_async_copy(w, w_ref, out_sem)

    @pl.when(i == 0)
    def _():
        copies = []
        for piece, first, rows, c, mask in parts:
            at = pl.multiple_of((member_ref[0] ^ mask) * rows, 16)
            copy = pltpu.make_async_copy(
                pieces[piece].at[first : first + rows], w.at[c, pl.ds(at, rows)], in_sem.at[len(copies)]
            )
            copy.start()
            copies.append(copy)
        for copy in copies:
            copy.wait()
        out.start()
        for c in range(3):
            wt[c] = w[c].T

    xhat, _ = norm_parts(x_ref[...].astype(f32))
    normed = (xhat * vector(vec_ref, "gain_one") + vector(vec_ref, "shift_one")).astype(bf16)
    n_ref[...] = normed
    kt = mm(wt[1], normed).astype(bf16)
    vt = (mm(wt[2], normed) + vector(vec_ref, "v_bias")).astype(bf16)
    kt_ref[...], vt_ref[...] = kt, vt
    k_ref[...], v_ref[...] = kt.T, vt.T

    @pl.when((i >= 1) & (i < pl.num_programs(0) - 1))
    def _():
        qt_ref[...] = (mm(wt[0], normed) + vector(vec_ref, "q_bias")).astype(bf16)

    @pl.when(i == pl.num_programs(0) - 1)
    def _():
        out.wait()


def run_project(x, vec, member, pieces, parts):
    D, span = x.shape
    steps = span // QT
    cols = pl.BlockSpec((D, QT), lambda i, _: (0, i))
    rows = pl.BlockSpec((QT, D), lambda i, _: (i, 0))
    own = pl.BlockSpec((D, QT), lambda i, _: (0, jnp.clip(i - 1, 0, steps - 3)))
    anywhere = pl.BlockSpec(memory_space=pl.ANY)
    shape = jax.ShapeDtypeStruct
    return pl.pallas_call(
        functools.partial(project, parts, len(pieces)),
        grid_spec=pltpu.PrefetchScalarGridSpec(
            num_scalar_prefetch=1,
            grid=(steps,),
            in_specs=[cols, whole((D, LANES), (0, VEC_BLOCK))] + [anywhere] * len(pieces),
            out_specs=[cols, own, cols, cols, rows, rows, anywhere],
            scratch_shapes=[
                pltpu.VMEM((4, D, D), bf16),
                pltpu.VMEM((3, D, D), bf16),
                pltpu.SemaphoreType.DMA((len(parts),)),
                pltpu.SemaphoreType.DMA,
            ],
        ),
        out_shape=[
            shape((D, span), bf16),
            shape((D, span - 2 * QT), bf16),
            shape((D, span), bf16),
            shape((D, span), bf16),
            shape((span, D), bf16),
            shape((span, D), bf16),
            shape((4, D, D), bf16),
        ],
        name="project",
        **kernel_params(11),
    )(member, x, vec, *pieces)


def project_weights(masks, member_ref, n_ref, dqt_ref, dk_ref, dv_ref, gwo_ref, *refs):
    outs, (sums_ref, gw, sem) = refs[:-3], refs[-3:]
    rows = dqt_ref.shape[1]
    halo = (n_ref.shape[1] - rows) // 2
    copies = []

    def send(c):
        if not masks:
            targets = [(gw.at[c], outs[0].at[c])]
        else:
            run = outs[0].shape[2]
            targets = []
            for far in (1, 0):
                for i, mask in enumerate(masks):
                    at = pl.multiple_of((member_ref[0] ^ (mask | far * CORE)) * run, 16)
                    targets.append((gw.at[c, pl.ds(at, run)], outs[far].at[i, c]))
        for source, target in targets:
            copy = pltpu.make_async_copy(source, target, sem.at[len(copies)])
            copy.start()
            copies.append(copy)

    gw[3] = gwo_ref[...]
    send(3)
    gw[0] = mm(n_ref[:, halo : halo + rows], dqt_ref[...], NT).astype(bf16)
    send(0)
    gw[1] = mm(n_ref[...], dk_ref[...]).astype(bf16)
    send(1)
    gw[2] = mm(n_ref[...], dv_ref[...]).astype(bf16)
    send(2)
    sums_ref[...] = row_sums([fold(dqt_ref[...].astype(f32))])
    sums_ref[1:2, :] = jnp.sum(dv_ref[...].astype(f32), axis=0, keepdims=True)
    for copy in copies:
        copy.wait()


def run_project_weights(normed, dqt, dk, dv, gwo, member, masks, run):
    D = normed.shape[0]
    shape = jax.ShapeDtypeStruct
    vmem, anywhere = pl.BlockSpec(memory_space=pltpu.VMEM), pl.BlockSpec(memory_space=pl.ANY)
    outs = [shape((len(masks), 4, run, D), bf16)] * 2 if masks else [shape((4, D, D), bf16)]
    return pl.pallas_call(
        functools.partial(project_weights, masks),
        in_specs=[pl.BlockSpec(memory_space=pltpu.SMEM)] + [vmem] * 5,
        out_specs=[anywhere] * len(outs) + [vmem],
        out_shape=outs + [shape((8, D), f32)],
        scratch_shapes=[pltpu.VMEM((4, D, D), bf16), pltpu.SemaphoreType.DMA((8 * max(1, len(masks)),))],
        name="project_weights",
        **kernel_params(8),
    )(member, normed, dqt, dk, dv, gwo)


def project_back(x_ref, dqt_ref, dk_ref, dv_ref, w_ref, mid_ref, vec_ref, grad_ref, rows_ref, sums_ref):
    i = pl.program_id(0)
    own = (i >= 1) & (i < pl.num_programs(0) - 1)

    @pl.when(i == 0)
    def _():
        sums_ref[...] = jnp.zeros_like(sums_ref)

    dqt = jnp.where(own, dqt_ref[...], jnp.zeros_like(dqt_ref))
    grad = mm(w_ref[1], dk_ref[...], NT) + mm(w_ref[2], dv_ref[...], NT) + mm(w_ref[0], dqt)
    xhat, scale = norm_parts(x_ref[...].astype(f32))
    sums_ref[0] += fold(grad * xhat)
    sums_ref[1] += fold(grad)
    grad_in = norm_back(grad, xhat, scale, vector(vec_ref, "gain_one"))
    grad_ref[...] = (grad_in + jnp.where(own, mid_ref[...], 0.0)).astype(bf16)

    @pl.when(i == pl.num_programs(0) - 1)
    def _():
        rows_ref[...] = row_sums([sums_ref[0], sums_ref[1]])


def run_project_back(x, dqt, dk, dv, w, grad_mid, vec):
    D, span = x.shape
    steps = span // QT
    cols = pl.BlockSpec((D, QT), lambda i: (0, i))
    rows = pl.BlockSpec((QT, D), lambda i: (i, 0))
    own = pl.BlockSpec((D, QT), lambda i: (0, jnp.clip(i - 1, 0, steps - 3)))
    shape = jax.ShapeDtypeStruct
    return pl.pallas_call(
        project_back,
        grid=(steps,),
        in_specs=[cols, own, rows, rows, whole((3, D, D)), own, whole((D, LANES), (0, VEC_BLOCK))],
        out_specs=[cols, whole((8, D))],
        out_shape=[shape((D, span), bf16), shape((8, D), f32)],
        scratch_shapes=[pltpu.VMEM((2, D, LANES), f32)],
        name="project_back",
        **kernel_params(10),
    )(x, dqt, dk, dv, w, grad_mid, vec)


def branch(att_ref, wo_ref, x_ref, vec_ref, mid_ref, n_ref):
    out = mm(wo_ref[0], att_ref[...]) + vector(vec_ref, "bias_out")
    middle = x_ref[...].astype(f32) + out
    mid_ref[...] = middle
    xhat, _ = norm_parts(middle)
    n_ref[...] = (xhat * vector(vec_ref, "gain_two") + vector(vec_ref, "shift_two")).astype(bf16)


def run_branch(att, w, x, vec):
    D, rows = att.shape
    cols = pl.BlockSpec((D, QT), lambda i: (0, i))
    return pl.pallas_call(
        branch,
        grid=(rows // QT,),
        in_specs=[
            cols,
            whole((1, D, D), (3, 0, 0)),
            pl.BlockSpec((D, QT), lambda i: (0, i + LONGEST // QT)),
            whole((D, LANES), (0, VEC_BLOCK)),
        ],
        out_specs=[cols, cols],
        out_shape=[jax.ShapeDtypeStruct((D, rows), f32), jax.ShapeDtypeStruct((D, rows), bf16)],
        name="branch",
        **kernel_params(5),
    )(att, w, x, vec)


def branch_back(
    gn_ref, got_ref, mid_ref, g_ref, att_ref, wo_ref, vec_ref,
    gmid_ref, gatt_ref, gwo_ref, rows_ref, wo, gwo_sum, sums_ref,
):
    i = pl.program_id(0)

    @pl.when(i == 0)
    def _():
        wo[...] = wo_ref[0].T
        gwo_sum[...] = jnp.zeros_like(gwo_sum)
        sums_ref[...] = jnp.zeros_like(sums_ref)

    grad = gn_ref[...] + got_ref[...].astype(f32)
    xhat, scale = norm_parts(mid_ref[...])
    g = g_ref[...].astype(f32)
    grad_mid = g + norm_back(grad, xhat, scale, vector(vec_ref, "gain_two"))
    gmid_ref[...] = grad_mid
    low = grad_mid.astype(bf16)
    gatt_ref[...] = mm(wo[...], low).astype(bf16)
    gwo_sum[...] += mm(low, att_ref[...], NT)
    sums_ref[0] += fold(low.astype(f32))
    sums_ref[1] += fold(grad * xhat)
    sums_ref[2] += fold(grad)
    sums_ref[3] += fold(g)

    @pl.when(i == pl.num_programs(0) - 1)
    def _():
        gwo_ref[...] = gwo_sum[...].astype(bf16)
        rows_ref[...] = row_sums([sums_ref[i] for i in range(4)])


def run_branch_back(gn, got, middle, g, att, w, vec):
    D, rows = att.shape
    cols = pl.BlockSpec((D, QT), lambda i: (0, i))
    shape = jax.ShapeDtypeStruct
    return pl.pallas_call(
        branch_back,
        grid=(rows // QT,),
        in_specs=[
            cols, cols, cols, cols, cols,
            whole((1, D, D), (3, 0, 0)),
            whole((D, LANES), (0, VEC_BLOCK)),
        ],
        out_specs=[cols, cols, whole((D, D)), whole((8, D))],
        out_shape=[
            shape((D, rows), f32),
            shape((D, rows), bf16),
            shape((D, D), bf16),
            shape((8, D), f32),
        ],
        scratch_shapes=[pltpu.VMEM((D, D), bf16), pltpu.VMEM((D, D), f32), pltpu.VMEM((4, D, LANES), f32)],
        name="branch_back",
        **kernel_params(9),
    )(gn, got, middle, g, att, w, vec)


def feed_forward(first, places, *refs):
    blocks, weights = len(places), 1 + max(p[0] for place in places for p in place)
    n2_in, g_in, refs = refs[0:2], refs[2:4], refs[4:]
    weights, refs = refs[:weights], refs[weights:]
    if not first:
        sums_in, refs = refs[:4], refs[4:]
    sums_out, refs = refs[:4], refs[4:]
    dw_out, refs = refs[: 2 * blocks], refs[2 * blocks :]
    dub_out, refs = refs[:blocks], refs[blocks:]
    n2, g, up, dt, ub, up_t, down, act, gh, dw, sums, low, in_sem, out_sem = refs
    D, F = up.shape
    f, rows = F // blocks, n2.shape[2]

    arrivals = {}

    def fetch(name, source, target):
        copy = pltpu.make_async_copy(source, target, in_sem.at[len(arrivals)])
        copy.start()
        arrivals[name] = copy

    def weight(name, target, b, part):
        ref, at = places[b][part]
        fetch((name, b), weights[ref].at[:, at : at + f], target.at[:, b * f : (b + 1) * f])

    for b in range(blocks):
        weight("up", up, b, 0)
    fetch("n2", n2_in[0], n2.at[0])
    for b in range(blocks):
        weight("dt", dt, b, 1)
        ref, at = places[b][2]
        fetch(("ub", b), weights[ref].at[at : at + 16], ub.at[b])
    fetch("g", g_in[0], g.at[0])
    fetch("n2 other", n2_in[1], n2.at[1])
    fetch("g other", g_in[1], g.at[1])
    if not first:
        for i in range(4):
            fetch(("sum", i), sums_in[i], low.at[i])

    departures = []

    def send(source, target):
        copy = pltpu.make_async_copy(source, target, out_sem.at[len(departures)])
        copy.start()
        departures.append(copy)

    columns = []
    for b in range(blocks):
        arrivals["up", b].wait()
        up_t[b * f : (b + 1) * f, :] = up[:, b * f : (b + 1) * f].T
    for b in range(blocks):
        arrivals["dt", b].wait()
        down[b * f : (b + 1) * f, :] = dt[:, b * f : (b + 1) * f].T
        arrivals["ub", b].wait()
        column = ub[b, :, :f].astype(f32).T[:, 0:1]
        columns.append(jnp.broadcast_to(column, (f, LANES)))
    bias = jnp.concatenate([jnp.concatenate(columns, axis=0)] * (QT // LANES), axis=1)
    arrivals["n2"].wait()
    arrivals["g"].wait()

    chunks = [(half, at) for half in range(2) for at in range(0, rows, QT)]

    def front(chunk):
        half, at = chunk
        if half == 1 and at == 0:
            arrivals["n2 other"].wait()
            arrivals["g other"].wait()
        return mm(up_t[...], n2[half, :, at : at + QT]), mm(down[...], g[half, :, at : at + QT])

    dub = jnp.zeros((F, LANES), f32)
    ready = front(chunks[0])
    for i, (half, at) in enumerate(chunks):
        following = front(chunks[i + 1]) if i + 1 < len(chunks) else None
        hidden, grad_act = ready
        hidden = hidden + bias
        cdf, pdf = normal_cdf(hidden)
        act[half, :, at : at + QT] = (hidden * cdf).astype(bf16)
        grad_hidden = (grad_act * (cdf + hidden * pdf)).astype(bf16)
        gh[half, :, at : at + QT] = grad_hidden
        dub = dub + fold(grad_hidden.astype(f32))
        ready = following
    for b in range(blocks):
        dub_out[b][...] = row_sums([dub[b * f : (b + 1) * f]])
    for part, (left, right) in enumerate(((n2, gh), (g, act))):
        dw[part] = (mm(left[0], right[0], NT) + mm(left[1], right[1], NT)).astype(bf16)
        for b in range(blocks):
            send(dw.at[part, :, b * f : (b + 1) * f], dw_out[2 * b + part])
    if not first:
        for i in range(4):
            arrivals["sum", i].wait()
    for i, (left, right) in enumerate(((up, gh), (dt, act))):
        for half in (1, 0):
            total = mm(left[...], right[half])
            k = 2 * i + half
            if not first:
                total = total + low[k].astype(f32)
            if half == 1 or first:
                low[k] = total.astype(bf16)
                send(low.at[k], sums_out[k])
            else:
                sums[i] = total
                send(sums.at[i], sums_out[k])
    for copy in departures:
        copy.wait()


def run_feed_forward(n2, g, blocks, sums):
    D, rows = n2[0].shape
    F = D
    first = sums is None
    weights, places = [], []
    for block in blocks:
        place = []
        for array, column in block:
            found = [i for i, w in enumerate(weights) if w is array]
            if not found:
                weights.append(array)
            place.append((found[0] if found else len(weights) - 1, column))
        places.append(place)
    sums = () if first else tuple(sums)
    count = len(blocks)
    shape = jax.ShapeDtypeStruct
    anywhere = pl.BlockSpec(memory_space=pl.ANY)
    vmem = pl.BlockSpec(memory_space=pltpu.VMEM)
    own_type = bf16 if first else f32
    outs = pl.pallas_call(
        functools.partial(feed_forward, first, places),
        in_specs=[anywhere] * (4 + len(weights) + len(sums)),
        out_specs=[anywhere] * (4 + 2 * count) + [vmem] * count,
        out_shape=[shape((D, rows), t) for t in (own_type, bf16, own_type, bf16)]
        + [shape((D, F), bf16)] * (2 * count)
        + [shape((8, F), f32)] * count,
        scratch_shapes=[
            pltpu.VMEM((2, D, rows), bf16),
            pltpu.VMEM((2, D, rows), bf16),
            pltpu.VMEM((D, count * F), bf16),
            pltpu.VMEM((D, count * F), bf16),
            pltpu.VMEM((count, 16, D), bf16),
            pltpu.VMEM((count * F, D), bf16),
            pltpu.VMEM((count * F, D), bf16),
            pltpu.VMEM((2, count * F, rows), bf16),
            pltpu.VMEM((2, count * F, rows), bf16),
            pltpu.VMEM((2, D, count * F), bf16),
            pltpu.VMEM((2, D, rows), f32),
            pltpu.VMEM((4, D, rows), bf16),
            pltpu.SemaphoreType.DMA((3 * count + 8,)),
            pltpu.SemaphoreType.DMA((2 * count + 4,)),
        ],
        name="feed_forward",
        **kernel_params(28),
    )(*n2, *g, *weights, *sums)
    grads = [(*outs[4 + 2 * b : 6 + 2 * b], outs[4 + 2 * count + b]) for b in range(count)]
    return outs[:4], grads


def z_rotate(x, k):
    n = lax.axis_size("narrow")
    return lax.ppermute(x, "narrow", [(i, (i + k) % n) for i in range(n)])


def z_gather(x):
    n, me = lax.axis_size("narrow"), lax.axis_index("narrow")
    stack = jnp.stack([x] + [z_rotate(x, k) for k in range(1, n)])
    return [lax.dynamic_index_in_dim(stack, lax.rem(me - j + n, n), 0, False) for j in range(n)]


def z_scatter_sum(pieces):
    n, me = lax.axis_size("narrow"), lax.axis_index("narrow")
    total = lax.dynamic_index_in_dim(pieces, me, 0, False).astype(f32)
    for k in range(1, n):
        piece = lax.dynamic_index_in_dim(pieces, lax.rem(me + k, n), 0, False)
        total = total + z_rotate(piece, k).astype(f32)
    return total


def swap(x, mask):
    n = lax.axis_size("wide")
    return lax.ppermute(x, "wide", [(i, i ^ mask) for i in range(n)])


def wide_sum(x):
    bit = 1
    while bit < lax.axis_size("wide"):
        x = x + swap(x, bit)
        bit *= 2
    return x


CORE, X, Y = 1, 2, 4


def after(deps, *values):
    n = len(values)
    tied = pl.pallas_call(
        lambda *refs: None,
        in_specs=[pl.BlockSpec(memory_space=pl.ANY)] * (n + len(deps)),
        out_specs=[pl.BlockSpec(memory_space=pl.ANY)] * n,
        out_shape=[jax.ShapeDtypeStruct(v.shape, v.dtype) for v in values],
        input_output_aliases={i: i for i in range(n)},
        name="tie",
    )(*values, *deps)
    return tied if n > 1 else tied[0]


def high_bits():
    bits, bit = [], 8
    while bit < lax.axis_size("wide"):
        bits.append(bit)
        bit *= 2
    return bits


def shards(
    tokens_in,
    ln1_gain,
    ln1_shift,
    w_qkv,
    qv_bias,
    w_out,
    out_bias,
    ln2_gain,
    ln2_shift,
    w_up,
    up_bias,
    w_down,
    down_bias,
    segment_ids,
    out_grad,
    predicted,
    labels,
):
    nn, me = lax.axis_size("narrow"), lax.axis_index("narrow")
    nw, mw = lax.axis_size("wide"), lax.axis_index("wide")
    part, tok = tokens_in.shape
    D = part * nn
    quarter = tok // nn
    halo = LONGEST
    span = quarter + 2 * halo
    high = high_bits()
    dw = w_qkv.shape[1]
    across = lambda x: lax.all_to_all(x, "narrow", 0, 0, tiled=True)

    position = jnp.arange(tok, dtype=jnp.int32)
    chunk = segment_ids * (tok // SEQ) + position // SEQ
    big = jnp.int32(2**30)
    chunk = jnp.concatenate([jnp.full((halo,), -1, jnp.int32), chunk, jnp.full((halo,), big, jnp.int32)])
    chunk = lax.dynamic_slice_in_dim(chunk, me * quarter, span, 0)
    chunk_own = chunk[halo : halo + quarter]
    tiles = quarter // QT
    edges = chunk_own.reshape(tiles, QT)
    low = jnp.sum((chunk[None] < edges[:, :1]).astype(jnp.int32), axis=1) // KT
    top = (jnp.sum((chunk[None] <= edges[:, -1:]).astype(jnp.int32), axis=1) + KT - 1) // KT
    small = (top - low <= 4).astype(jnp.int32)
    starts = jnp.minimum(low, span // KT - jnp.where(small == 1, 4, 6))
    segk = jnp.broadcast_to(chunk[:, None], (span, LANES))
    segq = jnp.broadcast_to(chunk_own[None], (8, quarter))

    piece = [w_qkv.reshape(3 * dw, part).T, w_out]
    piece += [jnp.zeros((part, VEC_BLOCK * LANES + VEC_AT - 4 * dw), bf16)]
    piece += [
        jnp.stack([ln1_gain, ln1_shift, qv_bias[0], qv_bias[1], out_bias, ln2_gain, ln2_shift, down_bias]).T
    ]
    piece = jnp.concatenate(piece, axis=1)
    piece = jnp.pad(piece, ((0, 0), (0, -piece.shape[1] % LANES)))
    vec = across(jnp.stack([piece] * nn)).reshape(D, -1)
    up_own = across(after((vec,), jnp.stack([w_up] * nn))).reshape(D, -1)
    units = up_bias.shape[0]
    bias_rows = jnp.pad(up_bias[None], ((0, 15), (0, D - units)))
    attn_own = after((vec,), jnp.concatenate([vec[:, : 4 * dw].T, bias_rows], axis=0))
    count, height = 1, 4 * dw + 16
    for bit in high:
        attn_own = jnp.concatenate([attn_own, swap(attn_own, bit)], axis=0)
        count *= 2
    cut = attn_own.shape[0] // 2 // 16 * 16
    from_x, from_y = swap(attn_own, X), swap(attn_own, Y)
    from_xy = swap(from_y[:cut], X), swap(from_x[cut:], Y)
    grad_blocks = jnp.stack([out_grad[:, j * quarter : (j + 1) * quarter] for j in range(nn)])
    padded = jnp.pad(tokens_in, ((0, 0), (halo, halo)))
    blocks = jnp.stack([padded[:, j * quarter : j * quarter + span] for j in range(nn)])
    blocks = after((starts, small, segk, segq, up_own, *from_xy, grad_blocks), blocks)
    x_low = across(blocks).reshape(D, span)
    dt_blocks = after((x_low,), jnp.stack([w_down.T] * nn))
    dt_own = across(dt_blocks).reshape(D, -1)
    bias_of = lambda a: jnp.concatenate(
        [a[j * height + 4 * dw : (j + 1) * height, :units] for j in range(count)], axis=1
    )
    if dw % 16 == 0:
        pieces = [attn_own, from_x, from_y, *from_xy]
        pieces += [swap(piece, CORE) for piece in pieces]
        parts = []
        for far in (0, 1):
            for i, mask in enumerate((0, X, Y)):
                parts += [(i + 5 * far, c * dw, dw, c, mask | far * CORE) for c in range(4)]
            for c in range(4):
                for first, last in ((c * dw, min((c + 1) * dw, cut)), (max(c * dw, cut), (c + 1) * dw)):
                    assert last <= first or last - first == dw
                    if last > first:
                        piece, start = (3, first) if last <= cut else (4, first - cut)
                        parts.append((piece + 5 * far, start, dw, c, (X | Y) | far * CORE))
        ub_own, ub_x, ub_y = (attn_own, 4 * dw), (from_x, 4 * dw), (from_y, 4 * dw)
        ub_xy = from_xy[1], 4 * dw - cut
    else:
        from_xy = jnp.concatenate(from_xy, axis=0)
        ub_own, ub_x, ub_y, ub_xy = ((bias_of(a), 0) for a in (attn_own, from_x, from_y, from_xy))
        half = jnp.concatenate([attn_own, from_x, from_y, from_xy], axis=0)
        half = half.reshape(-1, height, D)[:, : 4 * dw].reshape(-1, 4, dw, D)
        every = jnp.concatenate([half, swap(half, CORE)], axis=0)
        bits = high + [X, Y, CORE]
        place = lambda m: sum(((m // bit) % 2) << i for i, bit in enumerate(bits))
        every = [lax.dynamic_index_in_dim(every, place(mw ^ w), 0, True) for w in range(nw)]
        pieces = [jnp.concatenate(every, axis=0).transpose(1, 0, 2, 3).reshape(4 * D, D)]
        parts = [(0, c * D, D, c, 0) for c in range(4)]
    member = jnp.reshape(mw if dw % 16 == 0 else mw * 0, (1,)).astype(jnp.int32)

    for bit in high:
        up_own = jnp.concatenate([up_own, swap(up_own, bit)], axis=1)
    F = up_own.shape[1]
    up_x, up_y = swap(up_own, X), swap(up_own, Y)
    x_low = after((up_x, up_y), x_low)
    normed, qt, kt, vt, k, v, w_attn = run_project(x_low, vec, member, pieces, parts)
    groups = D // LANES
    forward_in = starts, small, qt, k, vt, segk, segq
    att, lse = run_forward(*forward_in, (0, 1))

    dt_own = after((att,), dt_own)
    grad_cols = across(after((dt_own,), grad_blocks)).reshape(D, quarter)
    for bit in high:
        dt_own = jnp.concatenate([dt_own, swap(dt_own, bit)], axis=1)
    dt_x, dt_y = swap(dt_own, X), swap(dt_own, Y)
    up_xy = swap(up_y, X)
    att = after((up_xy,), att)
    att, lse = run_forward(*forward_in, (1, 3), (att, lse))
    dt_x = after((att,), dt_x)
    dt_xy = swap(dt_x, Y)
    att, lse = run_forward(*forward_in, (3, groups), (att, lse))
    grad_cols = after((att,), grad_cols)
    grad_pair = grad_cols, swap(grad_cols, CORE)
    middle, normed_two = run_branch(att, w_attn, x_low, vec)

    normed_two = after((dt_xy,), normed_two)
    n2_pair = normed_two, swap(normed_two, CORE)
    blocks = [((up_xy, 0), (dt_xy, 0), ub_xy), ((up_x, 0), (dt_x, 0), ub_x)]
    sums, ((up_gxy, dt_gxy, ub_gxy), (up_gx, dt_gx, ub_gx)) = run_feed_forward(n2_pair, grad_pair, blocks, None)
    up_got_xy, dt_got_xy = swap(up_gxy, X), swap(dt_gxy, Y)
    blocks = [((up_y, 0), (dt_y, 0), ub_y), ((up_own, 0), (dt_own, 0), ub_own)]
    sums, ((up_gy, dt_gy, ub_gy), (up_g, dt_g, ub_g)) = run_feed_forward(n2_pair, grad_pair, blocks, sums)
    gn_sum, gn_other, out_sum, out_other = sums
    ub_g, ub_gx, ub_gy, ub_gxy = (rows[0] for rows in (ub_g, ub_gx, ub_gy, ub_gxy))
    gn_other = after((up_got_xy, dt_got_xy), gn_other)
    gn_got, out_got = swap(gn_other, CORE), swap(out_other, CORE)

    layer = (middle + (out_sum + out_got.astype(f32) + vec[:, VEC_LAST : VEC_LAST + 1].astype(f32))).astype(bf16)
    layer_out = across(layer.reshape(nn, part, quarter)).transpose(1, 0, 2).reshape(part, tok)

    add = lambda *terms: sum(t.astype(f32) for t in terms)
    up_gy = add(up_gy, up_got_xy).astype(bf16)
    up_got = swap(up_gx, X), swap(up_gy, Y)

    gn_got = after((layer,), gn_got)
    grad_mid, grad_att, grad_wo_t, sums_two = run_branch_back(
        gn_sum, gn_got, middle, grad_cols, att, w_attn, vec
    )
    back_in = starts, small, qt, kt, k, v, grad_att, att, lse, segk, segq
    dt_gx = add(dt_gx, dt_got_xy).astype(bf16)
    dt_got = swap(dt_gx, X), swap(dt_gy, Y)
    back_a = run_backward(*back_in, (0, 2))
    up_got_x, up_got_y, dt_got_x, dt_got_y = after((back_a[0],), *up_got, *dt_got)
    up_g, dt_g = add(up_g, up_got_x, up_got_y), add(dt_g, dt_got_x, dt_got_y)
    for bit in reversed(high):
        half = up_g.shape[1] // 2
        up_g = up_g[:, :half] + swap(up_g[:, half:].astype(bf16), bit).astype(f32)
        dt_g = dt_g[:, :half] + swap(dt_g[:, half:].astype(bf16), bit).astype(f32)
    ud_g = jnp.concatenate([up_g, dt_g], axis=1).astype(bf16)
    ud_grad = across(ud_g.reshape(nn, part, -1))
    dqt_a = after((ud_g, layer_out), back_a[0])
    dqt, dk, dv = run_backward(*back_in, (2, groups), (dqt_a, *back_a[1:]))
    ub_gx, ub_gy, ub_gxy = after((back_a[1],), ub_gx, ub_gy, ub_gxy)
    ub_g = ub_g + swap(ub_gx, X) + swap(ub_gy, Y) + swap(ub_gxy, X | Y)
    for bit in reversed(high):
        cut = ub_g.shape[0] // 2
        ub_g = ub_g[:cut] + swap(ub_g[cut:], bit)
    ub_g = jnp.pad(ub_g[None], ((0, 0), (0, D - units)))
    dqt = after((ub_g,), dqt)
    masks = [0]
    for bit in high:
        masks = masks + [m ^ bit for m in masks]
    masks = [m ^ b for b in (0, X, Y, X | Y) for m in masks]
    direct = masks if dw % 16 == 0 else []
    *grad_w, qv_rows = run_project_weights(normed, dqt, dk, dv, grad_wo_t, member, direct, dw)
    if not direct:
        grad_w = grad_w[0].reshape(4, nw, dw, D).transpose(1, 0, 2, 3)
        pick = lambda masks: jnp.concatenate(
            [lax.dynamic_index_in_dim(grad_w, mw ^ m, 0, True) for m in masks], axis=0
        )
        grad_w = pick(masks), pick([m ^ CORE for m in masks])
    attn_g, got = grad_w[0], swap(grad_w[1], CORE)
    dqt = after((grad_w[1], ud_grad), dqt)
    grad_in, sums_one = run_project_back(x_low, dqt, dk, dv, w_attn, grad_mid, vec)
    got = after((grad_in,), got)
    vector_rows = jnp.concatenate([sums_one[:2], qv_rows[:2], sums_two[:4]])
    ud_grad = jnp.sum(ud_grad.reshape(nn, part, -1).astype(f32), axis=0)
    up_grad, down_grad = ud_grad[:, :units], ud_grad[:, units:].T
    grad_in = across(grad_in.reshape(nn, part, span)).astype(f32)
    tokens_grad = sum(
        jnp.pad(grad_in[j], ((0, 0), (j * quarter, tok - (j + 1) * quarter))) for j in range(nn)
    )[:, halo : halo + tok]

    half = add(attn_g, got).astype(bf16)
    g0, gx, gy, gxy = (half[i * count : (i + 1) * count] for i in range(4))
    gy_low = add(gy[:, :2], swap(gxy[:, :2], X)).astype(bf16)
    gx_high = add(gx[:, 2:], swap(gxy[:, 2:], Y)).astype(bf16)
    gx = jnp.concatenate([gx[:, :2], gx_high], axis=1)
    gy = jnp.concatenate([gy_low, gy[:, 2:]], axis=1)
    g0 = add(g0, swap(gx, X), swap(gy, Y))
    for bit in reversed(high):
        cut = g0.shape[0] // 2
        g0 = g0[:cut] + swap(g0[cut:].astype(bf16), bit).astype(f32)
    g0 = g0[0].astype(bf16).reshape(4 * dw, D).T.reshape(nn, part, 4 * dw)
    g0 = after((grad_in,), g0)
    vector_rows = after((g0,), vector_rows)
    attn_grad = jnp.sum(across(g0).reshape(nn, part, 4 * dw).astype(f32), axis=0)
    qkv_grad = attn_grad[:, : 3 * dw].T.reshape(3, dw, part)
    out_weight_grad = attn_grad[:, 3 * dw :]

    class_ids = jnp.arange(CLASSES, dtype=jnp.int32)
    label_hits = labels[:, None] == class_ids
    counts = jnp.stack(
        [
            jnp.sum(((predicted[:, None] == class_ids) & label_hits).astype(f32), axis=0),
            jnp.sum(label_hits.astype(f32), axis=0),
        ]
    )
    counts = jnp.pad(counts.reshape(1, -1), ((0, 0), (0, D - counts.size)))
    sums = wide_sum(jnp.concatenate([vector_rows, counts]))
    counts = sums[8, : 2 * CLASSES].reshape(2, CLASSES)
    sums = jnp.concatenate([sums[:8], ub_g])
    sums = sums + sum(z_rotate(sums, r) for r in range(1, nn))
    ub_g = sums[8, :units]
    sums = lax.dynamic_slice_in_dim(sums[:8], me * part, part, 1)
    gain_one_g, shift_one_g, q_bias_g, v_bias_g, out_bias_g, gain_two_g, shift_two_g, down_bias_g = sums
    tallies = counts.astype(jnp.int32)
    accuracy = jnp.sum(counts[0]) / jnp.maximum(jnp.sum(counts[1]), 1.0)
    return (
        layer_out,
        tokens_grad,
        gain_one_g,
        shift_one_g,
        qkv_grad,
        jnp.stack([q_bias_g, v_bias_g]),
        out_weight_grad,
        out_bias_g,
        gain_two_g,
        shift_two_g,
        up_grad,
        ub_g,
        down_grad,
        down_bias_g,
        tallies,
        accuracy,
    )


def solution(mesh):
    return jax.shard_map(
        shards,
        mesh=mesh,
        in_specs=(
            P("narrow", "wide"),
            P("narrow"),
            P("narrow"),
            P(None, "wide", "narrow"),
            P(None, "narrow"),
            P("narrow", "wide"),
            P("narrow"),
            P("narrow"),
            P("narrow"),
            P("narrow", "wide"),
            P("wide"),
            P("wide", "narrow"),
            P("narrow"),
            P("wide"),
            P("narrow", "wide"),
            P("wide"),
            P("wide"),
        ),
        out_specs=(
            P("narrow", "wide"),
            P("narrow", "wide"),
            P("narrow"),
            P("narrow"),
            P(None, "wide", "narrow"),
            P(None, "narrow"),
            P("narrow", "wide"),
            P("narrow"),
            P("narrow"),
            P("narrow"),
            P("narrow", "wide"),
            P("wide"),
            P("wide", "narrow"),
            P("narrow"),
            P(),
            P(),
        ),
        check_vma=False,
    )
```

profile of v0, /device:TPU:0, one launch (start us, length us, event | category | flops | bytes accessed | tf_op | source)
XLA Modules:
  0.0 421.1 jit_solution(4472582398161846665)
XLA Ops:
  8.2 6.3 %all-to-all-start = ((bf16[4,160,384]{2,1,0:T(8,128)(2,1)}), bf16[4,160,384]{2,1,0:T(8,128)(2,1)S(1)}, u32[]{:S(2)}, u32[]{:S(2)}) async-start(bf16[4,160,384]{2,1,0:T(8,128)(2,1)} %stack.98), calls=%async_computation | async-start | bytes 983040 | tf_op jit(solution)/shard_map/all_to_all | solution.py:745
  17.8 10.5 %all-to-all-done = bf16[4,160,384]{2,1,0:T(8,128)(2,1)S(1)} async-done(((bf16[4,160,384]{2,1,0:T(8,128)(2,1)}), bf16[4,160,384]{2,1,0:T(8,128)(2,1)S(1)}, u32[]{:S(2)}, u32[]{:S(2)}) %all-to-all-start) | async-done | bytes 491552 | tf_op jit(solution)/shard_map/all_to_all | solution.py:745
  39.0 6.3 %collective-permute-done.2.refs_1_.refs_9_ = bf16[336,640]{1,0:T(8,128)(2,1)S(1)} collective-permute-done((bf16[336,640]{1,0:T(8,128)(2,1)}, bf16[336,640]{1,0:T(8,128)(2,1)S(1)}, u32[]{:S(2)}, u32[]{:S(2)}) %collective-permute-start.2) | collective-permute-done | bytes 430112 | tf_op jit(solution)/shard_map/ppermute | solution.py:682
  55.2 5.0 %all-to-all-start.2 = ((bf16[4,160,1280]{2,1,0:T(8,128)(2,1)}), bf16[4,160,1280]{2,1,0:T(8,128)(2,1)S(1)}, u32[]{:S(2)}, u32[]{:S(2)}) async-start(bf16[4,160,1280]{2,1,0:T(8,128)(2,1)} %tie.23), calls=%async_computation.2 | async-start | bytes 3276800 | tf_op jit(solution)/shard_map/all_to_all | solution.py:745
  62.5 15.7 %collective-permute-done.4.refs_1_.refs_7_ = bf16[640,640]{1,0:T(8,128)(2,1)S(1)} collective-permute-done((bf16[640,640]{1,0:T(8,128)(2,1)S(1)}, bf16[640,640]{1,0:T(8,128)(2,1)S(1)}, u32[]{:S(2)}, u32[]{:S(2)}) %collective-permute-start.4) | collective-permute-done | bytes 819232 | tf_op jit(solution)/shard_map/ppermute | solution.py:682
  80.2 16.4 %all-to-all-done.2 = bf16[4,160,1280]{2,1,0:T(8,128)(2,1)S(1)} async-done(((bf16[4,160,1280]{2,1,0:T(8,128)(2,1)}), bf16[4,160,1280]{2,1,0:T(8,128)(2,1)S(1)}, u32[]{:S(2)}, u32[]{:S(2)}) %all-to-all-start.2) | async-done | bytes 1638432 | tf_op jit(solution)/shard_map/all_to_all | solution.py:745
  104.3 12.4 %project.1 = (bf16[640,1280]{1,0:T(8,128)(2,1)}, bf16[640,768]{1,0:T(8,128)(2,1)}, bf16[640,1280]{1,0:T(8,128)(2,1)}, bf16[640,1280]{1,0:T(8,128)(2,1)}, bf16[12...) custom-call(s32[1]{0:T(128)} %bitcast.member_ref, bf16[640,1280]{1,0:T(8,128)(2,1)} %tie.24.x_ref, ...), custom_call_target="tpu_custom_call" | custom-call | flops 11000000512 | bytes 1000000 | tf_op jit(solution)/shard_map/project/pallas_call | solution.py:304
  116.6 7.7 %attend_forward.3 = (bf16[640,768]{1,0:T(8,128)(2,1)}, f32[40,768]{1,0:T(8,128)}) custom-call(s32[3]{0:T(128)} %get-tuple-element.170.refs_1_.start_ref, s32[3]{0:T(128)} %get-tuple-element.171.refs_2_.small_ref, bf16[640,768]{1,0:T(8,128)(2,1)} %get-tuple-element.73.q_ref.qt_ref, bf16[1280,640]{1,0:T(8,128)(2,1)} %get-tuple-element.74.k_ref, ...), custom_call_target="tpu_custom_call" | custom-call | flops 6000000000 | bytes 1000000 | tf_op jit(solution)/shard_map/attend_forward/pallas_call | solution.py:165
  126.3 5.3 %all-to-all-start.4 = ((bf16[4,160,768]{2,1,0:T(8,128)(2,1)}), bf16[4,160,768]{2,1,0:T(8,128)(2,1)S(1)}, u32[]{:S(2)}, u32[]{:S(2)}) async-start(bf16[4,160,768]{2,1,0:T(8,128)(2,1)} %tie.30), calls=%async_computation.4 | async-start | bytes 1966080 | tf_op jit(solution)/shard_map/all_to_all | solution.py:745
  131.6 12.8 %attend_forward.4 = (bf16[640,768]{1,0:T(8,128)(2,1)}, f32[40,768]{1,0:T(8,128)}) custom-call(s32[3]{0:T(128)} %get-tuple-element.170.refs_1_.start_ref, s32[3]{0:T(128)} %get-tuple-element.171.refs_2_.small_ref, bf16[640,768]{1,0:T(8,128)(2,1)} %get-tuple-element.73.q_ref.qt_ref, ...), custom_call_target="tpu_custom_call", output_to_operand_aliasing={{0}: (7, {}), {1}: (8, {})} | custom-call | flops 12000000000 | bytes 1000000 | tf_op jit(solution)/shard_map/attend_forward/pallas_call | solution.py:165
  148.1 12.8 %attend_forward.5 = (bf16[640,768]{1,0:T(8,128)(2,1)}, f32[40,768]{1,0:T(8,128)}) custom-call(s32[3]{0:T(128)} %get-tuple-element.170.refs_1_.start_ref, s32[3]{0:T(128)} %get-tuple-element.171.refs_2_.small_ref, bf16[640,768]{1,0:T(8,128)(2,1)} %get-tuple-element.73.q_ref.qt_ref, ...), custom_call_target="tpu_custom_call", output_to_operand_aliasing={{0}: (7, {}), {1}: (8, {})} | custom-call | flops 12000000000 | bytes 1000000 | tf_op jit(solution)/shard_map/attend_forward/pallas_call | solution.py:165
  160.9 5.1 %branch.1 = (f32[640,768]{1,0:T(8,128)}, bf16[640,768]{1,0:T(8,128)(2,1)}) custom-call(bf16[640,768]{1,0:T(8,128)(2,1)} %get-tuple-element.80.att_ref.refs_1_, bf16[4,640,640]{2,1,0:T(8,128)(2,1)} %get-tuple-element.81.wo_ref.w_ref, bf16[640,1280]{1,0:T(8,128)(2,1)} %tie.24.x_ref, bf16[640,384]{1,0:T(8,128)(2,1)} %bitcast.66), custom_call_target="tpu_custom_call" | custom-call | flops 5000000000 | bytes 1000000 | tf_op jit(solution)/shard_map/branch/pallas_call | solution.py:434
  172.1 27.7 %feed_forward.2 = (bf16[640,768]{1,0:T(8,128)(2,1)}, bf16[640,768]{1,0:T(8,128)(2,1)}, bf16[640,768]{1,0:T(8,128)(2,1)}, bf16[640,768]{1,0:T(8,128)(2,1)}, bf16[...) custom-call(bf16[640,768]{1,0:T(8,128)(2,1)} %tie.29.refs_0_, ...), custom_call_target="tpu_custom_call" | custom-call | flops 28000000000 | bytes 1000000 | tf_op jit(solution)/shard_map/feed_forward/pallas_call | solution.py:630
  203.9 29.0 %feed_forward.3 = (f32[640,768]{1,0:T(8,128)}, bf16[640,768]{1,0:T(8,128)(2,1)}, f32[640,768]{1,0:T(8,128)}, bf16[640,768]{1,0:T(8,128)(2,1)}, bf16[640,640]{1,0...) custom-call(bf16[640,768]{1,0:T(8,128)(2,1)} %tie.29.refs_0_, ...), custom_call_target="tpu_custom_call" | custom-call | flops 28000000000 | bytes 1000000 | tf_op jit(solution)/shard_map/feed_forward/pallas_call | solution.py:630
  250.6 5.1 %all-to-all-start.5 = ((bf16[4,160,768]{2,1,0:T(8,128)(2,1)}), bf16[4,160,768]{2,1,0:T(8,128)(2,1)S(1)}, u32[]{:S(2)}, u32[]{:S(2)}) async-start(bf16[4,160,768]{2,1,0:T(8,128)(2,1)} %bitcast.19), calls=%async_computation.5 | async-start | bytes 1966080 | tf_op jit(solution)/shard_map/all_to_all | solution.py:745
  255.6 9.1 %branch_back.1 = (f32[640,768]{1,0:T(8,128)}, bf16[640,768]{1,0:T(8,128)(2,1)}, bf16[640,640]{1,0:T(8,128)(2,1)}, f32[8,640]{1,0:T(8,128)}) custom-call(f32[640,768]{1,0:T(8,128)} %get-tuple-element.92.gn_ref, bf16[640,768]{1,0:T(8,128)(2,1)} %tie.33.got_ref, f32[640,768]{1,0:T(8,128)} %get-tuple-element.82.mid_ref, bf16[640,768]{1,0:T(8,128)(2,1)} %tie.31.refs_2_.g_ref, ...), custom_call_target="tpu_custom_call" | custom-call | flops 8999999488 | bytes 1000000 | tf_op jit(solution)/shard_map/branch_back/pallas_call | solution.py:485
  264.7 14.4 %attend_backward.2 = (bf16[640,768]{1,0:T(8,128)(2,1)}, bf16[1280,640]{1,0:T(8,128)(2,1)}, bf16[1280,640]{1,0:T(8,128)(2,1)}) custom-call(s32[3]{0:T(128)} %get-tuple-element.170.refs_1_.start_ref, s32[3]{0:T(128)} %get-tuple-element.171.refs_2_.small_ref, bf16[640,768]{1,0:T(8,128)(2,1)} %get-tuple-element.73.q_ref.qt_ref, ...), custom_call_target="tpu_custom_call" | custom-call | flops 14000000000 | bytes 1000000 | tf_op jit(solution)/shard_map/attend_backward/pallas_call | solution.py:190
  290.3 5.8 %all-to-all-start.6 = ((bf16[4,160,1280]{2,1,0:T(8,128)(2,1)}), bf16[4,160,1280]{2,1,0:T(8,128)(2,1)S(1)}, u32[]{:S(2)}, u32[]{:S(2)}) async-start(bf16[4,160,1280]{2,1,0:T(8,128)(2,1)} %pad_maximum_fusion.2), calls=%async_computation.6 | async-start | bytes 3276800 | tf_op jit(solution)/shard_map/all_to_all | solution.py:745
  297.2 19.9 %attend_backward.3 = (bf16[640,768]{1,0:T(8,128)(2,1)}, bf16[1280,640]{1,0:T(8,128)(2,1)}, bf16[1280,640]{1,0:T(8,128)(2,1)}) custom-call(s32[3]{0:T(128)} %get-tuple-element.170.refs_1_.start_ref, s32[3]{0:T(128)} %get-tuple-element.171.refs_2_.small_ref, ...), custom_call_target="tpu_custom_call", output_to_operand_aliasing={{0}: (11, {}), {1}: (12, {}), {2}: (13, {})} | custom-call | flops 20999999488 | bytes 1000000 | tf_op jit(solution)/shard_map/attend_backward/pallas_call | solution.py:190
  317.1 8.4 %project_weights.1 = (bf16[4,4,80,640]{3,2,1,0:T(8,128)(2,1)}, bf16[4,4,80,640]{3,2,1,0:T(8,128)(2,1)}, f32[8,640]{1,0:T(8,128)}) custom-call(s32[1]{0:T(128)} %bitcast.member_ref, bf16[640,1280]{1,0:T(8,128)(2,1)} %get-tuple-element.119.n_ref, bf16[640,768]{1,0:T(8,128)(2,1)} %tie.37.dqt_ref.refs_0_, bf16[1280,640]{1,0:T(8,128)(2,1)} %get-tuple-element.120.dk_ref, ...), custom_call_target="tpu_custom_call" | custom-call | flops 8000000000 | bytes 1000000 | tf_op jit(solution)/shard_map/project_weights/pallas_call | solution.py:372
  326.2 7.7 %all-to-all-done.6.refs_2_ = bf16[4,160,1280]{2,1,0:T(8,128)(2,1)S(1)} async-done(((bf16[4,160,1280]{2,1,0:T(8,128)(2,1)}), bf16[4,160,1280]{2,1,0:T(8,128)(2,1)S(1)}, u32[]{:S(2)}, u32[]{:S(2)}) %all-to-all-start.6) | async-done | bytes 1638432 | tf_op jit(solution)/shard_map/all_to_all | solution.py:745
  335.2 10.3 %project_back.1 = (bf16[640,1280]{1,0:T(8,128)(2,1)}, f32[8,640]{1,0:T(8,128)}) custom-call(bf16[640,1280]{1,0:T(8,128)(2,1)} %tie.24.x_ref, bf16[640,768]{1,0:T(8,128)(2,1)} %tie.38.dqt_ref, bf16[1280,640]{1,0:T(8,128)(2,1)} %get-tuple-element.120.dk_ref, bf16[1280,640]{1,0:T(8,128)(2,1)} %get-tuple-element.121.dv_ref, ...), custom_call_target="tpu_custom_call" | custom-call | flops 10000000000 | bytes 1000000 | tf_op jit(solution)/shard_map/project_back/pallas_call | solution.py:411
  366.1 4.4 %collective-permute-done.32 = bf16[1,4,80,640]{3,2,1,0:T(8,128)(2,1)} collective-permute-done((bf16[1,4,80,640]{3,2,1,0:T(8,128)(2,1)}, bf16[1,4,80,640]{3,2,1,0:T(8,128)(2,1)}, u32[]{:S(2)}, u32[]{:S(2)}) %collective-permute-start.32) | collective-permute-done | bytes 409632 | tf_op jit(solution)/shard_map/ppermute | solution.py:682
  373.9 13.0 %all-to-all-done.7 = bf16[4,160,1280]{2,1,0:T(8,128)(2,1)S(1)} async-done(((bf16[4,160,1280]{2,1,0:T(8,128)(2,1)}), bf16[4,160,1280]{2,1,0:T(8,128)(2,1)S(1)}, u32[]{:S(2)}, u32[]{:S(2)}) %all-to-all-start.7) | async-done | bytes 1638432 | tf_op jit(solution)/shard_map/all_to_all | solution.py:745
  (290 shorter events, 145.8 us)
Async XLA Ops:
  8.2 20.1 %all-to-all-start = ((bf16[4,160,384]{2,1,0:T(8,128)(2,1)}), bf16[4,160,384]{2,1,0:T(8,128)(2,1)S(1)}, u32[]{:S(2)}, u32[]{:S(2)}) async-start(bf16[4,160,384]{2,1,0:T(8,128)(2,1)} %stack.98), calls=%async_computation | async-start | bytes 983040 | tf_op jit(solution)/shard_map/all_to_all | solution.py:745
  29.4 23.9 %all-to-all-start.1 = ((bf16[4,160,640]{2,1,0:T(8,128)(2,1)}), bf16[4,160,640]{2,1,0:T(8,128)(2,1)S(1)}, u32[]{:S(2)}, u32[]{:S(2)}) async-start(bf16[4,160,640]{2,1,0:T(8,128)(2,1)} %tie.21), calls=%async_computation.1 | async-start | bytes 1638400 | tf_op jit(solution)/shard_map/all_to_all | solution.py:745
  55.2 41.5 %all-to-all-start.2 = ((bf16[4,160,1280]{2,1,0:T(8,128)(2,1)}), bf16[4,160,1280]{2,1,0:T(8,128)(2,1)S(1)}, u32[]{:S(2)}, u32[]{:S(2)}) async-start(bf16[4,160,1280]{2,1,0:T(8,128)(2,1)} %tie.23), calls=%async_computation.2 | async-start | bytes 3276800 | tf_op jit(solution)/shard_map/all_to_all | solution.py:745
  62.0 39.7 %collective-permute-start.6 = (bf16[336,640]{1,0:T(8,128)(2,1)S(1)}, bf16[336,640]{1,0:T(8,128)(2,1)}, u32[]{:S(2)}, u32[]{:S(2)}) collective-permute-start(bf16[336,640]{1,0:T(8,128)(2,1)S(1)} %copy-done.22), channel_id=1, source_target_pairs={{0,4},{4,0},{8,12},{12,8},{16,20},{20,16},{24,28},{28,24},{1,5},{5... | collective-permute-start | bytes 1290248 | tf_op jit(solution)/shard_map/ppermute | solution.py:682
  62.0 42.3 %collective-permute-start.7 = (bf16[336,640]{1,0:T(8,128)(2,1)}, bf16[336,640]{1,0:T(8,128)(2,1)}, u32[]{:S(2)}, u32[]{:S(2)}) collective-permute-start(bf16[336,640]{1,0:T(8,128)(2,1)} %copy-done.39), channel_id=1, source_target_pairs={{0,4},{4,0},{8,12},{12,8},{16,20},{20,16},{24,28},{28,24},{1,5},{5... | collective-permute-start | bytes 1290248 | tf_op jit(solution)/shard_map/ppermute | solution.py:682
  62.5 41.8 %collective-permute-start.8 = (bf16[336,640]{1,0:T(8,128)(2,1)}, bf16[336,640]{1,0:T(8,128)(2,1)}, u32[]{:S(2)}, u32[]{:S(2)}) collective-permute-start(bf16[336,640]{1,0:T(8,128)(2,1)} %copy-done.40), channel_id=1, source_target_pairs={{0,4},{4,0},{8,12},{12,8},{16,20},{20,16},{24,28},{28,24},{1,5},{5... | collective-permute-start | bytes 1290248 | tf_op jit(solution)/shard_map/ppermute | solution.py:682
  78.1 26.1 %collective-permute-start.10 = (bf16[176,640]{1,0:T(8,128)(2,1)S(1)}, bf16[176,640]{1,0:T(8,128)(2,1)}, u32[]{:S(2)}, u32[]{:S(2)}) collective-permute-start(bf16[176,640]{1,0:T(8,128)(2,1)S(1)} %copy-done.35), channel_id=1, source_target_pairs={{0,4},{4,0},{8,12},{12,8},{16,20},{20,16},{24,28},{28,24},{1,5},{5... | collective-permute-start | bytes 675848 | tf_op jit(solution)/shard_map/ppermute | solution.py:682
  80.2 24.0 %collective-permute-start.9 = (bf16[160,640]{1,0:T(8,128)(2,1)}, bf16[160,640]{1,0:T(8,128)(2,1)}, u32[]{:S(2)}, u32[]{:S(2)}) collective-permute-start(bf16[160,640]{1,0:T(8,128)(2,1)} %copy-done.38), channel_id=1, source_target_pairs={{0,4},{4,0},{8,12},{12,8},{16,20},{20,16},{24,28},{28,24},{1,5},{5... | collective-permute-start | bytes 614408 | tf_op jit(solution)/shard_map/ppermute | solution.py:682
  98.1 26.2 %all-to-all-start.3 = ((bf16[4,160,640]{2,1,0:T(8,128)(2,1)}), bf16[4,160,640]{2,1,0:T(8,128)(2,1)S(1)}, u32[]{:S(2)}, u32[]{:S(2)}) async-start(bf16[4,160,640]{2,1,0:T(8,128)(2,1)} %tie.26), calls=%async_computation.3 | async-start | bytes 1638400 | tf_op jit(solution)/shard_map/all_to_all | solution.py:745
  102.8 28.9 %collective-permute-start.11 = (bf16[640,640]{1,0:T(8,128)(2,1)S(1)}, bf16[640,640]{1,0:T(8,128)(2,1)}, u32[]{:S(2)}, u32[]{:S(2)}) collective-permute-start(bf16[640,640]{1,0:T(8,128)(2,1)S(1)} %copy-done.28), channel_id=1, source_target_pairs={{0,8},{4,12},{8,0},{12,4},{16,24},{20,28},{24,16},{28,20},{1,9},{5... | collective-permute-start | bytes 2457608 | tf_op jit(solution)/shard_map/ppermute | solution.py:682
  126.3 39.7 %all-to-all-start.4 = ((bf16[4,160,768]{2,1,0:T(8,128)(2,1)}), bf16[4,160,768]{2,1,0:T(8,128)(2,1)S(1)}, u32[]{:S(2)}, u32[]{:S(2)}) async-start(bf16[4,160,768]{2,1,0:T(8,128)(2,1)} %tie.30), calls=%async_computation.4 | async-start | bytes 1966080 | tf_op jit(solution)/shard_map/all_to_all | solution.py:745
  145.9 21.1 %collective-permute-start.13 = (bf16[640,640]{1,0:T(8,128)(2,1)}, bf16[640,640]{1,0:T(8,128)(2,1)S(1)}, u32[]{:S(2)}, u32[]{:S(2)}) collective-permute-start(bf16[640,640]{1,0:T(8,128)(2,1)} %tie.28.refs_8_), channel_id=1, source_target_pairs={{0,16},{4,20},{8,24},{12,28},{16,0},{20,4},{24,8},{28,12},{1,17},{... | collective-permute-start | bytes 2457608 | tf_op jit(solution)/shard_map/ppermute | solution.py:682
  168.4 34.6 %collective-permute-start.16 = (bf16[640,640]{1,0:T(8,128)(2,1)S(1)}, bf16[640,640]{1,0:T(8,128)(2,1)S(1)}, u32[]{:S(2)}, u32[]{:S(2)}) collective-permute-start(bf16[640,640]{1,0:T(8,128)(2,1)S(1)} %copy-done.7), channel_id=1, source_target_pairs={{0,16},{4,20},{8,24},{12,28},{16,0},{20,4},{24,8},{28,12},{1,17},{... | collective-permute-start | bytes 2457608 | tf_op jit(solution)/shard_map/ppermute | solution.py:682
  199.9 38.7 %collective-permute-start.18 = (bf16[640,640]{1,0:T(8,128)(2,1)}, bf16[640,640]{1,0:T(8,128)(2,1)S(1)}, u32[]{:S(2)}, u32[]{:S(2)}) collective-permute-start(bf16[640,640]{1,0:T(8,128)(2,1)} %get-tuple-element.94), channel_id=1, source_target_pairs={{0,8},{4,12},{8,0},{12,4},{16,24},{20,28},{24,16},{28,20},{1,9},{5... | collective-permute-start | bytes 2457608 | tf_op jit(solution)/shard_map/ppermute | solution.py:682
  202.6 36.0 %collective-permute-start.19 = (bf16[640,640]{1,0:T(8,128)(2,1)}, bf16[640,640]{1,0:T(8,128)(2,1)S(1)}, u32[]{:S(2)}, u32[]{:S(2)}) collective-permute-start(bf16[640,640]{1,0:T(8,128)(2,1)} %get-tuple-element.95), channel_id=1, source_target_pairs={{0,16},{4,20},{8,24},{12,28},{16,0},{20,4},{24,8},{28,12},{1,17},{... | collective-permute-start | bytes 2457608 | tf_op jit(solution)/shard_map/ppermute | solution.py:682
  234.2 47.4 %collective-permute-start.21 = (bf16[640,640]{1,0:T(8,128)(2,1)}, bf16[640,640]{1,0:T(8,128)(2,1)S(1)}, u32[]{:S(2)}, u32[]{:S(2)}) collective-permute-start(bf16[640,640]{1,0:T(8,128)(2,1)} %get-tuple-element.100), channel_id=1, source_target_pairs={{0,8},{4,12},{8,0},{12,4},{16,24},{20,28},{24,16},{28,20},{1,9},{5... | collective-permute-start | bytes 2457608 | tf_op jit(solution)/shard_map/ppermute | solution.py:682
  234.4 47.8 %collective-permute-start.24 = (bf16[640,640]{1,0:T(8,128)(2,1)}, bf16[640,640]{1,0:T(8,128)(2,1)S(1)}, u32[]{:S(2)}, u32[]{:S(2)}) collective-permute-start(bf16[640,640]{1,0:T(8,128)(2,1)} %get-tuple-element.103), channel_id=1, source_target_pairs={{0,16},{4,20},{8,24},{12,28},{16,0},{20,4},{24,8},{28,12},{1,17},{... | collective-permute-start | bytes 2457608 | tf_op jit(solution)/shard_map/ppermute | solution.py:682
  243.4 39.8 %collective-permute-start.22 = (bf16[640,640]{1,0:T(8,128)(2,1)}, bf16[640,640]{1,0:T(8,128)(2,1)S(1)}, u32[]{:S(2)}, u32[]{:S(2)}) collective-permute-start(bf16[640,640]{1,0:T(8,128)(2,1)} %add_convert_fusion.5), channel_id=1, source_target_pairs={{0,16},{4,20},{8,24},{12,28},{16,0},{20,4},{24,8},{28,12},{1,17},{... | collective-permute-start | bytes 2457608 | tf_op jit(solution)/shard_map/ppermute | solution.py:682
  246.2 37.0 %collective-permute-start.23 = (bf16[640,640]{1,0:T(8,128)(2,1)}, bf16[640,640]{1,0:T(8,128)(2,1)}, u32[]{:S(2)}, u32[]{:S(2)}) collective-permute-start(bf16[640,640]{1,0:T(8,128)(2,1)} %add_convert_fusion.4), channel_id=1, source_target_pairs={{0,8},{4,12},{8,0},{12,4},{16,24},{20,28},{24,16},{28,20},{1,9},{5... | collective-permute-start | bytes 2457608 | tf_op jit(solution)/shard_map/ppermute | solution.py:682
  250.6 39.7 %all-to-all-start.5 = ((bf16[4,160,768]{2,1,0:T(8,128)(2,1)}), bf16[4,160,768]{2,1,0:T(8,128)(2,1)S(1)}, u32[]{:S(2)}, u32[]{:S(2)}) async-start(bf16[4,160,768]{2,1,0:T(8,128)(2,1)} %bitcast.19), calls=%async_computation.5 | async-start | bytes 1966080 | tf_op jit(solution)/shard_map/all_to_all | solution.py:745
  290.3 43.6 %all-to-all-start.6 = ((bf16[4,160,1280]{2,1,0:T(8,128)(2,1)}), bf16[4,160,1280]{2,1,0:T(8,128)(2,1)S(1)}, u32[]{:S(2)}, u32[]{:S(2)}) async-start(bf16[4,160,1280]{2,1,0:T(8,128)(2,1)} %pad_maximum_fusion.2), calls=%async_computation.6 | async-start | bytes 3276800 | tf_op jit(solution)/shard_map/all_to_all | solution.py:745
  325.5 23.6 %collective-permute-start.28 = (bf16[4,4,80,640]{3,2,1,0:T(8,128)(2,1)}, bf16[4,4,80,640]{3,2,1,0:T(8,128)(2,1)}, u32[]{:S(2)}, u32[]{:S(2)}) collective-permute-start(bf16[4,4,80,640]{3,2,1,0:T(8,128)(2,1)} %get-tuple-element.123.refs_1_), channel_id=1, source_target_pairs={{0,4},{4,0},{8,12},{12,8},{16,20},{20,16},{24,28},{28,24},{1,5},{5... | collective-permute-start | bytes 4915208 | tf_op jit(solution)/shard_map/ppermute | solution.py:682
  345.5 41.4 %all-to-all-start.7 = ((bf16[4,160,1280]{2,1,0:T(8,128)(2,1)}), bf16[4,160,1280]{2,1,0:T(8,128)(2,1)S(1)}, u32[]{:S(2)}, u32[]{:S(2)}) async-start(bf16[4,160,1280]{2,1,0:T(8,128)(2,1)} %bitcast.75), calls=%async_computation.7 | async-start | bytes 3276800 | tf_op jit(solution)/shard_map/all_to_all | solution.py:745
  394.5 23.4 %all-to-all-start.8 = ((bf16[4,160,320]{2,1,0:T(8,128)(2,1)}), bf16[4,160,320]{2,1,0:T(8,128)(2,1)S(1)}, u32[]{:S(2)}, u32[]{:S(2)}) async-start(bf16[4,160,320]{2,1,0:T(8,128)(2,1)} %tie.40.refs_1_), calls=%async_computation.8 | async-start | bytes 983040 | tf_op jit(solution)/shard_map/all_to_all | solution.py:745
  (74 other events, 458.9 us)
where the time goes:
time: 429 us; the launch traced here: 421 us
  Pallas kernels  170 us (40%)
  waiting for transfers between devices  93.1 us (22%)
  starting transfers between devices  79.5 us (19%)
  local copies, waits for them, and re-layouts  42.7 us (10%)
  other arithmetic  32.1 us (7%)
    pallas_call x2, Pallas kernels, run_feed_forward(): pl.pallas_call(functools.partial(feed_forward, first, places), in_specs=[...  56.8 us
    all_to_all x9, waiting for transfers between devices, shards(): across = lambda x: lax.all_to_all(x, 'narrow', 0, 0, tiled=True)  47.9 us
    all_to_all x9, starting transfers between devices, shards(): across = lambda x: lax.all_to_all(x, 'narrow', 0, 0, tiled=True)  41.8 us
    ppermute x36, waiting for transfers between devices, swap(): return lax.ppermute(x, 'wide', [(i, i ^ mask) for i in range(n)])  39.6 us
    pallas_call x2, Pallas kernels, run_backward(): pl.pallas_call(attend_backward, grid_spec=pltpu.PrefetchScalarGridSpec(nu...  34.3 us
    pallas_call x3, Pallas kernels, run_forward(): pl.pallas_call(attend_forward, grid_spec=pltpu.PrefetchScalarGridSpec(num...  33.3 us
    ppermute x36, starting transfers between devices, swap(): return lax.ppermute(x, 'wide', [(i, i ^ mask) for i in range(n)])  32.7 us
    unnamed x102, local copies, waits for them, and re-layouts  14.2 us
  transfers between devices with their start and end apart: 48, of which 18 were waited for; matrix products, arithmetic and copies ran while one was open for 11% of the time, Pallas kernels for 40%

commit v1 on v0

--- a/solution.py
+++ b/solution.py
@@ -75,15 +75,19 @@
         keys = k_ref[pl.ds(start, window), :]
         bias = key_bias(segk_ref, segq_ref, start, window)
         q = q_ref[...]
+        rows = [slice(h * HEAD_DIM, (h + 1) * HEAD_DIM) for h in range(GROUP)]
+        scores = [mm(keys, head_only(q, h, 0)) for h in range(GROUP)]
+        ready = []
         for h in range(GROUP):
-            rows = slice(h * HEAD_DIM, (h + 1) * HEAD_DIM)
-            scores = mm(keys, head_only(q, h, 0)) + bias
-            top = jnp.max(scores, axis=0, keepdims=True)
-            probs = jnp.exp2((scores - top) * (SCALE * LOG2E))
+            masked = scores[h] + bias
+            top = jnp.max(masked, axis=0, keepdims=True)
+            probs = jnp.exp2((masked - top) * (SCALE * LOG2E))
             total = jnp.sum(probs, axis=0, keepdims=True)
-            out = mm(vt_ref[rows, pl.ds(start, window)], probs.astype(bf16))
-            att_ref[rows, :] = (out / total).astype(bf16)
             lse_ref[h : h + 1, :] = top * (SCALE * LOG2E) + jnp.log2(total)
+            ready.append((probs.astype(bf16), total))
+        for h, (probs, total) in enumerate(ready):
+            out = mm(vt_ref[rows[h], pl.ds(start, window)], probs)
+            att_ref[rows[h], :] = (out / total).astype(bf16)
 
     @pl.when(small_ref[tile] == 1)
     def _():
@@ -113,19 +117,20 @@
         qt, dot = qt_ref[...], dot_ref[...]
         q, do = qt.T, dot.T
         inner = dot.astype(f32) * att_ref[...].astype(f32)
-        dk = jnp.zeros((window, LANES), f32)
-        dv = jnp.zeros((window, LANES), f32)
+        rows = [slice(h * HEAD_DIM, (h + 1) * HEAD_DIM) for h in range(GROUP)]
+        products = [(mm(keys, head_only(qt, h, 0)), mm(values, head_only(dot, h, 0))) for h in range(GROUP)]
+        probs_low, grads_low = [], []
+        for h, (scores, grad_probs) in enumerate(products):
+            delta = jnp.sum(inner[rows[h], :], axis=0, keepdims=True)
+            probs = jnp.exp2((scores * (SCALE * LOG2E) - lse_ref[h : h + 1, :]) + bias)
+            probs_low.append(probs.astype(bf16))
+            grads_low.append((probs * (grad_probs - delta)).astype(bf16))
+        heads_of = lambda block: jnp.concatenate([head_only(block, h, 1) for h in range(GROUP)], axis=0)
+        dv = mm(jnp.concatenate(probs_low, axis=1), heads_of(do))
+        dk = mm(jnp.concatenate(grads_low, axis=1), heads_of(q))
         for h in range(GROUP):
-            rows = slice(h * HEAD_DIM, (h + 1) * HEAD_DIM)
-            delta = jnp.sum(inner[rows, :], axis=0, keepdims=True)
-            scores = mm(keys, head_only(qt, h, 0)) * (SCALE * LOG2E)
-            probs = jnp.exp2((scores - lse_ref[h : h + 1, :]) + bias)
-            dv = dv + mm(probs.astype(bf16), head_only(do, h, 1))
-            grad_probs = mm(values, head_only(dot, h, 0))
-            grad_scores = (probs * (grad_probs - delta)).astype(bf16)
-            dk = dk + mm(grad_scores, head_only(q, h, 1))
-            dq = mm(kt_ref[rows, at], grad_scores)
-            dqt_ref[rows, :] = (dq * SCALE).astype(bf16)
+            dq = mm(kt_ref[rows[h], at], grads_low[h])
+            dqt_ref[rows[h], :] = (dq * SCALE).astype(bf16)
         dk_sum[at, :] += dk
         dv_sum[at, :] += dv
 
@@ -177,7 +182,7 @@
             jax.ShapeDtypeStruct((groups * 8, rows), f32),
         ],
         name="attend_forward",
-        **kernel_params(6 * (end - begin)),
+        **kernel_params(4 * (end - begin)),
     )(starts, small, qt, k, vt, segk, segq, *outs)
 
 
@@ -207,7 +212,7 @@
         ],
         input_output_aliases={11: 0, 12: 1, 13: 2} if outs else {},
         name="attend_backward",
-        **kernel_params(7 * (end - begin)),
+        **kernel_params(6 * (end - begin)),
     )(starts, small, qt, kt, k, v, dot, att, lse, segk, segq, *outs)
 
 
@@ -503,7 +508,7 @@
     )(gn, got, middle, g, att, w, vec)
 
 
-def feed_forward(first, places, *refs):
+def feed_forward(first, final, places, *refs):
     blocks, weights = len(places), 1 + max(p[0] for place in places for p in place)
     n2_in, g_in, refs = refs[0:2], refs[2:4], refs[4:]
     weights, refs = refs[:weights], refs[weights:]
@@ -598,7 +603,7 @@
             k = 2 * i + half
             if not first:
                 total = total + low[k].astype(f32)
-            if half == 1 or first:
+            if half == 1 or not final:
                 low[k] = total.astype(bf16)
                 send(low.at[k], sums_out[k])
             else:
@@ -608,7 +613,7 @@
         copy.wait()
 
 
-def run_feed_forward(n2, g, blocks, sums):
+def run_feed_forward(n2, g, blocks, sums, final=False):
     D, rows = n2[0].shape
     F = D
     first = sums is None
@@ -626,9 +631,9 @@
     shape = jax.ShapeDtypeStruct
     anywhere = pl.BlockSpec(memory_space=pl.ANY)
     vmem = pl.BlockSpec(memory_space=pltpu.VMEM)
-    own_type = bf16 if first else f32
+    own_type = f32 if final else bf16
     outs = pl.pallas_call(
-        functools.partial(feed_forward, first, places),
+        functools.partial(feed_forward, first, final, places),
         in_specs=[anywhere] * (4 + len(weights) + len(sums)),
         out_specs=[anywhere] * (4 + 2 * count) + [vmem] * count,
         out_shape=[shape((D, rows), t) for t in (own_type, bf16, own_type, bf16)]
@@ -651,7 +656,7 @@
             pltpu.SemaphoreType.DMA((2 * count + 4,)),
         ],
         name="feed_forward",
-        **kernel_params(28),
+        **kernel_params(14 * count),
     )(*n2, *g, *weights, *sums)
     grads = [(*outs[4 + 2 * b : 6 + 2 * b], outs[4 + 2 * count + b]) for b in range(count)]
     return outs[:4], grads
@@ -846,45 +851,38 @@
     blocks = [((up_xy, 0), (dt_xy, 0), ub_xy), ((up_x, 0), (dt_x, 0), ub_x)]
     sums, ((up_gxy, dt_gxy, ub_gxy), (up_gx, dt_gx, ub_gx)) = run_feed_forward(n2_pair, grad_pair, blocks, None)
     up_got_xy, dt_got_xy = swap(up_gxy, X), swap(dt_gxy, Y)
-    blocks = [((up_y, 0), (dt_y, 0), ub_y), ((up_own, 0), (dt_own, 0), ub_own)]
-    sums, ((up_gy, dt_gy, ub_gy), (up_g, dt_g, ub_g)) = run_feed_forward(n2_pair, grad_pair, blocks, sums)
+    up_got_x = swap(up_gx, X)
+    blocks = [((up_y, 0), (dt_y, 0), ub_y)]
+    sums, ((up_gy, dt_gy, ub_gy),) = run_feed_forward(n2_pair, grad_pair, blocks, sums)
+    add = lambda *terms: sum(t.astype(f32) for t in terms)
+    dt_got_y = swap(dt_gy, Y)
+    up_gy, dt_gx = add(up_gy, up_got_xy).astype(bf16), add(dt_gx, dt_got_xy).astype(bf16)
+    up_got_y, dt_got_x = swap(up_gy, Y), swap(dt_gx, X)
+    sums = after((up_gy, dt_gx), *sums)
+    blocks = [((up_own, 0), (dt_own, 0), ub_own)]
+    sums, ((up_g, dt_g, ub_g),) = run_feed_forward(n2_pair, grad_pair, blocks, sums, True)
     gn_sum, gn_other, out_sum, out_other = sums
-    ub_g, ub_gx, ub_gy, ub_gxy = (rows[0] for rows in (ub_g, ub_gx, ub_gy, ub_gxy))
-    gn_other = after((up_got_xy, dt_got_xy), gn_other)
     gn_got, out_got = swap(gn_other, CORE), swap(out_other, CORE)
 
     layer = (middle + (out_sum + out_got.astype(f32) + vec[:, VEC_LAST : VEC_LAST + 1].astype(f32))).astype(bf16)
     layer_out = across(layer.reshape(nn, part, quarter)).transpose(1, 0, 2).reshape(part, tok)
-
-    add = lambda *terms: sum(t.astype(f32) for t in terms)
-    up_gy = add(up_gy, up_got_xy).astype(bf16)
-    up_got = swap(up_gx, X), swap(up_gy, Y)
 
     gn_got = after((layer,), gn_got)
     grad_mid, grad_att, grad_wo_t, sums_two = run_branch_back(
         gn_sum, gn_got, middle, grad_cols, att, w_attn, vec
     )
     back_in = starts, small, qt, kt, k, v, grad_att, att, lse, segk, segq
-    dt_gx = add(dt_gx, dt_got_xy).astype(bf16)
-    dt_got = swap(dt_gx, X), swap(dt_gy, Y)
     back_a = run_backward(*back_in, (0, 2))
-    up_got_x, up_got_y, dt_got_x, dt_got_y = after((back_a[0],), *up_got, *dt_got)
+    up_got_x, up_got_y, dt_got_x, dt_got_y = after((back_a[0],), up_got_x, up_got_y, dt_got_x, dt_got_y)
     up_g, dt_g = add(up_g, up_got_x, up_got_y), add(dt_g, dt_got_x, dt_got_y)
     for bit in reversed(high):
         half = up_g.shape[1] // 2
         up_g = up_g[:, :half] + swap(up_g[:, half:].astype(bf16), bit).astype(f32)
         dt_g = dt_g[:, :half] + swap(dt_g[:, half:].astype(bf16), bit).astype(f32)
     ud_g = jnp.concatenate([up_g, dt_g], axis=1).astype(bf16)
-    ud_grad = across(ud_g.reshape(nn, part, -1))
+    ud_grad = z_scatter_sum(ud_g.reshape(nn, part, -1))
     dqt_a = after((ud_g, layer_out), back_a[0])
     dqt, dk, dv = run_backward(*back_in, (2, groups), (dqt_a, *back_a[1:]))
-    ub_gx, ub_gy, ub_gxy = after((back_a[1],), ub_gx, ub_gy, ub_gxy)
-    ub_g = ub_g + swap(ub_gx, X) + swap(ub_gy, Y) + swap(ub_gxy, X | Y)
-    for bit in reversed(high):
-        cut = ub_g.shape[0] // 2
-        ub_g = ub_g[:cut] + swap(ub_g[cut:], bit)
-    ub_g = jnp.pad(ub_g[None], ((0, 0), (0, D - units)))
-    dqt = after((ub_g,), dqt)
     masks = [0]
     for bit in high:
         masks = masks + [m ^ bit for m in masks]
@@ -898,11 +896,10 @@
         )
         grad_w = pick(masks), pick([m ^ CORE for m in masks])
     attn_g, got = grad_w[0], swap(grad_w[1], CORE)
-    dqt = after((grad_w[1], ud_grad), dqt)
+    dqt = after((grad_w[1],), dqt)
     grad_in, sums_one = run_project_back(x_low, dqt, dk, dv, w_attn, grad_mid, vec)
     got = after((grad_in,), got)
     vector_rows = jnp.concatenate([sums_one[:2], qv_rows[:2], sums_two[:4]])
-    ud_grad = jnp.sum(ud_grad.reshape(nn, part, -1).astype(f32), axis=0)
     up_grad, down_grad = ud_grad[:, :units], ud_grad[:, units:].T
     grad_in = across(grad_in.reshape(nn, part, span)).astype(f32)
     tokens_grad = sum(
@@ -915,14 +912,19 @@
     gx_high = add(gx[:, 2:], swap(gxy[:, 2:], Y)).astype(bf16)
     gx = jnp.concatenate([gx[:, :2], gx_high], axis=1)
     gy = jnp.concatenate([gy_low, gy[:, 2:]], axis=1)
+    ub_g, ub_gx, ub_gy, ub_gxy = (rows[0] for rows in after((gx, gy), ub_g, ub_gx, ub_gy, ub_gxy))
+    ub_g = ub_g + swap(ub_gx, X) + swap(ub_gy, Y) + swap(ub_gxy, X | Y)
+    for bit in reversed(high):
+        cut = ub_g.shape[0] // 2
+        ub_g = ub_g[:cut] + swap(ub_g[cut:], bit)
+    ub_g = jnp.pad(ub_g[None], ((0, 0), (0, D - units)))
+    vector_rows = after((gx, gy), vector_rows)
     g0 = add(g0, swap(gx, X), swap(gy, Y))
     for bit in reversed(high):
         cut = g0.shape[0] // 2
         g0 = g0[:cut] + swap(g0[cut:].astype(bf16), bit).astype(f32)
     g0 = g0[0].astype(bf16).reshape(4 * dw, D).T.reshape(nn, part, 4 * dw)
-    g0 = after((grad_in,), g0)
-    vector_rows = after((g0,), vector_rows)
-    attn_grad = jnp.sum(across(g0).reshape(nn, part, 4 * dw).astype(f32), axis=0)
+    attn_grad = z_scatter_sum(g0)
     qkv_grad = attn_grad[:, : 3 * dw].T.reshape(3, dw, part)
     out_weight_grad = attn_grad[:, 3 * dw :]
 
@@ -937,7 +939,7 @@
     counts = jnp.pad(counts.reshape(1, -1), ((0, 0), (0, D - counts.size)))
     sums = wide_sum(jnp.concatenate([vector_rows, counts]))
     counts = sums[8, : 2 * CLASSES].reshape(2, CLASSES)
-    sums = jnp.concatenate([sums[:8], ub_g])
+    sums = after((g0,), jnp.concatenate([sums[:8], ub_g]))
     sums = sums + sum(z_rotate(sums, r) for r in range(1, nn))
     ub_g = sums[8, :units]
     sums = lax.dynamic_slice_in_dim(sums[:8], me * part, part, 1)

time: 429 us -> 412 us (0.960); the launches traced: 421 us -> 409 us
  waiting for transfers between devices: 93.1 us -> 72.1 us
  starting transfers between devices: 79.5 us -> 92.5 us
  Pallas kernels: 170 us -> 165 us
    all_to_all x9 -> x7, waiting for transfers between devices: 47.9 us -> 26.9 us  [shards(): across = lambda x: lax.all_to_all(x, 'narrow', 0, 0, tiled=True)]
    ppermute x3 -> x9, starting transfers between devices: 4.95 us -> 15.8 us  [z_rotate(): return lax.ppermute(x, 'narrow', [(i, (i + k) % n) for i in range(n)])]
    pallas_call x3, Pallas kernels: 33.3 us -> 25 us  [run_forward(): pl.pallas_call(attend_forward, grid_spec=pltpu.PrefetchScalarGridSpec(num...]
    pallas_call x2 -> x3, Pallas kernels: 56.8 us -> 62.2 us  [run_feed_forward(): pl.pallas_call(functools.partial(feed_forward, first, final, places), in_...]
    all_to_all x9 -> x7, starting transfers between devices: 41.8 us -> 45.2 us  [shards(): across = lambda x: lax.all_to_all(x, 'narrow', 0, 0, tiled=True)]
    unnamed x102 -> x80, local copies, waits for them, and re-layouts: 14.2 us -> 13.9 us
  transfers between devices with their start and end apart: 48 -> 52, of which waited for: 18 -> 15; matrix products, arithmetic and copies ran while one was open for 11% -> 11% of each run, Pallas kernels for 40% -> 36%
where the time goes in v1:
time: 412 us; the launch traced here: 409 us
  Pallas kernels  165 us (40%)
  starting transfers between devices  92.5 us (22%)
  waiting for transfers between devices  72.1 us (17%)
  local copies, waits for them, and re-layouts  41.2 us (10%)
  other arithmetic  34.4 us (8%)
    pallas_call x3, Pallas kernels, run_feed_forward(): pl.pallas_call(functools.partial(feed_forward, first, final, places), in_...  62.2 us
    all_to_all x7, starting transfers between devices, shards(): across = lambda x: lax.all_to_all(x, 'narrow', 0, 0, tiled=True)  45.2 us
    ppermute x36, waiting for transfers between devices, swap(): return lax.ppermute(x, 'wide', [(i, i ^ mask) for i in range(n)])  40.2 us
    pallas_call x2, Pallas kernels, run_backward(): pl.pallas_call(attend_backward, grid_spec=pltpu.PrefetchScalarGridSpec(nu...  32.6 us
    ppermute x36, starting transfers between devices, swap(): return lax.ppermute(x, 'wide', [(i, i ^ mask) for i in range(n)])  31.4 us
    all_to_all x7, waiting for transfers between devices, shards(): across = lambda x: lax.all_to_all(x, 'narrow', 0, 0, tiled=True)  26.9 us
    pallas_call x3, Pallas kernels, run_forward(): pl.pallas_call(attend_forward, grid_spec=pltpu.PrefetchScalarGridSpec(num...  25 us
    ppermute x9, starting transfers between devices, z_rotate(): return lax.ppermute(x, 'narrow', [(i, (i + k) % n) for i in range(n)])  15.8 us
  transfers between devices with their start and end apart: 52, of which 15 were waited for; matrix products, arithmetic and copies ran while one was open for 11% of the time, Pallas kernels for 36%

profile of v1, /device:TPU:0, one launch (start us, length us, event | category | flops | bytes accessed | tf_op | source)
XLA Modules:
  0.0 408.7 jit_solution(5891199210244503413)
XLA Ops:
  8.2 6.3 %all-to-all-start = ((bf16[4,160,384]{2,1,0:T(8,128)(2,1)}), bf16[4,160,384]{2,1,0:T(8,128)(2,1)S(1)}, u32[]{:S(2)}, u32[]{:S(2)}) async-start(bf16[4,160,384]{2,1,0:T(8,128)(2,1)} %stack.98), calls=%async_computation | async-start | bytes 983040 | tf_op jit(solution)/shard_map/all_to_all | solution.py:750
  17.8 10.5 %all-to-all-done = bf16[4,160,384]{2,1,0:T(8,128)(2,1)S(1)} async-done(((bf16[4,160,384]{2,1,0:T(8,128)(2,1)}), bf16[4,160,384]{2,1,0:T(8,128)(2,1)S(1)}, u32[]{:S(2)}, u32[]{:S(2)}) %all-to-all-start) | async-done | bytes 491552 | tf_op jit(solution)/shard_map/all_to_all | solution.py:750
  29.4 3.6 all-to-all-start.1
  40.0 6.3 %collective-permute-done.2.refs_1_.refs_9_ = bf16[336,640]{1,0:T(8,128)(2,1)S(1)} collective-permute-done((bf16[336,640]{1,0:T(8,128)(2,1)}, bf16[336,640]{1,0:T(8,128)(2,1)S(1)}, u32[]{:S(2)}, u32[]{:S(2)}) %collective-permute-start.2) | collective-permute-done | bytes 430112 | tf_op jit(solution)/shard_map/ppermute | solution.py:687
  50.3 3.9 collective-permute-done.1.refs_6_.refs_3_
  55.9 5.2 %all-to-all-start.2 = ((bf16[4,160,1280]{2,1,0:T(8,128)(2,1)}), bf16[4,160,1280]{2,1,0:T(8,128)(2,1)S(1)}, u32[]{:S(2)}, u32[]{:S(2)}) async-start(bf16[4,160,1280]{2,1,0:T(8,128)(2,1)} %tie.22), calls=%async_computation.2 | async-start | bytes 3276800 | tf_op jit(solution)/shard_map/all_to_all | solution.py:750
  63.4 14.7 %collective-permute-done.5.refs_2_.refs_4_ = bf16[640,640]{1,0:T(8,128)(2,1)S(1)} collective-permute-done((bf16[640,640]{1,0:T(8,128)(2,1)S(1)}, bf16[640,640]{1,0:T(8,128)(2,1)S(1)}, u32[]{:S(2)}, u32[]{:S(2)}) %collective-permute-start.5) | collective-permute-done | bytes 819232 | tf_op jit(solution)/shard_map/ppermute | solution.py:687
  80.2 16.4 %all-to-all-done.2 = bf16[4,160,1280]{2,1,0:T(8,128)(2,1)S(1)} async-done(((bf16[4,160,1280]{2,1,0:T(8,128)(2,1)}), bf16[4,160,1280]{2,1,0:T(8,128)(2,1)S(1)}, u32[]{:S(2)}, u32[]{:S(2)}) %all-to-all-start.2) | async-done | bytes 1638432 | tf_op jit(solution)/shard_map/all_to_all | solution.py:750
  104.2 12.4 %project.1 = (bf16[640,1280]{1,0:T(8,128)(2,1)}, bf16[640,768]{1,0:T(8,128)(2,1)}, bf16[640,1280]{1,0:T(8,128)(2,1)}, bf16[640,1280]{1,0:T(8,128)(2,1)}, bf16[12...) custom-call(s32[1]{0:T(128)} %bitcast.member_ref, bf16[640,1280]{1,0:T(8,128)(2,1)} %tie.23.x_ref, ...), custom_call_target="tpu_custom_call" | custom-call | flops 11000000512 | bytes 1000000 | tf_op jit(solution)/shard_map/project/pallas_call | solution.py:309
  116.6 5.9 %attend_forward.3 = (bf16[640,768]{1,0:T(8,128)(2,1)}, f32[40,768]{1,0:T(8,128)}) custom-call(s32[3]{0:T(128)} %get-tuple-element.172.refs_1_.start_ref, s32[3]{0:T(128)} %get-tuple-element.173.refs_2_.small_ref, bf16[640,768]{1,0:T(8,128)(2,1)} %get-tuple-element.82.q_ref.qt_ref, bf16[1280,640]{1,0:T(8,128)(2,1)} %get-tuple-element.83.k_ref, ...), custom_call_target="tpu_custom_call" | custom-call | flops 4000000000 | bytes 1000000 | tf_op jit(solution)/shard_map/attend_forward/pallas_call | solution.py:170
  124.3 16.3 %all-to-all-start.4 = ((bf16[4,160,768]{2,1,0:T(8,128)(2,1)}), bf16[4,160,768]{2,1,0:T(8,128)(2,1)S(1)}, u32[]{:S(2)}, u32[]{:S(2)}) async-start(bf16[4,160,768]{2,1,0:T(8,128)(2,1)} %tie.29), calls=%async_computation.4 | async-start | bytes 1966080 | tf_op jit(solution)/shard_map/all_to_all | solution.py:750
  141.5 9.5 %attend_forward.4 = (bf16[640,768]{1,0:T(8,128)(2,1)}, f32[40,768]{1,0:T(8,128)}) custom-call(s32[3]{0:T(128)} %get-tuple-element.172.refs_1_.start_ref, s32[3]{0:T(128)} %get-tuple-element.173.refs_2_.small_ref, bf16[640,768]{1,0:T(8,128)(2,1)} %get-tuple-element.82.q_ref.qt_ref, ...), custom_call_target="tpu_custom_call", output_to_operand_aliasing={{0}: (7, {}), {1}: (8, {})} | custom-call | flops 8000000000 | bytes 1000000 | tf_op jit(solution)/shard_map/attend_forward/pallas_call | solution.py:170
  154.1 9.5 %attend_forward.5 = (bf16[640,768]{1,0:T(8,128)(2,1)}, f32[40,768]{1,0:T(8,128)}) custom-call(s32[3]{0:T(128)} %get-tuple-element.172.refs_1_.start_ref, s32[3]{0:T(128)} %get-tuple-element.173.refs_2_.small_ref, bf16[640,768]{1,0:T(8,128)(2,1)} %get-tuple-element.82.q_ref.qt_ref, ...), custom_call_target="tpu_custom_call", output_to_operand_aliasing={{0}: (7, {}), {1}: (8, {})} | custom-call | flops 8000000000 | bytes 1000000 | tf_op jit(solution)/shard_map/attend_forward/pallas_call | solution.py:170
  163.6 4.7 %branch.1 = (f32[640,768]{1,0:T(8,128)}, bf16[640,768]{1,0:T(8,128)(2,1)}) custom-call(bf16[640,768]{1,0:T(8,128)(2,1)} %get-tuple-element.89.att_ref.refs_1_, bf16[4,640,640]{2,1,0:T(8,128)(2,1)} %get-tuple-element.90.wo_ref.w_ref, bf16[640,1280]{1,0:T(8,128)(2,1)} %tie.23.x_ref, bf16[640,384]{1,0:T(8,128)(2,1)} %bitcast.90), custom_call_target="tpu_custom_call" | custom-call | flops 5000000000 | bytes 1000000 | tf_op jit(solution)/shard_map/branch/pallas_call | solution.py:439
  174.9 27.9 %feed_forward.3 = (bf16[640,768]{1,0:T(8,128)(2,1)}, bf16[640,768]{1,0:T(8,128)(2,1)}, bf16[640,768]{1,0:T(8,128)(2,1)}, bf16[640,768]{1,0:T(8,128)(2,1)}, bf16[...) custom-call(bf16[640,768]{1,0:T(8,128)(2,1)} %tie.28.refs_0_, ...), custom_call_target="tpu_custom_call" | custom-call | flops 28000000000 | bytes 1000000 | tf_op jit(solution)/shard_map/feed_forward/pallas_call | solution.py:635
  206.2 16.9 %feed_forward.4 = (bf16[640,768]{1,0:T(8,128)(2,1)}, bf16[640,768]{1,0:T(8,128)(2,1)}, bf16[640,768]{1,0:T(8,128)(2,1)}, bf16[640,768]{1,0:T(8,128)(2,1)}, bf16[...) custom-call(bf16[640,768]{1,0:T(8,128)(2,1)} %tie.28.refs_0_, bf16[640,768]{1,0:T(8,128)(2,1)} %copy-done.37, ...), custom_call_target="tpu_custom_call" | custom-call | flops 14000000000 | bytes 1000000 | tf_op jit(solution)/shard_map/feed_forward/pallas_call | solution.py:635
  225.6 17.4 %feed_forward.5 = (f32[640,768]{1,0:T(8,128)}, bf16[640,768]{1,0:T(8,128)(2,1)}, f32[640,768]{1,0:T(8,128)}, bf16[640,768]{1,0:T(8,128)(2,1)}, bf16[640,640]{1,0...) custom-call(bf16[640,768]{1,0:T(8,128)(2,1)} %tie.28.refs_0_, bf16[640,768]{1,0:T(8,128)(2,1)} %copy-done.37, ...), custom_call_target="tpu_custom_call" | custom-call | flops 14000000000 | bytes 1000000 | tf_op jit(solution)/shard_map/feed_forward/pallas_call | solution.py:635
  252.2 5.2 %all-to-all-start.5 = ((bf16[4,160,768]{2,1,0:T(8,128)(2,1)}), bf16[4,160,768]{2,1,0:T(8,128)(2,1)S(1)}, u32[]{:S(2)}, u32[]{:S(2)}) async-start(bf16[4,160,768]{2,1,0:T(8,128)(2,1)} %bitcast.19), calls=%async_computation.5 | async-start | bytes 1966080 | tf_op jit(solution)/shard_map/all_to_all | solution.py:750
  257.4 9.0 %branch_back.1 = (f32[640,768]{1,0:T(8,128)}, bf16[640,768]{1,0:T(8,128)(2,1)}, bf16[640,640]{1,0:T(8,128)(2,1)}, f32[8,640]{1,0:T(8,128)}) custom-call(f32[640,768]{1,0:T(8,128)} %get-tuple-element.113.gn_ref, bf16[640,768]{1,0:T(8,128)(2,1)} %tie.32.got_ref, f32[640,768]{1,0:T(8,128)} %get-tuple-element.91.mid_ref, bf16[640,768]{1,0:T(8,128)(2,1)} %tie.30.refs_2_.g_ref, ...), custom_call_target="tpu_custom_call" | custom-call | flops 8999999488 | bytes 1000000 | tf_op jit(solution)/shard_map/branch_back/pallas_call | solution.py:490
  266.4 13.6 %attend_backward.2 = (bf16[640,768]{1,0:T(8,128)(2,1)}, bf16[1280,640]{1,0:T(8,128)(2,1)}, bf16[1280,640]{1,0:T(8,128)(2,1)}) custom-call(s32[3]{0:T(128)} %get-tuple-element.172.refs_1_.start_ref, s32[3]{0:T(128)} %get-tuple-element.173.refs_2_.small_ref, bf16[640,768]{1,0:T(8,128)(2,1)} %get-tuple-element.82.q_ref.qt_ref, ...), custom_call_target="tpu_custom_call" | custom-call | flops 12000000000 | bytes 1000000 | tf_op jit(solution)/shard_map/attend_backward/pallas_call | solution.py:195
  296.8 19.0 %attend_backward.3 = (bf16[640,768]{1,0:T(8,128)(2,1)}, bf16[1280,640]{1,0:T(8,128)(2,1)}, bf16[1280,640]{1,0:T(8,128)(2,1)}) custom-call(s32[3]{0:T(128)} %get-tuple-element.172.refs_1_.start_ref, s32[3]{0:T(128)} %get-tuple-element.173.refs_2_.small_ref, ...), custom_call_target="tpu_custom_call", output_to_operand_aliasing={{0}: (11, {}), {1}: (12, {}), {2}: (13, {})} | custom-call | flops 17999998976 | bytes 1000000 | tf_op jit(solution)/shard_map/attend_backward/pallas_call | solution.py:195
  315.8 8.4 %project_weights.1 = (bf16[4,4,80,640]{3,2,1,0:T(8,128)(2,1)}, bf16[4,4,80,640]{3,2,1,0:T(8,128)(2,1)}, f32[8,640]{1,0:T(8,128)}) custom-call(s32[1]{0:T(128)} %bitcast.member_ref, bf16[640,1280]{1,0:T(8,128)(2,1)} %get-tuple-element.129.n_ref, bf16[640,768]{1,0:T(8,128)(2,1)} %get-tuple-element.128.dqt_ref.refs_0_, ...), custom_call_target="tpu_custom_call" | custom-call | flops 8000000000 | bytes 1000000 | tf_op jit(solution)/shard_map/project_weights/pallas_call | solution.py:377
  327.0 10.3 %project_back.1 = (bf16[640,1280]{1,0:T(8,128)(2,1)}, f32[8,640]{1,0:T(8,128)}) custom-call(bf16[640,1280]{1,0:T(8,128)(2,1)} %tie.23.x_ref, bf16[640,768]{1,0:T(8,128)(2,1)} %tie.35.dqt_ref, bf16[1280,640]{1,0:T(8,128)(2,1)} %get-tuple-element.130.dk_ref, bf16[1280,640]{1,0:T(8,128)(2,1)} %get-tuple-element.131.dv_ref, ...), custom_call_target="tpu_custom_call" | custom-call | flops 10000000000 | bytes 1000000 | tf_op jit(solution)/shard_map/project_back/pallas_call | solution.py:416
  347.6 5.1 %all-to-all-start.6 = ((bf16[4,160,1280]{2,1,0:T(8,128)(2,1)}), bf16[4,160,1280]{2,1,0:T(8,128)(2,1)S(1)}, u32[]{:S(2)}, u32[]{:S(2)}) async-start(bf16[4,160,1280]{2,1,0:T(8,128)(2,1)} %bitcast.21), calls=%async_computation.6 | async-start | bytes 3276800 | tf_op jit(solution)/shard_map/all_to_all | solution.py:750
  (278 shorter events, 146.7 us)
Async XLA Ops:
  29.4 24.8 %all-to-all-start.1 = ((bf16[4,160,640]{2,1,0:T(8,128)(2,1)}), bf16[4,160,640]{2,1,0:T(8,128)(2,1)S(1)}, u32[]{:S(2)}, u32[]{:S(2)}) async-start(bf16[4,160,640]{2,1,0:T(8,128)(2,1)} %tie.20), calls=%async_computation.1 | async-start | bytes 1638400 | tf_op jit(solution)/shard_map/all_to_all | solution.py:750
  55.9 40.7 %all-to-all-start.2 = ((bf16[4,160,1280]{2,1,0:T(8,128)(2,1)}), bf16[4,160,1280]{2,1,0:T(8,128)(2,1)S(1)}, u32[]{:S(2)}, u32[]{:S(2)}) async-start(bf16[4,160,1280]{2,1,0:T(8,128)(2,1)} %tie.22), calls=%async_computation.2 | async-start | bytes 3276800 | tf_op jit(solution)/shard_map/all_to_all | solution.py:750
  62.8 38.8 %collective-permute-start.6 = (bf16[336,640]{1,0:T(8,128)(2,1)S(1)}, bf16[336,640]{1,0:T(8,128)(2,1)}, u32[]{:S(2)}, u32[]{:S(2)}) collective-permute-start(bf16[336,640]{1,0:T(8,128)(2,1)S(1)} %copy-done.14), channel_id=1, source_target_pairs={{0,4},{4,0},{8,12},{12,8},{16,20},{20,16},{24,28},{28,24},{1,5},{5... | collective-permute-start | bytes 1290248 | tf_op jit(solution)/shard_map/ppermute | solution.py:687
  62.8 41.4 %collective-permute-start.7 = (bf16[336,640]{1,0:T(8,128)(2,1)}, bf16[336,640]{1,0:T(8,128)(2,1)}, u32[]{:S(2)}, u32[]{:S(2)}) collective-permute-start(bf16[336,640]{1,0:T(8,128)(2,1)} %copy-done.29), channel_id=1, source_target_pairs={{0,4},{4,0},{8,12},{12,8},{16,20},{20,16},{24,28},{28,24},{1,5},{5... | collective-permute-start | bytes 1290248 | tf_op jit(solution)/shard_map/ppermute | solution.py:687
  63.3 40.9 %collective-permute-start.8 = (bf16[336,640]{1,0:T(8,128)(2,1)}, bf16[336,640]{1,0:T(8,128)(2,1)}, u32[]{:S(2)}, u32[]{:S(2)}) collective-permute-start(bf16[336,640]{1,0:T(8,128)(2,1)} %copy-done.30), channel_id=1, source_target_pairs={{0,4},{4,0},{8,12},{12,8},{16,20},{20,16},{24,28},{28,24},{1,5},{5... | collective-permute-start | bytes 1290248 | tf_op jit(solution)/shard_map/ppermute | solution.py:687
  78.1 26.1 %collective-permute-start.10 = (bf16[176,640]{1,0:T(8,128)(2,1)}, bf16[176,640]{1,0:T(8,128)(2,1)}, u32[]{:S(2)}, u32[]{:S(2)}) collective-permute-start(bf16[176,640]{1,0:T(8,128)(2,1)} %collective-permute-done.3.refs_7_.refs_4_.refs_6_), channel_id=1, source_target_pairs={{0,4},{4,0},{8,12},{12,8},{16,20},{20,16},{24,28},{28,24},{1,5},{5... | collective-permute-start | bytes 675848 | tf_op jit(solution)/shard_map/ppermute | solution.py:687
  80.2 24.0 %collective-permute-start.9 = (bf16[160,640]{1,0:T(8,128)(2,1)}, bf16[160,640]{1,0:T(8,128)(2,1)}, u32[]{:S(2)}, u32[]{:S(2)}) collective-permute-start(bf16[160,640]{1,0:T(8,128)(2,1)} %collective-permute-done.1.refs_6_.refs_3_), channel_id=1, source_target_pairs={{0,4},{4,0},{8,12},{12,8},{16,20},{20,16},{24,28},{28,24},{1,5},{5... | collective-permute-start | bytes 614408 | tf_op jit(solution)/shard_map/ppermute | solution.py:687
  98.1 24.5 %all-to-all-start.3 = ((bf16[4,160,640]{2,1,0:T(8,128)(2,1)}), bf16[4,160,640]{2,1,0:T(8,128)(2,1)S(1)}, u32[]{:S(2)}, u32[]{:S(2)}) async-start(bf16[4,160,640]{2,1,0:T(8,128)(2,1)} %tie.25), calls=%async_computation.3 | async-start | bytes 1638400 | tf_op jit(solution)/shard_map/all_to_all | solution.py:750
  102.7 37.9 %collective-permute-start.11 = (bf16[640,640]{1,0:T(8,128)(2,1)S(1)}, bf16[640,640]{1,0:T(8,128)(2,1)S(1)}, u32[]{:S(2)}, u32[]{:S(2)}) collective-permute-start(bf16[640,640]{1,0:T(8,128)(2,1)S(1)} %copy-done.20), channel_id=1, source_target_pairs={{0,8},{4,12},{8,0},{12,4},{16,24},{20,28},{24,16},{28,20},{1,9},{5... | collective-permute-start | bytes 2457608 | tf_op jit(solution)/shard_map/ppermute | solution.py:687
  123.5 27.6 %collective-permute-start.12 = (bf16[640,640]{1,0:T(8,128)(2,1)}, bf16[640,640]{1,0:T(8,128)(2,1)S(1)}, u32[]{:S(2)}, u32[]{:S(2)}) collective-permute-start(bf16[640,640]{1,0:T(8,128)(2,1)} %tie.26.refs_1_.refs_5_), channel_id=1, source_target_pairs={{0,8},{4,12},{8,0},{12,4},{16,24},{20,28},{24,16},{28,20},{1,9},{5... | collective-permute-start | bytes 2457608 | tf_op jit(solution)/shard_map/ppermute | solution.py:687
  124.3 44.1 %all-to-all-start.4 = ((bf16[4,160,768]{2,1,0:T(8,128)(2,1)}), bf16[4,160,768]{2,1,0:T(8,128)(2,1)S(1)}, u32[]{:S(2)}, u32[]{:S(2)}) async-start(bf16[4,160,768]{2,1,0:T(8,128)(2,1)} %tie.29), calls=%async_computation.4 | async-start | bytes 1966080 | tf_op jit(solution)/shard_map/all_to_all | solution.py:750
  171.2 34.1 %collective-permute-start.16 = (bf16[640,640]{1,0:T(8,128)(2,1)S(1)}, bf16[640,640]{1,0:T(8,128)(2,1)S(1)}, u32[]{:S(2)}, u32[]{:S(2)}) collective-permute-start(bf16[640,640]{1,0:T(8,128)(2,1)S(1)} %copy-done.4), channel_id=1, source_target_pairs={{0,16},{4,20},{8,24},{12,28},{16,0},{20,4},{24,8},{28,12},{1,17},{... | collective-permute-start | bytes 2457608 | tf_op jit(solution)/shard_map/ppermute | solution.py:687
  202.8 20.6 %collective-permute-start.18 = (bf16[640,640]{1,0:T(8,128)(2,1)}, bf16[640,640]{1,0:T(8,128)(2,1)S(1)}, u32[]{:S(2)}, u32[]{:S(2)}) collective-permute-start(bf16[640,640]{1,0:T(8,128)(2,1)} %get-tuple-element.104), channel_id=1, source_target_pairs={{0,16},{4,20},{8,24},{12,28},{16,0},{20,4},{24,8},{28,12},{1,17},{... | collective-permute-start | bytes 2457608 | tf_op jit(solution)/shard_map/ppermute | solution.py:687
  203.8 20.7 %collective-permute-start.17 = (bf16[640,640]{1,0:T(8,128)(2,1)}, bf16[640,640]{1,0:T(8,128)(2,1)S(1)}, u32[]{:S(2)}, u32[]{:S(2)}) collective-permute-start(bf16[640,640]{1,0:T(8,128)(2,1)} %get-tuple-element.102), channel_id=1, source_target_pairs={{0,8},{4,12},{8,0},{12,4},{16,24},{20,28},{24,16},{28,20},{1,9},{5... | collective-permute-start | bytes 2457608 | tf_op jit(solution)/shard_map/ppermute | solution.py:687
  244.7 35.3 %collective-permute-start.24 = (bf16[640,640]{1,0:T(8,128)(2,1)}, bf16[640,640]{1,0:T(8,128)(2,1)S(1)}, u32[]{:S(2)}, u32[]{:S(2)}) collective-permute-start(bf16[640,640]{1,0:T(8,128)(2,1)} %get-tuple-element.120), channel_id=1, source_target_pairs={{0,16},{4,20},{8,24},{12,28},{16,0},{20,4},{24,8},{28,12},{1,17},{... | collective-permute-start | bytes 2457608 | tf_op jit(solution)/shard_map/ppermute | solution.py:687
  245.7 34.3 %collective-permute-start.21 = (bf16[640,640]{1,0:T(8,128)(2,1)}, bf16[640,640]{1,0:T(8,128)(2,1)S(1)}, u32[]{:S(2)}, u32[]{:S(2)}) collective-permute-start(bf16[640,640]{1,0:T(8,128)(2,1)} %get-tuple-element.119), channel_id=1, source_target_pairs={{0,8},{4,12},{8,0},{12,4},{16,24},{20,28},{24,16},{28,20},{1,9},{5... | collective-permute-start | bytes 2457608 | tf_op jit(solution)/shard_map/ppermute | solution.py:687
  247.2 36.3 %collective-permute-start.23 = (bf16[640,640]{1,0:T(8,128)(2,1)}, bf16[640,640]{1,0:T(8,128)(2,1)S(1)}, u32[]{:S(2)}, u32[]{:S(2)}) collective-permute-start(bf16[640,640]{1,0:T(8,128)(2,1)} %add_convert_fusion.4.refs_5_), channel_id=1, source_target_pairs={{0,8},{4,12},{8,0},{12,4},{16,24},{20,28},{24,16},{28,20},{1,9},{5... | collective-permute-start | bytes 2457608 | tf_op jit(solution)/shard_map/ppermute | solution.py:687
  247.7 35.7 %collective-permute-start.22 = (bf16[640,640]{1,0:T(8,128)(2,1)}, bf16[640,640]{1,0:T(8,128)(2,1)}, u32[]{:S(2)}, u32[]{:S(2)}) collective-permute-start(bf16[640,640]{1,0:T(8,128)(2,1)} %add_convert_fusion.5.refs_4_), channel_id=1, source_target_pairs={{0,16},{4,20},{8,24},{12,28},{16,0},{20,4},{24,8},{28,12},{1,17},{... | collective-permute-start | bytes 2457608 | tf_op jit(solution)/shard_map/ppermute | solution.py:687
  252.2 43.6 %all-to-all-start.5 = ((bf16[4,160,768]{2,1,0:T(8,128)(2,1)}), bf16[4,160,768]{2,1,0:T(8,128)(2,1)S(1)}, u32[]{:S(2)}, u32[]{:S(2)}) async-start(bf16[4,160,768]{2,1,0:T(8,128)(2,1)} %bitcast.19), calls=%async_computation.5 | async-start | bytes 1966080 | tf_op jit(solution)/shard_map/all_to_all | solution.py:750
  288.4 36.2 %collective-permute-start.42 = (bf16[160,1280]{1,0:T(8,128)(2,1)}, bf16[160,1280]{1,0:T(8,128)(2,1)}, u32[]{:S(2)}, u32[]{:S(2)}) collective-permute-start(bf16[160,1280]{1,0:T(8,128)(2,1)} %get-tuple-element.178), channel_id=1, source_target_pairs={{0,1},{1,2},{2,3},{3,0},{4,5},{5,6},{6,7},{7,4},{8,9},{9,10},{10,1... | collective-permute-start | bytes 1228808 | tf_op jit(solution)/shard_map/ppermute | solution.py:667
  290.6 34.0 %collective-permute-start.43 = (bf16[160,1280]{1,0:T(8,128)(2,1)}, bf16[160,1280]{1,0:T(8,128)(2,1)}, u32[]{:S(2)}, u32[]{:S(2)}) collective-permute-start(bf16[160,1280]{1,0:T(8,128)(2,1)} %get-tuple-element.179), channel_id=1, source_target_pairs={{0,2},{1,3},{2,0},{3,1},{4,6},{5,7},{6,4},{7,5},{8,10},{9,11},{10,... | collective-permute-start | bytes 1228808 | tf_op jit(solution)/shard_map/ppermute | solution.py:667
  293.0 31.7 %collective-permute-start.44 = (bf16[160,1280]{1,0:T(8,128)(2,1)}, bf16[160,1280]{1,0:T(8,128)(2,1)}, u32[]{:S(2)}, u32[]{:S(2)}) collective-permute-start(bf16[160,1280]{1,0:T(8,128)(2,1)} %get-tuple-element.180), channel_id=1, source_target_pairs={{0,3},{1,0},{2,1},{3,2},{4,7},{5,4},{6,5},{7,6},{8,11},{9,8},{10,9... | collective-permute-start | bytes 1228808 | tf_op jit(solution)/shard_map/ppermute | solution.py:667
  347.6 57.7 %all-to-all-start.6 = ((bf16[4,160,1280]{2,1,0:T(8,128)(2,1)}), bf16[4,160,1280]{2,1,0:T(8,128)(2,1)S(1)}, u32[]{:S(2)}, u32[]{:S(2)}) async-start(bf16[4,160,1280]{2,1,0:T(8,128)(2,1)} %bitcast.21), calls=%async_computation.6 | async-start | bytes 3276800 | tf_op jit(solution)/shard_map/all_to_all | solution.py:750
  356.1 22.0 %collective-permute-start.35 = (bf16[1,4,80,640]{3,2,1,0:T(8,128)(2,1)}, bf16[1,4,80,640]{3,2,1,0:T(8,128)(2,1)}, u32[]{:S(2)}, u32[]{:S(2)}) collective-permute-start(bf16[1,4,80,640]{3,2,1,0:T(8,128)(2,1)} %pad_maximum_fusion.4.refs_2_.refs_5_), channel_id=1, source_target_pairs={{0,16},{4,20},{8,24},{12,28},{16,0},{20,4},{24,8},{28,12},{1,17},{... | collective-permute-start | bytes 1228808 | tf_op jit(solution)/shard_map/ppermute | solution.py:687
  (67 other events, 477.6 us)

commit v2 on v1

--- a/solution.py
+++ b/solution.py
@@ -160,7 +160,7 @@
     }
 
 
-def run_forward(starts, small, qt, k, vt, segk, segq, span_of_groups, outs=()):
+def run_forward(starts, small, qt, k, vt, segk, segq, span_of_groups, outs=(), first=()):
     D, rows = qt.shape
     span = k.shape[0]
     begin, end = span_of_groups
@@ -173,7 +173,7 @@
             num_scalar_prefetch=2,
             grid=(end - begin, rows // QT),
             in_specs=[s["q_cols"], s["k_rows"], s["k_cols"], s["segk"], s["segq"]]
-            + [pl.BlockSpec(memory_space=pl.ANY)] * len(outs),
+            + [pl.BlockSpec(memory_space=pl.ANY)] * (len(outs) + len(first)),
             out_specs=[s["q_cols"], s["lse"]],
         ),
         input_output_aliases={7: 0, 8: 1} if outs else {},
@@ -183,10 +183,10 @@
         ],
         name="attend_forward",
         **kernel_params(4 * (end - begin)),
-    )(starts, small, qt, k, vt, segk, segq, *outs)
-
-
-def run_backward(starts, small, qt, kt, k, v, dot, att, lse, segk, segq, span_of_groups, outs=()):
+    )(starts, small, qt, k, vt, segk, segq, *outs, *first)
+
+
+def run_backward(starts, small, qt, kt, k, v, dot, att, lse, segk, segq, span_of_groups, outs=(), first=()):
     D, rows = qt.shape
     span = k.shape[0]
     begin, end = span_of_groups
@@ -201,7 +201,7 @@
                 s["q_cols"], s["k_cols"], s["k_rows"], s["k_rows"], s["q_cols"], s["q_cols"],
                 s["lse"], s["segk"], s["segq"],
             ]
-            + [pl.BlockSpec(memory_space=pl.ANY)] * len(outs),
+            + [pl.BlockSpec(memory_space=pl.ANY)] * (len(outs) + len(first)),
             out_specs=[s["q_cols"], s["k_rows"], s["k_rows"]],
             scratch_shapes=[pltpu.VMEM((span, LANES), f32), pltpu.VMEM((span, LANES), f32)],
         ),
@@ -213,7 +213,7 @@
         input_output_aliases={11: 0, 12: 1, 13: 2} if outs else {},
         name="attend_backward",
         **kernel_params(6 * (end - begin)),
-    )(starts, small, qt, kt, k, v, dot, att, lse, segk, segq, *outs)
+    )(starts, small, qt, kt, k, v, dot, att, lse, segk, segq, *outs, *first)
 
 
 def norm_parts(cols):
@@ -259,8 +259,39 @@
     }
 
 
+def pack(qkv_ref, out_ref, *refs):
+    vectors, (piece_ref, rows, turned) = refs[:-3], refs[-3:]
+    part, dw = out_ref.shape
+    rows[...] = jnp.zeros_like(rows)
+    turned[...] = jnp.zeros_like(turned)
+    turned[:part, :dw] = out_ref[...].astype(f32)
+    for c in range(3):
+        rows[c * dw : (c + 1) * dw, :part] = qkv_ref[c].astype(f32)
+    rows[3 * dw : 4 * dw, :] = turned[...].T[:dw, :]
+    at = VEC_BLOCK * LANES + VEC_AT
+    for ref in vectors:
+        count = ref.shape[0] if len(ref.shape) == 2 else 1
+        rows[at : at + count, :part] = ref[...].reshape(count, part).astype(f32)
+        at += count
+    piece = rows[...].T[:part, :].astype(bf16)
+    for n in range(piece_ref.shape[0]):
+        piece_ref[n] = piece
+
+
+def run_pack(w_qkv, w_out, vectors, members):
+    part = w_out.shape[0]
+    height, wide = (VEC_BLOCK + 1) * LANES, -(-part // LANES) * LANES
+    return pl.pallas_call(
+        pack,
+        out_shape=jax.ShapeDtypeStruct((members, part, height), bf16),
+        scratch_shapes=[pltpu.VMEM((height, wide), f32), pltpu.VMEM((wide, LANES), f32)],
+        name="pack",
+        **kernel_params(2),
+    )(w_qkv, w_out, *vectors)
+
+
 def project(parts, count, member_ref, x_ref, vec_ref, *refs):
-    pieces, refs = refs[:count], refs[count:]
+    pieces, refs = refs[:count], refs[-11:]
     n_ref, qt_ref, kt_ref, vt_ref, k_ref, v_ref, w_ref, w, wt, in_sem, out_sem = refs
     i = pl.program_id(0)
     out = pltpu.make_async_copy(w, w_ref, out_sem)
@@ -298,7 +329,7 @@
         out.wait()
 
 
-def run_project(x, vec, member, pieces, parts):
+def run_project(x, vec, member, pieces, parts, first):
     D, span = x.shape
     steps = span // QT
     cols = pl.BlockSpec((D, QT), lambda i, _: (0, i))
@@ -311,7 +342,7 @@
         grid_spec=pltpu.PrefetchScalarGridSpec(
             num_scalar_prefetch=1,
             grid=(steps,),
-            in_specs=[cols, whole((D, LANES), (0, VEC_BLOCK))] + [anywhere] * len(pieces),
+            in_specs=[cols, whole((D, LANES), (0, VEC_BLOCK))] + [anywhere] * (len(pieces) + len(first)),
             out_specs=[cols, own, cols, cols, rows, rows, anywhere],
             scratch_shapes=[
                 pltpu.VMEM((4, D, D), bf16),
@@ -331,7 +362,7 @@
         ],
         name="project",
         **kernel_params(11),
-    )(member, x, vec, *pieces)
+    )(member, x, vec, *pieces, *first)
 
 
 def project_weights(masks, member_ref, n_ref, dqt_ref, dk_ref, dv_ref, gwo_ref, *refs):
@@ -385,7 +416,8 @@
     )(member, normed, dqt, dk, dv, gwo)
 
 
-def project_back(x_ref, dqt_ref, dk_ref, dv_ref, w_ref, mid_ref, vec_ref, grad_ref, rows_ref, sums_ref):
+def project_back(x_ref, dqt_ref, dk_ref, dv_ref, w_ref, mid_ref, vec_ref, *refs):
+    grad_ref, rows_ref, sums_ref = refs[-3:]
     i = pl.program_id(0)
     own = (i >= 1) & (i < pl.num_programs(0) - 1)
 
@@ -406,7 +438,7 @@
         rows_ref[...] = row_sums([sums_ref[0], sums_ref[1]])
 
 
-def run_project_back(x, dqt, dk, dv, w, grad_mid, vec):
+def run_project_back(x, dqt, dk, dv, w, grad_mid, vec, first):
     D, span = x.shape
     steps = span // QT
     cols = pl.BlockSpec((D, QT), lambda i: (0, i))
@@ -416,13 +448,14 @@
     return pl.pallas_call(
         project_back,
         grid=(steps,),
-        in_specs=[cols, own, rows, rows, whole((3, D, D)), own, whole((D, LANES), (0, VEC_BLOCK))],
+        in_specs=[cols, own, rows, rows, whole((3, D, D)), own, whole((D, LANES), (0, VEC_BLOCK))]
+        + [pl.BlockSpec(memory_space=pl.ANY)] * len(first),
         out_specs=[cols, whole((8, D))],
         out_shape=[shape((D, span), bf16), shape((8, D), f32)],
         scratch_shapes=[pltpu.VMEM((2, D, LANES), f32)],
         name="project_back",
         **kernel_params(10),
-    )(x, dqt, dk, dv, w, grad_mid, vec)
+    )(x, dqt, dk, dv, w, grad_mid, vec, *first)
 
 
 def branch(att_ref, wo_ref, x_ref, vec_ref, mid_ref, n_ref):
@@ -508,12 +541,13 @@
     )(gn, got, middle, g, att, w, vec)
 
 
-def feed_forward(first, final, places, *refs):
+def feed_forward(first, final, ahead, places, *refs):
     blocks, weights = len(places), 1 + max(p[0] for place in places for p in place)
     n2_in, g_in, refs = refs[0:2], refs[2:4], refs[4:]
     weights, refs = refs[:weights], refs[weights:]
     if not first:
         sums_in, refs = refs[:4], refs[4:]
+    refs = refs[ahead:]
     sums_out, refs = refs[:4], refs[4:]
     dw_out, refs = refs[: 2 * blocks], refs[2 * blocks :]
     dub_out, refs = refs[:blocks], refs[blocks:]
@@ -613,7 +647,7 @@
         copy.wait()
 
 
-def run_feed_forward(n2, g, blocks, sums, final=False):
+def run_feed_forward(n2, g, blocks, sums, final=False, ahead=()):
     D, rows = n2[0].shape
     F = D
     first = sums is None
@@ -633,8 +667,8 @@
     vmem = pl.BlockSpec(memory_space=pltpu.VMEM)
     own_type = f32 if final else bf16
     outs = pl.pallas_call(
-        functools.partial(feed_forward, first, final, places),
-        in_specs=[anywhere] * (4 + len(weights) + len(sums)),
+        functools.partial(feed_forward, first, final, len(ahead), places),
+        in_specs=[anywhere] * (4 + len(weights) + len(sums) + len(ahead)),
         out_specs=[anywhere] * (4 + 2 * count) + [vmem] * count,
         out_shape=[shape((D, rows), t) for t in (own_type, bf16, own_type, bf16)]
         + [shape((D, F), bf16)] * (2 * count)
@@ -657,7 +691,7 @@
         ],
         name="feed_forward",
         **kernel_params(14 * count),
-    )(*n2, *g, *weights, *sums)
+    )(*n2, *g, *weights, *sums, *ahead)
     grads = [(*outs[4 + 2 * b : 6 + 2 * b], outs[4 + 2 * count + b]) for b in range(count)]
     return outs[:4], grads
 
@@ -764,14 +798,9 @@
     segk = jnp.broadcast_to(chunk[:, None], (span, LANES))
     segq = jnp.broadcast_to(chunk_own[None], (8, quarter))
 
-    piece = [w_qkv.reshape(3 * dw, part).T, w_out]
-    piece += [jnp.zeros((part, VEC_BLOCK * LANES + VEC_AT - 4 * dw), bf16)]
-    piece += [
-        jnp.stack([ln1_gain, ln1_shift, qv_bias[0], qv_bias[1], out_bias, ln2_gain, ln2_shift, down_bias]).T
-    ]
-    piece = jnp.concatenate(piece, axis=1)
-    piece = jnp.pad(piece, ((0, 0), (0, -piece.shape[1] % LANES)))
-    vec = across(jnp.stack([piece] * nn)).reshape(D, -1)
+    vectors = [ln1_gain, ln1_shift, qv_bias, out_bias, ln2_gain, ln2_shift, down_bias]
+    piece = run_pack(w_qkv, w_out, vectors, nn)
+    vec = across(piece).reshape(D, -1)
     up_own = across(after((vec,), jnp.stack([w_up] * nn))).reshape(D, -1)
     units = up_bias.shape[0]
     bias_rows = jnp.pad(up_bias[None], ((0, 15), (0, D - units)))
@@ -825,8 +854,7 @@
         up_own = jnp.concatenate([up_own, swap(up_own, bit)], axis=1)
     F = up_own.shape[1]
     up_x, up_y = swap(up_own, X), swap(up_own, Y)
-    x_low = after((up_x, up_y), x_low)
-    normed, qt, kt, vt, k, v, w_attn = run_project(x_low, vec, member, pieces, parts)
+    normed, qt, kt, vt, k, v, w_attn = run_project(x_low, vec, member, pieces, parts, (up_x, up_y))
     groups = D // LANES
     forward_in = starts, small, qt, k, vt, segk, segq
     att, lse = run_forward(*forward_in, (0, 1))
@@ -837,8 +865,7 @@
         dt_own = jnp.concatenate([dt_own, swap(dt_own, bit)], axis=1)
     dt_x, dt_y = swap(dt_own, X), swap(dt_own, Y)
     up_xy = swap(up_y, X)
-    att = after((up_xy,), att)
-    att, lse = run_forward(*forward_in, (1, 3), (att, lse))
+    att, lse = run_forward(*forward_in, (1, 3), (att, lse), (up_xy,))
     dt_x = after((att,), dt_x)
     dt_xy = swap(dt_x, Y)
     att, lse = run_forward(*forward_in, (3, groups), (att, lse))
@@ -858,9 +885,8 @@
     dt_got_y = swap(dt_gy, Y)
     up_gy, dt_gx = add(up_gy, up_got_xy).astype(bf16), add(dt_gx, dt_got_xy).astype(bf16)
     up_got_y, dt_got_x = swap(up_gy, Y), swap(dt_gx, X)
-    sums = after((up_gy, dt_gx), *sums)
     blocks = [((up_own, 0), (dt_own, 0), ub_own)]
-    sums, ((up_g, dt_g, ub_g),) = run_feed_forward(n2_pair, grad_pair, blocks, sums, True)
+    sums, ((up_g, dt_g, ub_g),) = run_feed_forward(n2_pair, grad_pair, blocks, sums, True, (up_gy, dt_gx))
     gn_sum, gn_other, out_sum, out_other = sums
     gn_got, out_got = swap(gn_other, CORE), swap(out_other, CORE)
 
@@ -872,7 +898,7 @@
         gn_sum, gn_got, middle, grad_cols, att, w_attn, vec
     )
     back_in = starts, small, qt, kt, k, v, grad_att, att, lse, segk, segq
-    back_a = run_backward(*back_in, (0, 2))
+    back_a = run_backward(*back_in, (0, 3))
     up_got_x, up_got_y, dt_got_x, dt_got_y = after((back_a[0],), up_got_x, up_got_y, dt_got_x, dt_got_y)
     up_g, dt_g = add(up_g, up_got_x, up_got_y), add(dt_g, dt_got_x, dt_got_y)
     for bit in reversed(high):
@@ -881,8 +907,7 @@
         dt_g = dt_g[:, :half] + swap(dt_g[:, half:].astype(bf16), bit).astype(f32)
     ud_g = jnp.concatenate([up_g, dt_g], axis=1).astype(bf16)
     ud_grad = z_scatter_sum(ud_g.reshape(nn, part, -1))
-    dqt_a = after((ud_g, layer_out), back_a[0])
-    dqt, dk, dv = run_backward(*back_in, (2, groups), (dqt_a, *back_a[1:]))
+    dqt, dk, dv = run_backward(*back_in, (3, groups), back_a, (ud_g, layer_out))
     masks = [0]
     for bit in high:
         masks = masks + [m ^ bit for m in masks]
@@ -896,8 +921,7 @@
         )
         grad_w = pick(masks), pick([m ^ CORE for m in masks])
     attn_g, got = grad_w[0], swap(grad_w[1], CORE)
-    dqt = after((grad_w[1],), dqt)
-    grad_in, sums_one = run_project_back(x_low, dqt, dk, dv, w_attn, grad_mid, vec)
+    grad_in, sums_one = run_project_back(x_low, dqt, dk, dv, w_attn, grad_mid, vec, (grad_w[1],))
     got = after((grad_in,), got)
     vector_rows = jnp.concatenate([sums_one[:2], qv_rows[:2], sums_two[:4]])
     up_grad, down_grad = ud_grad[:, :units], ud_grad[:, units:].T

time: 412 us -> 408 us (level)
  local copies, waits for them, and re-layouts: 41.2 us -> 33.7 us
    ppermute x36, waiting for transfers between devices: 40.2 us -> 21.7 us  [swap(): return lax.ppermute(x, 'wide', [(i, i ^ mask) for i in range(n)])]
    all_to_all x7, waiting for transfers between devices: 26.9 us -> 43.3 us  [shards(): across = lambda x: lax.all_to_all(x, 'narrow', 0, 0, tiled=True)]
    another operation x8 -> x0, local copies, waits for them, and re-layouts: 5.47 us -> none  [the longest x7 4.65 us: shards(): jnp.stack([ln1_gain, ln1_shift, qv_bias[0], qv_bias[1], out_bias, ln2_gai...]
    pallas_call x3 -> x4, Pallas kernels: 62.2 us -> 64.2 us  [the longest x3 62.2 us: run_feed_forward(): pl.pallas_call(functools.partial(feed_forward, first, final, len(ahead),...]
  transfers between devices with their start and end apart: 52 -> 52, of which waited for: 15 -> 17; matrix products, arithmetic and copies ran while one was open for 11% -> 11% of each run, Pallas kernels for 36% -> 36%
where the time goes in v2:
time: 408 us; the launch traced here: 405 us
  Pallas kernels  167 us (41%)
  starting transfers between devices  95.5 us (23%)
  waiting for transfers between devices  72.5 us (18%)
  local copies, waits for them, and re-layouts  33.7 us (8%)
  other arithmetic  32.6 us (8%)
    pallas_call x3, Pallas kernels, run_feed_forward(): pl.pallas_call(functools.partial(feed_forward, first, final, len(ahead),...  62.2 us
    all_to_all x7, starting transfers between devices, shards(): across = lambda x: lax.all_to_all(x, 'narrow', 0, 0, tiled=True)  48.3 us
    all_to_all x7, waiting for transfers between devices, shards(): across = lambda x: lax.all_to_all(x, 'narrow', 0, 0, tiled=True)  43.3 us
    ppermute x36, starting transfers between devices, swap(): return lax.ppermute(x, 'wide', [(i, i ^ mask) for i in range(n)])  33.6 us
    pallas_call x2, Pallas kernels, run_backward(): pl.pallas_call(attend_backward, grid_spec=pltpu.PrefetchScalarGridSpec(nu...  32.7 us
    pallas_call x3, Pallas kernels, run_forward(): pl.pallas_call(attend_forward, grid_spec=pltpu.PrefetchScalarGridSpec(num...  24.9 us
    ppermute x36, waiting for transfers between devices, swap(): return lax.ppermute(x, 'wide', [(i, i ^ mask) for i in range(n)])  21.7 us
    ppermute x9, starting transfers between devices, z_rotate(): return lax.ppermute(x, 'narrow', [(i, (i + k) % n) for i in range(n)])  13.6 us
  transfers between devices with their start and end apart: 52, of which 17 were waited for; matrix products, arithmetic and copies ran while one was open for 11% of the time, Pallas kernels for 36%

profile of v2, /device:TPU:0, one launch (start us, length us, event | category | flops | bytes accessed | tf_op | source)
XLA Modules:
  0.0 404.7 jit_solution(11820258261881217729)
XLA Ops:
  2.6 6.4 %all-to-all-start = ((bf16[4,160,384]{2,1,0:T(8,128)(2,1)}), bf16[4,160,384]{2,1,0:T(8,128)(2,1)S(1)}, u32[]{:S(2)}, u32[]{:S(2)}) async-start(bf16[4,160,384]{2,1,0:T(8,128)(2,1)} %pack.1), calls=%async_computation | async-start | bytes 983040 | tf_op jit(solution)/shard_map/all_to_all | solution.py:784
  11.5 11.4 %all-to-all-done = bf16[4,160,384]{2,1,0:T(8,128)(2,1)S(1)} async-done(((bf16[4,160,384]{2,1,0:T(8,128)(2,1)}), bf16[4,160,384]{2,1,0:T(8,128)(2,1)S(1)}, u32[]{:S(2)}, u32[]{:S(2)}) %all-to-all-start) | async-done | bytes 491552 | tf_op jit(solution)/shard_map/all_to_all | solution.py:784
  23.9 3.6 all-to-all-start.1
  33.5 6.3 %collective-permute-done.2.refs_1_.refs_9_ = bf16[336,640]{1,0:T(8,128)(2,1)S(1)} collective-permute-done((bf16[336,640]{1,0:T(8,128)(2,1)}, bf16[336,640]{1,0:T(8,128)(2,1)S(1)}, u32[]{:S(2)}, u32[]{:S(2)}) %collective-permute-start.2) | collective-permute-done | bytes 430112 | tf_op jit(solution)/shard_map/ppermute | solution.py:721
  43.8 3.7 collective-permute-done.1.refs_6_.refs_3_
  49.7 5.0 %all-to-all-start.2 = ((bf16[4,160,1280]{2,1,0:T(8,128)(2,1)}), bf16[4,160,1280]{2,1,0:T(8,128)(2,1)S(1)}, u32[]{:S(2)}, u32[]{:S(2)}) async-start(bf16[4,160,1280]{2,1,0:T(8,128)(2,1)} %tie.17), calls=%async_computation.2 | async-start | bytes 3276800 | tf_op jit(solution)/shard_map/all_to_all | solution.py:784
  59.9 31.3 %all-to-all-done.2 = bf16[4,160,1280]{2,1,0:T(8,128)(2,1)S(1)} async-done(((bf16[4,160,1280]{2,1,0:T(8,128)(2,1)}), bf16[4,160,1280]{2,1,0:T(8,128)(2,1)S(1)}, u32[]{:S(2)}, u32[]{:S(2)}) %all-to-all-start.2) | async-done | bytes 1638432 | tf_op jit(solution)/shard_map/all_to_all | solution.py:784
  97.8 12.3 %project.1 = (bf16[640,1280]{1,0:T(8,128)(2,1)}, bf16[640,768]{1,0:T(8,128)(2,1)}, bf16[640,1280]{1,0:T(8,128)(2,1)}, bf16[640,1280]{1,0:T(8,128)(2,1)}, bf16[12...) custom-call(s32[1]{0:T(128)} %bitcast.member_ref, bf16[640,1280]{1,0:T(8,128)(2,1)} %bitcast.91, ...), custom_call_target="tpu_custom_call" | custom-call | flops 11000000512 | bytes 1000000 | tf_op jit(solution)/shard_map/project/pallas_call | solution.py:340
  110.1 6.0 %attend_forward.3 = (bf16[640,768]{1,0:T(8,128)(2,1)}, f32[40,768]{1,0:T(8,128)}) custom-call(s32[3]{0:T(128)} %get-tuple-element.164.refs_1_.start_ref, s32[3]{0:T(128)} %get-tuple-element.165.refs_2_.small_ref, bf16[640,768]{1,0:T(8,128)(2,1)} %get-tuple-element.78.q_ref.qt_ref, bf16[1280,640]{1,0:T(8,128)(2,1)} %get-tuple-element.79.k_ref, ...), custom_call_target="tpu_custom_call" | custom-call | flops 4000000000 | bytes 1000000 | tf_op jit(solution)/shard_map/attend_forward/pallas_call | solution.py:170
  118.8 15.3 %all-to-all-start.4 = ((bf16[4,160,768]{2,1,0:T(8,128)(2,1)}), bf16[4,160,768]{2,1,0:T(8,128)(2,1)S(1)}, u32[]{:S(2)}, u32[]{:S(2)}) async-start(bf16[4,160,768]{2,1,0:T(8,128)(2,1)} %tie.22), calls=%async_computation.4 | async-start | bytes 1966080 | tf_op jit(solution)/shard_map/all_to_all | solution.py:784
  135.1 9.5 %attend_forward.4 = (bf16[640,768]{1,0:T(8,128)(2,1)}, f32[40,768]{1,0:T(8,128)}) custom-call(s32[3]{0:T(128)} %get-tuple-element.164.refs_1_.start_ref, s32[3]{0:T(128)} %get-tuple-element.165.refs_2_.small_ref, bf16[640,768]{1,0:T(8,128)(2,1)} %get-tuple-element.78.q_ref.qt_ref, ...), custom_call_target="tpu_custom_call", output_to_operand_aliasing={{0}: (7, {}), {1}: (8, {})} | custom-call | flops 8000000000 | bytes 1000000 | tf_op jit(solution)/shard_map/attend_forward/pallas_call | solution.py:170
  147.1 9.5 %attend_forward.5 = (bf16[640,768]{1,0:T(8,128)(2,1)}, f32[40,768]{1,0:T(8,128)}) custom-call(s32[3]{0:T(128)} %get-tuple-element.164.refs_1_.start_ref, s32[3]{0:T(128)} %get-tuple-element.165.refs_2_.small_ref, bf16[640,768]{1,0:T(8,128)(2,1)} %get-tuple-element.78.q_ref.qt_ref, ...), custom_call_target="tpu_custom_call", output_to_operand_aliasing={{0}: (7, {}), {1}: (8, {})} | custom-call | flops 8000000000 | bytes 1000000 | tf_op jit(solution)/shard_map/attend_forward/pallas_call | solution.py:170
  156.5 4.8 %branch.1 = (f32[640,768]{1,0:T(8,128)}, bf16[640,768]{1,0:T(8,128)(2,1)}) custom-call(bf16[640,768]{1,0:T(8,128)(2,1)} %get-tuple-element.85.att_ref.refs_1_, bf16[4,640,640]{2,1,0:T(8,128)(2,1)} %get-tuple-element.86.wo_ref.w_ref, bf16[640,1280]{1,0:T(8,128)(2,1)} %bitcast.92, bf16[640,384]{1,0:T(8,128)(2,1)} %bitcast.84), custom_call_target="tpu_custom_call" | custom-call | flops 5000000000 | bytes 1000000 | tf_op jit(solution)/shard_map/branch/pallas_call | solution.py:472
  169.1 27.9 %feed_forward.3 = (bf16[640,768]{1,0:T(8,128)(2,1)}, bf16[640,768]{1,0:T(8,128)(2,1)}, bf16[640,768]{1,0:T(8,128)(2,1)}, bf16[640,768]{1,0:T(8,128)(2,1)}, bf16[...) custom-call(bf16[640,768]{1,0:T(8,128)(2,1)} %tie.21.refs_0_, ...), custom_call_target="tpu_custom_call" | custom-call | flops 28000000000 | bytes 1000000 | tf_op jit(solution)/shard_map/feed_forward/pallas_call | solution.py:669
  200.3 17.0 %feed_forward.4 = (bf16[640,768]{1,0:T(8,128)(2,1)}, bf16[640,768]{1,0:T(8,128)(2,1)}, bf16[640,768]{1,0:T(8,128)(2,1)}, bf16[640,768]{1,0:T(8,128)(2,1)}, bf16[...) custom-call(bf16[640,768]{1,0:T(8,128)(2,1)} %tie.21.refs_0_, bf16[640,768]{1,0:T(8,128)(2,1)} %copy-done.35, ...), custom_call_target="tpu_custom_call" | custom-call | flops 14000000000 | bytes 1000000 | tf_op jit(solution)/shard_map/feed_forward/pallas_call | solution.py:669
  220.2 17.3 %feed_forward.5 = (f32[640,768]{1,0:T(8,128)}, bf16[640,768]{1,0:T(8,128)(2,1)}, f32[640,768]{1,0:T(8,128)}, bf16[640,768]{1,0:T(8,128)(2,1)}, bf16[640,640]{1,0...) custom-call(bf16[640,768]{1,0:T(8,128)(2,1)} %tie.21.refs_0_, bf16[640,768]{1,0:T(8,128)(2,1)} %copy-done.35, ...), custom_call_target="tpu_custom_call" | custom-call | flops 14000000000 | bytes 1000000 | tf_op jit(solution)/shard_map/feed_forward/pallas_call | solution.py:669
  246.8 5.0 %all-to-all-start.5 = ((bf16[4,160,768]{2,1,0:T(8,128)(2,1)}), bf16[4,160,768]{2,1,0:T(8,128)(2,1)S(1)}, u32[]{:S(2)}, u32[]{:S(2)}) async-start(bf16[4,160,768]{2,1,0:T(8,128)(2,1)} %bitcast.16), calls=%async_computation.5 | async-start | bytes 1966080 | tf_op jit(solution)/shard_map/all_to_all | solution.py:784
  251.8 9.0 %branch_back.1 = (f32[640,768]{1,0:T(8,128)}, bf16[640,768]{1,0:T(8,128)(2,1)}, bf16[640,640]{1,0:T(8,128)(2,1)}, f32[8,640]{1,0:T(8,128)}) custom-call(f32[640,768]{1,0:T(8,128)} %get-tuple-element.105.gn_ref, bf16[640,768]{1,0:T(8,128)(2,1)} %tie.24.got_ref, f32[640,768]{1,0:T(8,128)} %get-tuple-element.87.mid_ref, bf16[640,768]{1,0:T(8,128)(2,1)} %tie.23.refs_2_.g_ref, ...), custom_call_target="tpu_custom_call" | custom-call | flops 8999999488 | bytes 1000000 | tf_op jit(solution)/shard_map/branch_back/pallas_call | solution.py:523
  260.8 18.9 %attend_backward.2 = (bf16[640,768]{1,0:T(8,128)(2,1)}, bf16[1280,640]{1,0:T(8,128)(2,1)}, bf16[1280,640]{1,0:T(8,128)(2,1)}) custom-call(s32[3]{0:T(128)} %get-tuple-element.164.refs_1_.start_ref, s32[3]{0:T(128)} %get-tuple-element.165.refs_2_.small_ref, bf16[640,768]{1,0:T(8,128)(2,1)} %get-tuple-element.78.q_ref.qt_ref, ...), custom_call_target="tpu_custom_call" | custom-call | flops 17999998976 | bytes 1000000 | tf_op jit(solution)/shard_map/attend_backward/pallas_call | solution.py:195
  291.5 13.8 %attend_backward.3 = (bf16[640,768]{1,0:T(8,128)(2,1)}, bf16[1280,640]{1,0:T(8,128)(2,1)}, bf16[1280,640]{1,0:T(8,128)(2,1)}) custom-call(s32[3]{0:T(128)} %get-tuple-element.164.refs_1_.start_ref, s32[3]{0:T(128)} %get-tuple-element.165.refs_2_.small_ref, ...), custom_call_target="tpu_custom_call", output_to_operand_aliasing={{0}: (11, {}), {1}: (12, {}), {2}: (13, {})} | custom-call | flops 12000000000 | bytes 1000000 | tf_op jit(solution)/shard_map/attend_backward/pallas_call | solution.py:195
  305.3 8.4 %project_weights.1 = (bf16[4,4,80,640]{3,2,1,0:T(8,128)(2,1)}, bf16[4,4,80,640]{3,2,1,0:T(8,128)(2,1)}, f32[8,640]{1,0:T(8,128)}) custom-call(s32[1]{0:T(128)} %bitcast.member_ref, bf16[640,1280]{1,0:T(8,128)(2,1)} %get-tuple-element.124.n_ref, bf16[640,768]{1,0:T(8,128)(2,1)} %get-tuple-element.120.dqt_ref, bf16[1280,640]{1,0:T(8,128)(2,1)} %get-tuple-element.121.dk_ref, ...), custom_call_target="tpu_custom_call" | custom-call | flops 8000000000 | bytes 1000000 | tf_op jit(solution)/shard_map/project_weights/pallas_call | solution.py:408
  318.4 10.3 %project_back.1 = (bf16[640,1280]{1,0:T(8,128)(2,1)}, f32[8,640]{1,0:T(8,128)}) custom-call(bf16[640,1280]{1,0:T(8,128)(2,1)} %bitcast.93, bf16[640,768]{1,0:T(8,128)(2,1)} %get-tuple-element.120.dqt_ref, bf16[1280,640]{1,0:T(8,128)(2,1)} %get-tuple-element.121.dk_ref, bf16[1280,640]{1,0:T(8,128)(2,1)} %get-tuple-element.122.dv_ref, ...), custom_call_target="tpu_custom_call" | custom-call | flops 10000000000 | bytes 1000000 | tf_op jit(solution)/shard_map/project_back/pallas_call | solution.py:448
  339.1 9.5 %all-to-all-start.6 = ((bf16[4,160,1280]{2,1,0:T(8,128)(2,1)}), bf16[4,160,1280]{2,1,0:T(8,128)(2,1)S(1)}, u32[]{:S(2)}, u32[]{:S(2)}) async-start(bf16[4,160,1280]{2,1,0:T(8,128)(2,1)} %bitcast.18), calls=%async_computation.6 | async-start | bytes 3276800 | tf_op jit(solution)/shard_map/all_to_all | solution.py:784
  390.4 4.8 %collective-permute-done.37 = f32[9,640]{1,0:T(8,128)S(1)} collective-permute-done((f32[9,640]{1,0:T(8,128)}, f32[9,640]{1,0:T(8,128)S(1)}, u32[]{:S(2)}, u32[]{:S(2)}) %collective-permute-start.37) | collective-permute-done | bytes 23072 | tf_op jit(solution)/shard_map/ppermute | solution.py:701
  (264 shorter events, 133.9 us)
Async XLA Ops:
  2.6 20.2 %all-to-all-start = ((bf16[4,160,384]{2,1,0:T(8,128)(2,1)}), bf16[4,160,384]{2,1,0:T(8,128)(2,1)S(1)}, u32[]{:S(2)}, u32[]{:S(2)}) async-start(bf16[4,160,384]{2,1,0:T(8,128)(2,1)} %pack.1), calls=%async_computation | async-start | bytes 983040 | tf_op jit(solution)/shard_map/all_to_all | solution.py:784
  23.9 23.9 %all-to-all-start.1 = ((bf16[4,160,640]{2,1,0:T(8,128)(2,1)}), bf16[4,160,640]{2,1,0:T(8,128)(2,1)S(1)}, u32[]{:S(2)}, u32[]{:S(2)}) async-start(bf16[4,160,640]{2,1,0:T(8,128)(2,1)} %tie.15), calls=%async_computation.1 | async-start | bytes 1638400 | tf_op jit(solution)/shard_map/all_to_all | solution.py:784
  49.7 41.5 %all-to-all-start.2 = ((bf16[4,160,1280]{2,1,0:T(8,128)(2,1)}), bf16[4,160,1280]{2,1,0:T(8,128)(2,1)S(1)}, u32[]{:S(2)}, u32[]{:S(2)}) async-start(bf16[4,160,1280]{2,1,0:T(8,128)(2,1)} %tie.17), calls=%async_computation.2 | async-start | bytes 3276800 | tf_op jit(solution)/shard_map/all_to_all | solution.py:784
  54.6 41.5 %collective-permute-start.10 = (bf16[640,640]{1,0:T(8,128)(2,1)S(1)}, bf16[640,640]{1,0:T(8,128)(2,1)}, u32[]{:S(2)}, u32[]{:S(2)}) collective-permute-start(bf16[640,640]{1,0:T(8,128)(2,1)S(1)} %bitcast.101), channel_id=1, source_target_pairs={{0,16},{4,20},{8,24},{12,28},{16,0},{20,4},{24,8},{28,12},{1,17},{... | collective-permute-start | bytes 2457608 | tf_op jit(solution)/shard_map/ppermute | solution.py:721
  56.2 41.5 %collective-permute-start.9 = (bf16[640,640]{1,0:T(8,128)(2,1)S(1)}, bf16[640,640]{1,0:T(8,128)(2,1)}, u32[]{:S(2)}, u32[]{:S(2)}) collective-permute-start(bf16[640,640]{1,0:T(8,128)(2,1)S(1)} %bitcast.102), channel_id=1, source_target_pairs={{0,8},{4,12},{8,0},{12,4},{16,24},{20,28},{24,16},{28,20},{1,9},{5... | collective-permute-start | bytes 2457608 | tf_op jit(solution)/shard_map/ppermute | solution.py:721
  56.5 41.2 %collective-permute-start.5 = (bf16[336,640]{1,0:T(8,128)(2,1)}, bf16[336,640]{1,0:T(8,128)(2,1)}, u32[]{:S(2)}, u32[]{:S(2)}) collective-permute-start(bf16[336,640]{1,0:T(8,128)(2,1)} %copy-done.27), channel_id=1, source_target_pairs={{0,4},{4,0},{8,12},{12,8},{16,20},{20,16},{24,28},{28,24},{1,5},{5... | collective-permute-start | bytes 1290248 | tf_op jit(solution)/shard_map/ppermute | solution.py:721
  56.6 41.2 %collective-permute-start.6 = (bf16[336,640]{1,0:T(8,128)(2,1)}, bf16[336,640]{1,0:T(8,128)(2,1)}, u32[]{:S(2)}, u32[]{:S(2)}) collective-permute-start(bf16[336,640]{1,0:T(8,128)(2,1)} %copy-done.28), channel_id=1, source_target_pairs={{0,4},{4,0},{8,12},{12,8},{16,20},{20,16},{24,28},{28,24},{1,5},{5... | collective-permute-start | bytes 1290248 | tf_op jit(solution)/shard_map/ppermute | solution.py:721
  59.8 37.9 %collective-permute-start.8 = (bf16[176,640]{1,0:T(8,128)(2,1)S(1)}, bf16[176,640]{1,0:T(8,128)(2,1)}, u32[]{:S(2)}, u32[]{:S(2)}) collective-permute-start(bf16[176,640]{1,0:T(8,128)(2,1)S(1)} %copy-done.23), channel_id=1, source_target_pairs={{0,4},{4,0},{8,12},{12,8},{16,20},{20,16},{24,28},{28,24},{1,5},{5... | collective-permute-start | bytes 675848 | tf_op jit(solution)/shard_map/ppermute | solution.py:721
  92.7 23.8 %all-to-all-start.3 = ((bf16[4,160,640]{2,1,0:T(8,128)(2,1)}), bf16[4,160,640]{2,1,0:T(8,128)(2,1)S(1)}, u32[]{:S(2)}, u32[]{:S(2)}) async-start(bf16[4,160,640]{2,1,0:T(8,128)(2,1)} %tie.18), calls=%async_computation.3 | async-start | bytes 1638400 | tf_op jit(solution)/shard_map/all_to_all | solution.py:784
  96.2 38.0 %collective-permute-start.11 = (bf16[640,640]{1,0:T(8,128)(2,1)}, bf16[640,640]{1,0:T(8,128)(2,1)S(1)}, u32[]{:S(2)}, u32[]{:S(2)}) collective-permute-start(bf16[640,640]{1,0:T(8,128)(2,1)} %collective-permute-done.10.refs_11_.refs_4_), channel_id=1, source_target_pairs={{0,8},{4,12},{8,0},{12,4},{16,24},{20,28},{24,16},{28,20},{1,9},{5... | collective-permute-start | bytes 2457608 | tf_op jit(solution)/shard_map/ppermute | solution.py:721
  117.3 27.3 %collective-permute-start.12 = (bf16[640,640]{1,0:T(8,128)(2,1)}, bf16[640,640]{1,0:T(8,128)(2,1)S(1)}, u32[]{:S(2)}, u32[]{:S(2)}) collective-permute-start(bf16[640,640]{1,0:T(8,128)(2,1)} %tie.19.refs_1_.refs_5_), channel_id=1, source_target_pairs={{0,8},{4,12},{8,0},{12,4},{16,24},{20,28},{24,16},{28,20},{1,9},{5... | collective-permute-start | bytes 2457608 | tf_op jit(solution)/shard_map/ppermute | solution.py:721
  118.8 42.5 %all-to-all-start.4 = ((bf16[4,160,768]{2,1,0:T(8,128)(2,1)}), bf16[4,160,768]{2,1,0:T(8,128)(2,1)S(1)}, u32[]{:S(2)}, u32[]{:S(2)}) async-start(bf16[4,160,768]{2,1,0:T(8,128)(2,1)} %tie.22), calls=%async_computation.4 | async-start | bytes 1966080 | tf_op jit(solution)/shard_map/all_to_all | solution.py:784
  165.4 34.0 %collective-permute-start.16 = (bf16[640,640]{1,0:T(8,128)(2,1)S(1)}, bf16[640,640]{1,0:T(8,128)(2,1)S(1)}, u32[]{:S(2)}, u32[]{:S(2)}) collective-permute-start(bf16[640,640]{1,0:T(8,128)(2,1)S(1)} %copy-done.3), channel_id=1, source_target_pairs={{0,16},{4,20},{8,24},{12,28},{16,0},{20,4},{24,8},{28,12},{1,17},{... | collective-permute-start | bytes 2457608 | tf_op jit(solution)/shard_map/ppermute | solution.py:721
  197.0 20.6 %collective-permute-start.18 = (bf16[640,640]{1,0:T(8,128)(2,1)}, bf16[640,640]{1,0:T(8,128)(2,1)S(1)}, u32[]{:S(2)}, u32[]{:S(2)}) collective-permute-start(bf16[640,640]{1,0:T(8,128)(2,1)} %get-tuple-element.100), channel_id=1, source_target_pairs={{0,16},{4,20},{8,24},{12,28},{16,0},{20,4},{24,8},{28,12},{1,17},{... | collective-permute-start | bytes 2457608 | tf_op jit(solution)/shard_map/ppermute | solution.py:721
  239.3 40.4 %collective-permute-start.24 = (bf16[640,640]{1,0:T(8,128)(2,1)}, bf16[640,640]{1,0:T(8,128)(2,1)S(1)}, u32[]{:S(2)}, u32[]{:S(2)}) collective-permute-start(bf16[640,640]{1,0:T(8,128)(2,1)} %get-tuple-element.114), channel_id=1, source_target_pairs={{0,16},{4,20},{8,24},{12,28},{16,0},{20,4},{24,8},{28,12},{1,17},{... | collective-permute-start | bytes 2457608 | tf_op jit(solution)/shard_map/ppermute | solution.py:721
  240.7 39.0 %collective-permute-start.21 = (bf16[640,640]{1,0:T(8,128)(2,1)}, bf16[640,640]{1,0:T(8,128)(2,1)S(1)}, u32[]{:S(2)}, u32[]{:S(2)}) collective-permute-start(bf16[640,640]{1,0:T(8,128)(2,1)} %get-tuple-element.113), channel_id=1, source_target_pairs={{0,8},{4,12},{8,0},{12,4},{16,24},{20,28},{24,16},{28,20},{1,9},{5... | collective-permute-start | bytes 2457608 | tf_op jit(solution)/shard_map/ppermute | solution.py:721
  241.3 38.4 %collective-permute-start.23 = (bf16[640,640]{1,0:T(8,128)(2,1)}, bf16[640,640]{1,0:T(8,128)(2,1)S(1)}, u32[]{:S(2)}, u32[]{:S(2)}) collective-permute-start(bf16[640,640]{1,0:T(8,128)(2,1)} %add_convert_fusion.4.refs_12_), channel_id=1, source_target_pairs={{0,8},{4,12},{8,0},{12,4},{16,24},{20,28},{24,16},{28,20},{1,9},{5... | collective-permute-start | bytes 2457608 | tf_op jit(solution)/shard_map/ppermute | solution.py:721
  242.7 37.0 %collective-permute-start.22 = (bf16[640,640]{1,0:T(8,128)(2,1)}, bf16[640,640]{1,0:T(8,128)(2,1)}, u32[]{:S(2)}, u32[]{:S(2)}) collective-permute-start(bf16[640,640]{1,0:T(8,128)(2,1)} %add_convert_fusion.5.refs_11_), channel_id=1, source_target_pairs={{0,16},{4,20},{8,24},{12,28},{16,0},{20,4},{24,8},{28,12},{1,17},{... | collective-permute-start | bytes 2457608 | tf_op jit(solution)/shard_map/ppermute | solution.py:721
  246.8 43.6 %all-to-all-start.5 = ((bf16[4,160,768]{2,1,0:T(8,128)(2,1)}), bf16[4,160,768]{2,1,0:T(8,128)(2,1)S(1)}, u32[]{:S(2)}, u32[]{:S(2)}) async-start(bf16[4,160,768]{2,1,0:T(8,128)(2,1)} %bitcast.16), calls=%async_computation.5 | async-start | bytes 1966080 | tf_op jit(solution)/shard_map/all_to_all | solution.py:784
  285.2 28.9 %collective-permute-start.42 = (bf16[160,1280]{1,0:T(8,128)(2,1)}, bf16[160,1280]{1,0:T(8,128)(2,1)}, u32[]{:S(2)}, u32[]{:S(2)}) collective-permute-start(bf16[160,1280]{1,0:T(8,128)(2,1)} %get-tuple-element.170), channel_id=1, source_target_pairs={{0,1},{1,2},{2,3},{3,0},{4,5},{5,6},{6,7},{7,4},{8,9},{9,10},{10,1... | collective-permute-start | bytes 1228808 | tf_op jit(solution)/shard_map/ppermute | solution.py:701
  285.3 30.7 %collective-permute-start.43 = (bf16[160,1280]{1,0:T(8,128)(2,1)}, bf16[160,1280]{1,0:T(8,128)(2,1)}, u32[]{:S(2)}, u32[]{:S(2)}) collective-permute-start(bf16[160,1280]{1,0:T(8,128)(2,1)} %get-tuple-element.171), channel_id=1, source_target_pairs={{0,2},{1,3},{2,0},{3,1},{4,6},{5,7},{6,4},{7,5},{8,10},{9,11},{10,... | collective-permute-start | bytes 1228808 | tf_op jit(solution)/shard_map/ppermute | solution.py:701
  287.6 28.4 %collective-permute-start.44 = (bf16[160,1280]{1,0:T(8,128)(2,1)}, bf16[160,1280]{1,0:T(8,128)(2,1)}, u32[]{:S(2)}, u32[]{:S(2)}) collective-permute-start(bf16[160,1280]{1,0:T(8,128)(2,1)} %get-tuple-element.172), channel_id=1, source_target_pairs={{0,3},{1,0},{2,1},{3,2},{4,7},{5,4},{6,5},{7,6},{8,11},{9,8},{10,9... | collective-permute-start | bytes 1228808 | tf_op jit(solution)/shard_map/ppermute | solution.py:701
  339.1 62.2 %all-to-all-start.6 = ((bf16[4,160,1280]{2,1,0:T(8,128)(2,1)}), bf16[4,160,1280]{2,1,0:T(8,128)(2,1)S(1)}, u32[]{:S(2)}, u32[]{:S(2)}) async-start(bf16[4,160,1280]{2,1,0:T(8,128)(2,1)} %bitcast.18), calls=%async_computation.6 | async-start | bytes 3276800 | tf_op jit(solution)/shard_map/all_to_all | solution.py:784
  352.0 22.0 %collective-permute-start.35 = (bf16[1,4,80,640]{3,2,1,0:T(8,128)(2,1)}, bf16[1,4,80,640]{3,2,1,0:T(8,128)(2,1)}, u32[]{:S(2)}, u32[]{:S(2)}) collective-permute-start(bf16[1,4,80,640]{3,2,1,0:T(8,128)(2,1)} %pad_maximum_fusion.4.refs_2_.refs_5_), channel_id=1, source_target_pairs={{0,16},{4,20},{8,24},{12,28},{16,0},{20,4},{24,8},{28,12},{1,17},{... | collective-permute-start | bytes 1228808 | tf_op jit(solution)/shard_map/ppermute | solution.py:721
  (68 other events, 454.4 us)

commit v3 on v2

--- a/solution.py
+++ b/solution.py
@@ -365,8 +365,8 @@
     )(member, x, vec, *pieces, *first)
 
 
-def project_weights(masks, member_ref, n_ref, dqt_ref, dk_ref, dv_ref, gwo_ref, *refs):
-    outs, (sums_ref, gw, sem) = refs[:-3], refs[-3:]
+def project_weights(masks, ahead, member_ref, n_ref, dqt_ref, dk_ref, dv_ref, gwo_ref, *refs):
+    outs, (sums_ref, gw, sem) = refs[ahead:-3], refs[-3:]
     rows = dqt_ref.shape[1]
     halo = (n_ref.shape[1] - rows) // 2
     copies = []
@@ -400,25 +400,26 @@
         copy.wait()
 
 
-def run_project_weights(normed, dqt, dk, dv, gwo, member, masks, run):
+def run_project_weights(normed, dqt, dk, dv, gwo, member, masks, run, first):
     D = normed.shape[0]
     shape = jax.ShapeDtypeStruct
     vmem, anywhere = pl.BlockSpec(memory_space=pltpu.VMEM), pl.BlockSpec(memory_space=pl.ANY)
     outs = [shape((len(masks), 4, run, D), bf16)] * 2 if masks else [shape((4, D, D), bf16)]
     return pl.pallas_call(
-        functools.partial(project_weights, masks),
-        in_specs=[pl.BlockSpec(memory_space=pltpu.SMEM)] + [vmem] * 5,
+        functools.partial(project_weights, masks, len(first)),
+        in_specs=[pl.BlockSpec(memory_space=pltpu.SMEM)] + [vmem] * 5 + [anywhere] * len(first),
         out_specs=[anywhere] * len(outs) + [vmem],
         out_shape=outs + [shape((8, D), f32)],
         scratch_shapes=[pltpu.VMEM((4, D, D), bf16), pltpu.SemaphoreType.DMA((8 * max(1, len(masks)),))],
         name="project_weights",
         **kernel_params(8),
-    )(member, normed, dqt, dk, dv, gwo)
-
-
-def project_back(x_ref, dqt_ref, dk_ref, dv_ref, w_ref, mid_ref, vec_ref, *refs):
-    grad_ref, rows_ref, sums_ref = refs[-3:]
+    )(member, normed, dqt, dk, dv, gwo, *first)
+
+
+def project_back(x_ref, dqt_ref, dk_ref, dv_ref, w_ref, mid_ref, vec_ref, run_ref, got_ref, *refs):
+    grad_ref, rows_ref, both_ref, sums_ref = refs[-4:]
     i = pl.program_id(0)
+    both_ref[...] = (run_ref[...].astype(f32) + got_ref[...].astype(f32)).astype(bf16)
     own = (i >= 1) & (i < pl.num_programs(0) - 1)
 
     @pl.when(i == 0)
@@ -438,24 +439,25 @@
         rows_ref[...] = row_sums([sums_ref[0], sums_ref[1]])
 
 
-def run_project_back(x, dqt, dk, dv, w, grad_mid, vec, first):
+def run_project_back(x, dqt, dk, dv, w, grad_mid, vec, runs, got, first):
     D, span = x.shape
     steps = span // QT
     cols = pl.BlockSpec((D, QT), lambda i: (0, i))
     rows = pl.BlockSpec((QT, D), lambda i: (i, 0))
     own = pl.BlockSpec((D, QT), lambda i: (0, jnp.clip(i - 1, 0, steps - 3)))
+    fourth = pl.BlockSpec((runs.shape[0] // 4, *runs.shape[1:]), lambda i: (jnp.minimum(i, 3), 0, 0, 0))
     shape = jax.ShapeDtypeStruct
     return pl.pallas_call(
         project_back,
         grid=(steps,),
-        in_specs=[cols, own, rows, rows, whole((3, D, D)), own, whole((D, LANES), (0, VEC_BLOCK))]
+        in_specs=[cols, own, rows, rows, whole((3, D, D)), own, whole((D, LANES), (0, VEC_BLOCK)), fourth, fourth]
         + [pl.BlockSpec(memory_space=pl.ANY)] * len(first),
-        out_specs=[cols, whole((8, D))],
-        out_shape=[shape((D, span), bf16), shape((8, D), f32)],
+        out_specs=[cols, whole((8, D)), fourth],
+        out_shape=[shape((D, span), bf16), shape((8, D), f32), shape(runs.shape, bf16)],
         scratch_shapes=[pltpu.VMEM((2, D, LANES), f32)],
         name="project_back",
-        **kernel_params(10),
-    )(x, dqt, dk, dv, w, grad_mid, vec, *first)
+        **kernel_params(1),
+    )(x, dqt, dk, dv, w, grad_mid, vec, runs, got, *first)
 
 
 def branch(att_ref, wo_ref, x_ref, vec_ref, mid_ref, n_ref):
@@ -707,13 +709,14 @@
     return [lax.dynamic_index_in_dim(stack, lax.rem(me - j + n, n), 0, False) for j in range(n)]
 
 
-def z_scatter_sum(pieces):
+def z_scatter(pieces):
     n, me = lax.axis_size("narrow"), lax.axis_index("narrow")
-    total = lax.dynamic_index_in_dim(pieces, me, 0, False).astype(f32)
-    for k in range(1, n):
-        piece = lax.dynamic_index_in_dim(pieces, lax.rem(me + k, n), 0, False)
-        total = total + z_rotate(piece, k).astype(f32)
-    return total
+    piece = lambda k: lax.dynamic_index_in_dim(pieces, lax.rem(me + k, n), 0, False)
+    return [piece(0)] + [z_rotate(piece(k), k) for k in range(1, n)]
+
+
+def add(*terms):
+    return sum(t.astype(f32) for t in terms)
 
 
 def swap(x, mask):
@@ -881,7 +884,6 @@
     up_got_x = swap(up_gx, X)
     blocks = [((up_y, 0), (dt_y, 0), ub_y)]
     sums, ((up_gy, dt_gy, ub_gy),) = run_feed_forward(n2_pair, grad_pair, blocks, sums)
-    add = lambda *terms: sum(t.astype(f32) for t in terms)
     dt_got_y = swap(dt_gy, Y)
     up_gy, dt_gx = add(up_gy, up_got_xy).astype(bf16), add(dt_gx, dt_got_xy).astype(bf16)
     up_got_y, dt_got_x = swap(up_gy, Y), swap(dt_gx, X)
@@ -906,14 +908,16 @@
         up_g = up_g[:, :half] + swap(up_g[:, half:].astype(bf16), bit).astype(f32)
         dt_g = dt_g[:, :half] + swap(dt_g[:, half:].astype(bf16), bit).astype(f32)
     ud_g = jnp.concatenate([up_g, dt_g], axis=1).astype(bf16)
-    ud_grad = z_scatter_sum(ud_g.reshape(nn, part, -1))
+    ud_grad = z_scatter(ud_g.reshape(nn, part, -1))
     dqt, dk, dv = run_backward(*back_in, (3, groups), back_a, (ud_g, layer_out))
     masks = [0]
     for bit in high:
         masks = masks + [m ^ bit for m in masks]
     masks = [m ^ b for b in (0, X, Y, X | Y) for m in masks]
     direct = masks if dw % 16 == 0 else []
-    *grad_w, qv_rows = run_project_weights(normed, dqt, dk, dv, grad_wo_t, member, direct, dw)
+    *grad_w, qv_rows = run_project_weights(
+        normed, dqt, dk, dv, grad_wo_t, member, direct, dw, ud_grad[1:2]
+    )
     if not direct:
         grad_w = grad_w[0].reshape(4, nw, dw, D).transpose(1, 0, 2, 3)
         pick = lambda masks: jnp.concatenate(
@@ -921,16 +925,17 @@
         )
         grad_w = pick(masks), pick([m ^ CORE for m in masks])
     attn_g, got = grad_w[0], swap(grad_w[1], CORE)
-    grad_in, sums_one = run_project_back(x_low, dqt, dk, dv, w_attn, grad_mid, vec, (grad_w[1],))
-    got = after((grad_in,), got)
+    grad_in, sums_one, half = run_project_back(
+        x_low, dqt, dk, dv, w_attn, grad_mid, vec, attn_g, got, ()
+    )
     vector_rows = jnp.concatenate([sums_one[:2], qv_rows[:2], sums_two[:4]])
+    ud_grad = add(*ud_grad[:2], *(after((sums_one,), piece) for piece in ud_grad[2:]))
     up_grad, down_grad = ud_grad[:, :units], ud_grad[:, units:].T
     grad_in = across(grad_in.reshape(nn, part, span)).astype(f32)
     tokens_grad = sum(
         jnp.pad(grad_in[j], ((0, 0), (j * quarter, tok - (j + 1) * quarter))) for j in range(nn)
     )[:, halo : halo + tok]
 
-    half = add(attn_g, got).astype(bf16)
     g0, gx, gy, gxy = (half[i * count : (i + 1) * count] for i in range(4))
     gy_low = add(gy[:, :2], swap(gxy[:, :2], X)).astype(bf16)
     gx_high = add(gx[:, 2:], swap(gxy[:, 2:], Y)).astype(bf16)
@@ -948,7 +953,7 @@
         cut = g0.shape[0] // 2
         g0 = g0[:cut] + swap(g0[cut:].astype(bf16), bit).astype(f32)
     g0 = g0[0].astype(bf16).reshape(4 * dw, D).T.reshape(nn, part, 4 * dw)
-    attn_grad = z_scatter_sum(g0)
+    attn_grad = add(*z_scatter(g0))
     qkv_grad = attn_grad[:, : 3 * dw].T.reshape(3, dw, part)
     out_weight_grad = attn_grad[:, 3 * dw :]
 

time: 408 us -> 406 us (level)
  starting transfers between devices: 95.5 us -> 102 us
  waiting for transfers between devices: 72.5 us -> 66.8 us
  other arithmetic: 32.6 us -> 28.5 us
    ppermute x9, starting transfers between devices: 13.6 us -> 25.7 us  [z_rotate(): return lax.ppermute(x, 'narrow', [(i, (i + k) % n) for i in range(n)])]
    all_to_all x7, starting transfers between devices: 48.3 us -> 43.2 us  [shards(): across = lambda x: lax.all_to_all(x, 'narrow', 0, 0, tiled=True)]
    unnamed x80 -> x86, local copies, waits for them, and re-layouts: 12.7 us -> 11.1 us
  transfers between devices with their start and end apart: 52 -> 52, of which waited for: 17 -> 15; matrix products, arithmetic and copies ran while one was open for 11% -> 11% of each run, Pallas kernels for 36% -> 35%
where the time goes in v3:
time: 406 us; the launch traced here: 403 us
  Pallas kernels  168 us (41%)
  starting transfers between devices  102 us (25%)
  waiting for transfers between devices  66.8 us (16%)
  local copies, waits for them, and re-layouts  33.2 us (8%)
  other arithmetic  28.5 us (7%)
    pallas_call x3, Pallas kernels, run_feed_forward(): pl.pallas_call(functools.partial(feed_forward, first, final, len(ahead),...  62.2 us
    all_to_all x7, starting transfers between devices, shards(): across = lambda x: lax.all_to_all(x, 'narrow', 0, 0, tiled=True)  43.2 us
    all_to_all x7, waiting for transfers between devices, shards(): across = lambda x: lax.all_to_all(x, 'narrow', 0, 0, tiled=True)  41.7 us
    ppermute x36, starting transfers between devices, swap(): return lax.ppermute(x, 'wide', [(i, i ^ mask) for i in range(n)])  33.4 us
    pallas_call x2, Pallas kernels, run_backward(): pl.pallas_call(attend_backward, grid_spec=pltpu.PrefetchScalarGridSpec(nu...  32.7 us
    ppermute x9, starting transfers between devices, z_rotate(): return lax.ppermute(x, 'narrow', [(i, (i + k) % n) for i in range(n)])  25.7 us
    pallas_call x3, Pallas kernels, run_forward(): pl.pallas_call(attend_forward, grid_spec=pltpu.PrefetchScalarGridSpec(num...  24.9 us
    ppermute x36, waiting for transfers between devices, swap(): return lax.ppermute(x, 'wide', [(i, i ^ mask) for i in range(n)])  20.9 us
  transfers between devices with their start and end apart: 52, of which 15 were waited for; matrix products, arithmetic and copies ran while one was open for 11% of the time, Pallas kernels for 35%

profile of v3, /device:TPU:0, one launch (start us, length us, event | category | flops | bytes accessed | tf_op | source)
XLA Modules:
  0.0 402.6 jit_solution(2576711239016937050)
XLA Ops:
  2.6 6.4 %all-to-all-start = ((bf16[4,160,384]{2,1,0:T(8,128)(2,1)}), bf16[4,160,384]{2,1,0:T(8,128)(2,1)S(1)}, u32[]{:S(2)}, u32[]{:S(2)}) async-start(bf16[4,160,384]{2,1,0:T(8,128)(2,1)} %pack.1), calls=%async_computation | async-start | bytes 983040 | tf_op jit(solution)/shard_map/all_to_all | solution.py:787
  12.3 10.5 %all-to-all-done = bf16[4,160,384]{2,1,0:T(8,128)(2,1)S(1)} async-done(((bf16[4,160,384]{2,1,0:T(8,128)(2,1)}), bf16[4,160,384]{2,1,0:T(8,128)(2,1)S(1)}, u32[]{:S(2)}, u32[]{:S(2)}) %all-to-all-start) | async-done | bytes 491552 | tf_op jit(solution)/shard_map/all_to_all | solution.py:787
  23.9 3.6 all-to-all-start.1
  34.5 6.3 %collective-permute-done.2.refs_1_.refs_9_ = bf16[336,640]{1,0:T(8,128)(2,1)S(1)} collective-permute-done((bf16[336,640]{1,0:T(8,128)(2,1)}, bf16[336,640]{1,0:T(8,128)(2,1)S(1)}, u32[]{:S(2)}, u32[]{:S(2)}) %collective-permute-start.2) | collective-permute-done | bytes 430112 | tf_op jit(solution)/shard_map/ppermute | solution.py:724
  44.8 3.8 collective-permute-done.1.refs_6_.refs_3_
  50.4 5.2 %all-to-all-start.2 = ((bf16[4,160,1280]{2,1,0:T(8,128)(2,1)}), bf16[4,160,1280]{2,1,0:T(8,128)(2,1)S(1)}, u32[]{:S(2)}, u32[]{:S(2)}) async-start(bf16[4,160,1280]{2,1,0:T(8,128)(2,1)} %tie.18), calls=%async_computation.2 | async-start | bytes 3276800 | tf_op jit(solution)/shard_map/all_to_all | solution.py:787
  60.1 31.1 %all-to-all-done.2 = bf16[4,160,1280]{2,1,0:T(8,128)(2,1)S(1)} async-done(((bf16[4,160,1280]{2,1,0:T(8,128)(2,1)}), bf16[4,160,1280]{2,1,0:T(8,128)(2,1)S(1)}, u32[]{:S(2)}, u32[]{:S(2)}) %all-to-all-start.2) | async-done | bytes 1638432 | tf_op jit(solution)/shard_map/all_to_all | solution.py:787
  98.4 12.3 %project.1 = (bf16[640,1280]{1,0:T(8,128)(2,1)}, bf16[640,768]{1,0:T(8,128)(2,1)}, bf16[640,1280]{1,0:T(8,128)(2,1)}, bf16[640,1280]{1,0:T(8,128)(2,1)}, bf16[12...) custom-call(s32[1]{0:T(128)} %bitcast.member_ref, bf16[640,1280]{1,0:T(8,128)(2,1)} %bitcast.78, ...), custom_call_target="tpu_custom_call" | custom-call | flops 11000000512 | bytes 1000000 | tf_op jit(solution)/shard_map/project/pallas_call | solution.py:340
  110.7 6.0 %attend_forward.3 = (bf16[640,768]{1,0:T(8,128)(2,1)}, f32[40,768]{1,0:T(8,128)}) custom-call(s32[3]{0:T(128)} %get-tuple-element.166.refs_1_.start_ref, s32[3]{0:T(128)} %get-tuple-element.167.refs_2_.small_ref, bf16[640,768]{1,0:T(8,128)(2,1)} %get-tuple-element.79.q_ref.qt_ref, bf16[1280,640]{1,0:T(8,128)(2,1)} %get-tuple-element.80.k_ref, ...), custom_call_target="tpu_custom_call" | custom-call | flops 4000000000 | bytes 1000000 | tf_op jit(solution)/shard_map/attend_forward/pallas_call | solution.py:170
  118.8 15.5 %all-to-all-start.4 = ((bf16[4,160,768]{2,1,0:T(8,128)(2,1)}), bf16[4,160,768]{2,1,0:T(8,128)(2,1)S(1)}, u32[]{:S(2)}, u32[]{:S(2)}) async-start(bf16[4,160,768]{2,1,0:T(8,128)(2,1)} %tie.23), calls=%async_computation.4 | async-start | bytes 1966080 | tf_op jit(solution)/shard_map/all_to_all | solution.py:787
  134.3 9.5 %attend_forward.4 = (bf16[640,768]{1,0:T(8,128)(2,1)}, f32[40,768]{1,0:T(8,128)}) custom-call(s32[3]{0:T(128)} %get-tuple-element.166.refs_1_.start_ref, s32[3]{0:T(128)} %get-tuple-element.167.refs_2_.small_ref, bf16[640,768]{1,0:T(8,128)(2,1)} %get-tuple-element.79.q_ref.qt_ref, ...), custom_call_target="tpu_custom_call", output_to_operand_aliasing={{0}: (7, {}), {1}: (8, {})} | custom-call | flops 8000000000 | bytes 1000000 | tf_op jit(solution)/shard_map/attend_forward/pallas_call | solution.py:170
  146.6 9.5 %attend_forward.5 = (bf16[640,768]{1,0:T(8,128)(2,1)}, f32[40,768]{1,0:T(8,128)}) custom-call(s32[3]{0:T(128)} %get-tuple-element.166.refs_1_.start_ref, s32[3]{0:T(128)} %get-tuple-element.167.refs_2_.small_ref, bf16[640,768]{1,0:T(8,128)(2,1)} %get-tuple-element.79.q_ref.qt_ref, ...), custom_call_target="tpu_custom_call", output_to_operand_aliasing={{0}: (7, {}), {1}: (8, {})} | custom-call | flops 8000000000 | bytes 1000000 | tf_op jit(solution)/shard_map/attend_forward/pallas_call | solution.py:170
  156.1 4.8 %branch.1 = (f32[640,768]{1,0:T(8,128)}, bf16[640,768]{1,0:T(8,128)(2,1)}) custom-call(bf16[640,768]{1,0:T(8,128)(2,1)} %get-tuple-element.86.att_ref.refs_1_, bf16[4,640,640]{2,1,0:T(8,128)(2,1)} %get-tuple-element.87.wo_ref.w_ref, bf16[640,1280]{1,0:T(8,128)(2,1)} %bitcast.79, bf16[640,384]{1,0:T(8,128)(2,1)} %bitcast.84), custom_call_target="tpu_custom_call" | custom-call | flops 5000000000 | bytes 1000000 | tf_op jit(solution)/shard_map/branch/pallas_call | solution.py:474
  168.4 27.9 %feed_forward.3 = (bf16[640,768]{1,0:T(8,128)(2,1)}, bf16[640,768]{1,0:T(8,128)(2,1)}, bf16[640,768]{1,0:T(8,128)(2,1)}, bf16[640,768]{1,0:T(8,128)(2,1)}, bf16[...) custom-call(bf16[640,768]{1,0:T(8,128)(2,1)} %tie.22.refs_0_, ...), custom_call_target="tpu_custom_call" | custom-call | flops 28000000000 | bytes 1000000 | tf_op jit(solution)/shard_map/feed_forward/pallas_call | solution.py:671
  199.6 17.0 %feed_forward.4 = (bf16[640,768]{1,0:T(8,128)(2,1)}, bf16[640,768]{1,0:T(8,128)(2,1)}, bf16[640,768]{1,0:T(8,128)(2,1)}, bf16[640,768]{1,0:T(8,128)(2,1)}, bf16[...) custom-call(bf16[640,768]{1,0:T(8,128)(2,1)} %tie.22.refs_0_, bf16[640,768]{1,0:T(8,128)(2,1)} %copy-done.38, ...), custom_call_target="tpu_custom_call" | custom-call | flops 14000000000 | bytes 1000000 | tf_op jit(solution)/shard_map/feed_forward/pallas_call | solution.py:671
  219.2 17.3 %feed_forward.5 = (f32[640,768]{1,0:T(8,128)}, bf16[640,768]{1,0:T(8,128)(2,1)}, f32[640,768]{1,0:T(8,128)}, bf16[640,768]{1,0:T(8,128)(2,1)}, bf16[640,640]{1,0...) custom-call(bf16[640,768]{1,0:T(8,128)(2,1)} %tie.22.refs_0_, bf16[640,768]{1,0:T(8,128)(2,1)} %copy-done.38, ...), custom_call_target="tpu_custom_call" | custom-call | flops 14000000000 | bytes 1000000 | tf_op jit(solution)/shard_map/feed_forward/pallas_call | solution.py:671
  245.7 5.1 %all-to-all-start.5 = ((bf16[4,160,768]{2,1,0:T(8,128)(2,1)}), bf16[4,160,768]{2,1,0:T(8,128)(2,1)S(1)}, u32[]{:S(2)}, u32[]{:S(2)}) async-start(bf16[4,160,768]{2,1,0:T(8,128)(2,1)} %bitcast.16), calls=%async_computation.5 | async-start | bytes 1966080 | tf_op jit(solution)/shard_map/all_to_all | solution.py:787
  250.8 9.0 %branch_back.1 = (f32[640,768]{1,0:T(8,128)}, bf16[640,768]{1,0:T(8,128)(2,1)}, bf16[640,640]{1,0:T(8,128)(2,1)}, f32[8,640]{1,0:T(8,128)}) custom-call(f32[640,768]{1,0:T(8,128)} %get-tuple-element.106.gn_ref, bf16[640,768]{1,0:T(8,128)(2,1)} %tie.25.got_ref, f32[640,768]{1,0:T(8,128)} %get-tuple-element.88.mid_ref, bf16[640,768]{1,0:T(8,128)(2,1)} %tie.24.refs_2_.g_ref, ...), custom_call_target="tpu_custom_call" | custom-call | flops 8999999488 | bytes 1000000 | tf_op jit(solution)/shard_map/branch_back/pallas_call | solution.py:525
  259.9 18.9 %attend_backward.2 = (bf16[640,768]{1,0:T(8,128)(2,1)}, bf16[1280,640]{1,0:T(8,128)(2,1)}, bf16[1280,640]{1,0:T(8,128)(2,1)}) custom-call(s32[3]{0:T(128)} %get-tuple-element.166.refs_1_.start_ref, s32[3]{0:T(128)} %get-tuple-element.167.refs_2_.small_ref, bf16[640,768]{1,0:T(8,128)(2,1)} %get-tuple-element.79.q_ref.qt_ref, ...), custom_call_target="tpu_custom_call" | custom-call | flops 17999998976 | bytes 1000000 | tf_op jit(solution)/shard_map/attend_backward/pallas_call | solution.py:195
  288.7 13.8 %attend_backward.3 = (bf16[640,768]{1,0:T(8,128)(2,1)}, bf16[1280,640]{1,0:T(8,128)(2,1)}, bf16[1280,640]{1,0:T(8,128)(2,1)}) custom-call(s32[3]{0:T(128)} %get-tuple-element.166.refs_1_.start_ref, s32[3]{0:T(128)} %get-tuple-element.167.refs_2_.small_ref, ...), custom_call_target="tpu_custom_call", output_to_operand_aliasing={{0}: (11, {}), {1}: (12, {}), {2}: (13, {})} | custom-call | flops 12000000000 | bytes 1000000 | tf_op jit(solution)/shard_map/attend_backward/pallas_call | solution.py:195
  303.3 8.4 %project_weights.1 = (bf16[4,4,80,640]{3,2,1,0:T(8,128)(2,1)}, bf16[4,4,80,640]{3,2,1,0:T(8,128)(2,1)}, f32[8,640]{1,0:T(8,128)}) custom-call(s32[1]{0:T(128)} %bitcast.member_ref, bf16[640,1280]{1,0:T(8,128)(2,1)} %get-tuple-element.125.n_ref, bf16[640,768]{1,0:T(8,128)(2,1)} %get-tuple-element.121.dqt_ref, bf16[1280,640]{1,0:T(8,128)(2,1)} %get-tuple-element.122.dk_ref, ...), custom_call_target="tpu_custom_call" | custom-call | flops 8000000000 | bytes 1000000 | tf_op jit(solution)/shard_map/project_weights/pallas_call | solution.py:408
  317.9 11.6 %project_back.1 = (bf16[640,1280]{1,0:T(8,128)(2,1)}, f32[8,640]{1,0:T(8,128)}, bf16[4,4,80,640]{3,2,1,0:T(8,128)(2,1)}) custom-call(bf16[640,1280]{1,0:T(8,128)(2,1)} %bitcast.80, bf16[640,768]{1,0:T(8,128)(2,1)} %get-tuple-element.121.dqt_ref, bf16[1280,640]{1,0:T(8,128)(2,1)} %get-tuple-element.122.dk_ref, bf16[1280,640]{1,0:T(8,128)(2,1)} %get-tuple-element.123.dv_ref, ...), custom_call_target="tpu_custom_call" | custom-call | flops 1000000000 | bytes 1000000 | tf_op jit(solution)/shard_map/project_back/pallas_call | solution.py:450
  334.9 3.8 all-to-all-start.6
  368.6 13.7 %collective-permute-start.37 = (f32[9,640]{1,0:T(8,128)}, f32[9,640]{1,0:T(8,128)S(1)}, u32[]{:S(2)}, u32[]{:S(2)}) collective-permute-start(f32[9,640]{1,0:T(8,128)} %tie.29), channel_id=1, source_target_pairs={{0,1},{1,2},{2,3},{3,0},{4,5},{5,6},{6,7},{7,4},{8,9},{9,10},{10,1... | collective-permute-start | bytes 69128 | tf_op jit(solution)/shard_map/ppermute | solution.py:703
  (270 shorter events, 127.7 us)
Async XLA Ops:
  2.6 20.2 %all-to-all-start = ((bf16[4,160,384]{2,1,0:T(8,128)(2,1)}), bf16[4,160,384]{2,1,0:T(8,128)(2,1)S(1)}, u32[]{:S(2)}, u32[]{:S(2)}) async-start(bf16[4,160,384]{2,1,0:T(8,128)(2,1)} %pack.1), calls=%async_computation | async-start | bytes 983040 | tf_op jit(solution)/shard_map/all_to_all | solution.py:787
  23.9 24.6 %all-to-all-start.1 = ((bf16[4,160,640]{2,1,0:T(8,128)(2,1)}), bf16[4,160,640]{2,1,0:T(8,128)(2,1)S(1)}, u32[]{:S(2)}, u32[]{:S(2)}) async-start(bf16[4,160,640]{2,1,0:T(8,128)(2,1)} %tie.16), calls=%async_computation.1 | async-start | bytes 1638400 | tf_op jit(solution)/shard_map/all_to_all | solution.py:787
  50.4 40.8 %all-to-all-start.2 = ((bf16[4,160,1280]{2,1,0:T(8,128)(2,1)}), bf16[4,160,1280]{2,1,0:T(8,128)(2,1)S(1)}, u32[]{:S(2)}, u32[]{:S(2)}) async-start(bf16[4,160,1280]{2,1,0:T(8,128)(2,1)} %tie.18), calls=%async_computation.2 | async-start | bytes 3276800 | tf_op jit(solution)/shard_map/all_to_all | solution.py:787
  55.6 40.5 %collective-permute-start.10 = (bf16[640,640]{1,0:T(8,128)(2,1)S(1)}, bf16[640,640]{1,0:T(8,128)(2,1)}, u32[]{:S(2)}, u32[]{:S(2)}) collective-permute-start(bf16[640,640]{1,0:T(8,128)(2,1)S(1)} %bitcast.101), channel_id=1, source_target_pairs={{0,16},{4,20},{8,24},{12,28},{16,0},{20,4},{24,8},{28,12},{1,17},{... | collective-permute-start | bytes 2457608 | tf_op jit(solution)/shard_map/ppermute | solution.py:724
  57.2 40.5 %collective-permute-start.9 = (bf16[640,640]{1,0:T(8,128)(2,1)S(1)}, bf16[640,640]{1,0:T(8,128)(2,1)}, u32[]{:S(2)}, u32[]{:S(2)}) collective-permute-start(bf16[640,640]{1,0:T(8,128)(2,1)S(1)} %bitcast.102), channel_id=1, source_target_pairs={{0,8},{4,12},{8,0},{12,4},{16,24},{20,28},{24,16},{28,20},{1,9},{5... | collective-permute-start | bytes 2457608 | tf_op jit(solution)/shard_map/ppermute | solution.py:724
  57.3 40.3 %collective-permute-start.5 = (bf16[336,640]{1,0:T(8,128)(2,1)}, bf16[336,640]{1,0:T(8,128)(2,1)}, u32[]{:S(2)}, u32[]{:S(2)}) collective-permute-start(bf16[336,640]{1,0:T(8,128)(2,1)} %copy-done.30), channel_id=1, source_target_pairs={{0,4},{4,0},{8,12},{12,8},{16,20},{20,16},{24,28},{28,24},{1,5},{5... | collective-permute-start | bytes 1290248 | tf_op jit(solution)/shard_map/ppermute | solution.py:724
  57.3 40.3 %collective-permute-start.6 = (bf16[336,640]{1,0:T(8,128)(2,1)}, bf16[336,640]{1,0:T(8,128)(2,1)}, u32[]{:S(2)}, u32[]{:S(2)}) collective-permute-start(bf16[336,640]{1,0:T(8,128)(2,1)} %copy-done.31), channel_id=1, source_target_pairs={{0,4},{4,0},{8,12},{12,8},{16,20},{20,16},{24,28},{28,24},{1,5},{5... | collective-permute-start | bytes 1290248 | tf_op jit(solution)/shard_map/ppermute | solution.py:724
  59.9 37.8 %collective-permute-start.8 = (bf16[176,640]{1,0:T(8,128)(2,1)S(1)}, bf16[176,640]{1,0:T(8,128)(2,1)S(1)}, u32[]{:S(2)}, u32[]{:S(2)}) collective-permute-start(bf16[176,640]{1,0:T(8,128)(2,1)S(1)} %copy-done.26), channel_id=1, source_target_pairs={{0,4},{4,0},{8,12},{12,8},{16,20},{20,16},{24,28},{28,24},{1,5},{5... | collective-permute-start | bytes 675848 | tf_op jit(solution)/shard_map/ppermute | solution.py:724
  92.6 24.1 %all-to-all-start.3 = ((bf16[4,160,640]{2,1,0:T(8,128)(2,1)}), bf16[4,160,640]{2,1,0:T(8,128)(2,1)S(1)}, u32[]{:S(2)}, u32[]{:S(2)}) async-start(bf16[4,160,640]{2,1,0:T(8,128)(2,1)} %tie.19), calls=%async_computation.3 | async-start | bytes 1638400 | tf_op jit(solution)/shard_map/all_to_all | solution.py:787
  96.1 38.2 %collective-permute-start.11 = (bf16[640,640]{1,0:T(8,128)(2,1)}, bf16[640,640]{1,0:T(8,128)(2,1)}, u32[]{:S(2)}, u32[]{:S(2)}) collective-permute-start(bf16[640,640]{1,0:T(8,128)(2,1)} %collective-permute-done.10.refs_11_.refs_4_), channel_id=1, source_target_pairs={{0,8},{4,12},{8,0},{12,4},{16,24},{20,28},{24,16},{28,20},{1,9},{5... | collective-permute-start | bytes 2457608 | tf_op jit(solution)/shard_map/ppermute | solution.py:724
  117.6 26.2 %collective-permute-start.12 = (bf16[640,640]{1,0:T(8,128)(2,1)}, bf16[640,640]{1,0:T(8,128)(2,1)S(1)}, u32[]{:S(2)}, u32[]{:S(2)}) collective-permute-start(bf16[640,640]{1,0:T(8,128)(2,1)} %tie.20.refs_1_.refs_5_), channel_id=1, source_target_pairs={{0,8},{4,12},{8,0},{12,4},{16,24},{20,28},{24,16},{28,20},{1,9},{5... | collective-permute-start | bytes 2457608 | tf_op jit(solution)/shard_map/ppermute | solution.py:724
  118.8 42.1 %all-to-all-start.4 = ((bf16[4,160,768]{2,1,0:T(8,128)(2,1)}), bf16[4,160,768]{2,1,0:T(8,128)(2,1)S(1)}, u32[]{:S(2)}, u32[]{:S(2)}) async-start(bf16[4,160,768]{2,1,0:T(8,128)(2,1)} %tie.23), calls=%async_computation.4 | async-start | bytes 1966080 | tf_op jit(solution)/shard_map/all_to_all | solution.py:787
  164.6 34.0 %collective-permute-start.16 = (bf16[640,640]{1,0:T(8,128)(2,1)S(1)}, bf16[640,640]{1,0:T(8,128)(2,1)S(1)}, u32[]{:S(2)}, u32[]{:S(2)}) collective-permute-start(bf16[640,640]{1,0:T(8,128)(2,1)S(1)} %copy-done.4), channel_id=1, source_target_pairs={{0,16},{4,20},{8,24},{12,28},{16,0},{20,4},{24,8},{28,12},{1,17},{... | collective-permute-start | bytes 2457608 | tf_op jit(solution)/shard_map/ppermute | solution.py:724
  196.3 20.6 %collective-permute-start.18 = (bf16[640,640]{1,0:T(8,128)(2,1)}, bf16[640,640]{1,0:T(8,128)(2,1)S(1)}, u32[]{:S(2)}, u32[]{:S(2)}) collective-permute-start(bf16[640,640]{1,0:T(8,128)(2,1)} %get-tuple-element.101), channel_id=1, source_target_pairs={{0,16},{4,20},{8,24},{12,28},{16,0},{20,4},{24,8},{28,12},{1,17},{... | collective-permute-start | bytes 2457608 | tf_op jit(solution)/shard_map/ppermute | solution.py:724
  197.8 20.2 %collective-permute-start.17 = (bf16[640,640]{1,0:T(8,128)(2,1)}, bf16[640,640]{1,0:T(8,128)(2,1)S(1)}, u32[]{:S(2)}, u32[]{:S(2)}) collective-permute-start(bf16[640,640]{1,0:T(8,128)(2,1)} %get-tuple-element.99), channel_id=1, source_target_pairs={{0,8},{4,12},{8,0},{12,4},{16,24},{20,28},{24,16},{28,20},{1,9},{5... | collective-permute-start | bytes 2457608 | tf_op jit(solution)/shard_map/ppermute | solution.py:724
  238.2 40.6 %collective-permute-start.24 = (bf16[640,640]{1,0:T(8,128)(2,1)}, bf16[640,640]{1,0:T(8,128)(2,1)S(1)}, u32[]{:S(2)}, u32[]{:S(2)}) collective-permute-start(bf16[640,640]{1,0:T(8,128)(2,1)} %get-tuple-element.115), channel_id=1, source_target_pairs={{0,16},{4,20},{8,24},{12,28},{16,0},{20,4},{24,8},{28,12},{1,17},{... | collective-permute-start | bytes 2457608 | tf_op jit(solution)/shard_map/ppermute | solution.py:724
  239.7 39.1 %collective-permute-start.21 = (bf16[640,640]{1,0:T(8,128)(2,1)}, bf16[640,640]{1,0:T(8,128)(2,1)S(1)}, u32[]{:S(2)}, u32[]{:S(2)}) collective-permute-start(bf16[640,640]{1,0:T(8,128)(2,1)} %get-tuple-element.114), channel_id=1, source_target_pairs={{0,8},{4,12},{8,0},{12,4},{16,24},{20,28},{24,16},{28,20},{1,9},{5... | collective-permute-start | bytes 2457608 | tf_op jit(solution)/shard_map/ppermute | solution.py:724
  240.5 38.3 %collective-permute-start.23 = (bf16[640,640]{1,0:T(8,128)(2,1)}, bf16[640,640]{1,0:T(8,128)(2,1)S(1)}, u32[]{:S(2)}, u32[]{:S(2)}) collective-permute-start(bf16[640,640]{1,0:T(8,128)(2,1)} %add_convert_fusion.3.refs_12_), channel_id=1, source_target_pairs={{0,8},{4,12},{8,0},{12,4},{16,24},{20,28},{24,16},{28,20},{1,9},{5... | collective-permute-start | bytes 2457608 | tf_op jit(solution)/shard_map/ppermute | solution.py:724
  241.7 37.1 %collective-permute-start.22 = (bf16[640,640]{1,0:T(8,128)(2,1)}, bf16[640,640]{1,0:T(8,128)(2,1)}, u32[]{:S(2)}, u32[]{:S(2)}) collective-permute-start(bf16[640,640]{1,0:T(8,128)(2,1)} %add_convert_fusion.4.refs_11_), channel_id=1, source_target_pairs={{0,16},{4,20},{8,24},{12,28},{16,0},{20,4},{24,8},{28,12},{1,17},{... | collective-permute-start | bytes 2457608 | tf_op jit(solution)/shard_map/ppermute | solution.py:724
  245.7 41.9 %all-to-all-start.5 = ((bf16[4,160,768]{2,1,0:T(8,128)(2,1)}), bf16[4,160,768]{2,1,0:T(8,128)(2,1)S(1)}, u32[]{:S(2)}, u32[]{:S(2)}) async-start(bf16[4,160,768]{2,1,0:T(8,128)(2,1)} %bitcast.16), calls=%async_computation.5 | async-start | bytes 1966080 | tf_op jit(solution)/shard_map/all_to_all | solution.py:787
  312.0 26.7 %collective-permute-start.43 = (bf16[160,1280]{1,0:T(8,128)(2,1)}, bf16[160,1280]{1,0:T(8,128)(2,1)}, u32[]{:S(2)}, u32[]{:S(2)}) collective-permute-start(bf16[160,1280]{1,0:T(8,128)(2,1)} %get-tuple-element.172), channel_id=1, source_target_pairs={{0,2},{1,3},{2,0},{3,1},{4,6},{5,7},{6,4},{7,5},{8,10},{9,11},{10,... | collective-permute-start | bytes 1228808 | tf_op jit(solution)/shard_map/ppermute | solution.py:703
  314.4 24.9 %collective-permute-start.44 = (bf16[160,1280]{1,0:T(8,128)(2,1)}, bf16[160,1280]{1,0:T(8,128)(2,1)}, u32[]{:S(2)}, u32[]{:S(2)}) collective-permute-start(bf16[160,1280]{1,0:T(8,128)(2,1)} %get-tuple-element.174), channel_id=1, source_target_pairs={{0,3},{1,0},{2,1},{3,2},{4,7},{5,4},{6,5},{7,6},{8,11},{9,8},{10,9... | collective-permute-start | bytes 1228808 | tf_op jit(solution)/shard_map/ppermute | solution.py:703
  334.9 64.3 %all-to-all-start.6 = ((bf16[4,160,1280]{2,1,0:T(8,128)(2,1)}), bf16[4,160,1280]{2,1,0:T(8,128)(2,1)S(1)}, u32[]{:S(2)}, u32[]{:S(2)}) async-start(bf16[4,160,1280]{2,1,0:T(8,128)(2,1)} %bitcast.104), calls=%async_computation.6 | async-start | bytes 3276800 | tf_op jit(solution)/shard_map/all_to_all | solution.py:787
  343.5 21.4 %collective-permute-start.36 = (bf16[1,4,80,640]{3,2,1,0:T(8,128)(2,1)S(1)}, bf16[1,4,80,640]{3,2,1,0:T(8,128)(2,1)S(1)}, u32[]{:S(2)}, u32[]{:S(2)}) collective-permute-start(bf16[1,4,80,640]{3,2,1,0:T(8,128)(2,1)S(1)} %pad_maximum_fusion.4.refs_2_.refs_5_), channel_id=1, source_target_pairs={{0,16},{4,20},{8,24},{12,28},{16,0},{20,4},{24,8},{28,12},{1,17},{... | collective-permute-start | bytes 1228808 | tf_op jit(solution)/shard_map/ppermute | solution.py:724
  (71 other events, 483.9 us)
